TPU v7x, 512 devices: a whole 4x8x8 slice. The times are simulated.
512 devices in a mesh: grp: 16 (over z, core), sp: 32 (over x, y).
Axes of the slice: x: 4, y: 8, z: 8, core: 2. Of those that a mesh axis runs over, the one named last changes fastest.
Arguments:
- q_src: bfloat16 [128, 16, 32, 4096], P(None, 'grp', 'sp'), may hold values from -4.5 to 4.5
- k_src: bfloat16 [128, 16, 32, 1024], P(None, 'grp', 'sp'), may hold values from -4.5 to 4.5
- v_src: bfloat16 [128, 16, 32, 1024], P(None, 'grp', 'sp'), may hold values from -4.5 to 4.5
- grad_src: bfloat16 [128, 16, 32, 4096], P(None, 'grp', 'sp'), may hold values from -4.5 to 4.5
- doc_lengths: int32 [192], replicated, may hold values from 0 to 5, as said below
- doc_groups: int32 [192], replicated, may hold values from 0 to 15, as said below
- doc_offsets: int32 [192], replicated, may hold values from 0 to 11, as said below
Outputs:
- dq_grp: bfloat16 [16, 192, 32, 4096], P('grp', None, 'sp')
- dk_grp: bfloat16 [16, 192, 32, 1024], P('grp', None, 'sp')
- dv_grp: bfloat16 [16, 192, 32, 1024], P('grp', None, 'sp')
Inputs may be any that keep to these rules, and one draw needn't show every extreme that they name: `doc_lengths`: documents of positive length come first, absent ones (length 0) last; the lengths sum to 128 and one document has exactly 5 blocks. `doc_groups`: placed at their offsets, the documents of a group cover its blocks 0 up to its total without gaps or intersection; every group receives at least one block, none more than 12, and one group exactly 12. Absent documents name group 0. `doc_offsets`: absent documents have offset 0.
All inputs are finite; a program needn't handle non-finite values.
Results may differ from a plain program's by a relative error of at most 0.0091.
Values may be sent and summed in bfloat16 or wider, within the bound.
No kernel may reach another device: no remote copies, remote signals or barrier semaphores. Data moves between devices by JAX's collectives and lax.ppermute only.
A program may use at most 64 MiB of HBM per device.

v0:
```python
import math

import jax
import jax.numpy as jnp
from jax import lax
from jax.sharding import PartitionSpec as P

HEADS = 32
KV_HEADS = 8
HEAD_DIM = 128


NEG_FILL = -1e30


def unchanged(passed):
    return passed


def collapse(array):
    rounded = lax.optimization_barrier(array)
    return jnp.sum(rounded.astype(jnp.float32), axis=2)


def pair_fold(low_part, high_part):
    return lax.optimization_barrier(
        (low_part.astype(jnp.float32) + high_part.astype(jnp.float32)).astype(jnp.bfloat16)
    )


def halves_total(array):
    half = array.shape[2] // 2
    return collapse(pair_fold(array[:, :, :half], array[:, :, half:]))


def attend(q_heads, k_heads, v_heads, g_heads, first_tok):
    tokens_here, kv_local, q_per_kv, head_dim = q_heads.shape
    span_len = math.gcd(tokens_here, 512)
    blocks = tokens_here // span_len
    factor = head_dim ** (-0.5)
    lane_pos = jnp.arange(span_len, dtype=jnp.int32)
    block_low = jnp.min(first_tok.reshape(blocks, span_len), axis=1)
    heads_shape = (kv_local, q_per_kv, span_len)

    def cut_block(array, index):
        return lax.dynamic_slice_in_dim(array, index * span_len, span_len, 0)

    def pair_logits(q_block, first_q, q_index, k_index):
        k_block = cut_block(k_heads, k_index)
        logits = (
            jnp.einsum("qjih,kjh->jiqk", q_block, k_block, preferred_element_type=jnp.float32)
            * factor
        )
        q_pos = q_index * span_len + lane_pos
        k_pos = k_index * span_len + lane_pos
        allowed = (k_pos[None, :] <= q_pos[:, None]) & (k_pos[None, :] >= first_q[:, None])
        return (logits, allowed)

    def is_live(q_index, k_index):
        return block_low[q_index] <= k_index * span_len + span_len - 1

    def row_norm(q_index):
        q_block = cut_block(q_heads, q_index)
        first_q = cut_block(first_tok, q_index)

        def visit_key(k_index, running):

            def update(running):
                row_high, row_mass = running
                logits, allowed = pair_logits(q_block, first_q, q_index, k_index)
                logits = jnp.where(allowed, logits, NEG_FILL)
                new_high = jnp.maximum(row_high, jnp.max(logits, axis=-1))
                row_mass = row_mass * jnp.exp(row_high - new_high) + jnp.sum(
                    jnp.where(allowed, jnp.exp(logits - new_high[..., None]), 0.0), axis=-1
                )
                return (new_high, row_mass)

            return lax.cond(is_live(q_index, k_index), update, unchanged, running)

        initial = (
            jnp.full(heads_shape, NEG_FILL, jnp.float32),
            jnp.zeros(heads_shape, jnp.float32),
        )
        row_high, row_mass = lax.fori_loop(0, q_index + 1, visit_key, initial)
        return row_high + jnp.log(row_mass)

    log_norm = lax.map(row_norm, jnp.arange(blocks, dtype=jnp.int32))

    def row_delta(q_index):
        q_block = cut_block(q_heads, q_index)
        first_q = cut_block(first_tok, q_index)
        norm_row = log_norm[q_index]

        def visit_key(k_index, acc_out):

            def update(acc_out):
                logits, allowed = pair_logits(q_block, first_q, q_index, k_index)
                weights = jnp.where(allowed, jnp.exp(logits - norm_row[..., None]), 0.0).astype(
                    jnp.bfloat16
                )
                v_block = cut_block(v_heads, k_index)
                return acc_out + jnp.einsum(
                    "jiqk,kjh->jiqh", weights, v_block, preferred_element_type=jnp.float32
                )

            return lax.cond(is_live(q_index, k_index), update, unchanged, acc_out)

        acc_out = lax.fori_loop(
            0, q_index + 1, visit_key, jnp.zeros(heads_shape + (head_dim,), jnp.float32)
        )
        g_block = cut_block(g_heads, q_index)
        return jnp.einsum("jiqh,qjih->jiq", acc_out, g_block, preferred_element_type=jnp.float32)

    delta_all = lax.map(row_delta, jnp.arange(blocks, dtype=jnp.int32))

    def back_row(q_index, carried):
        grad_q, grad_k, grad_v = carried
        q_block = cut_block(q_heads, q_index)
        g_block = cut_block(g_heads, q_index)
        first_q = cut_block(first_tok, q_index)
        norm_row = log_norm[q_index]
        delta_row = delta_all[q_index]

        def visit_key(k_index, inner):

            def update(inner):
                q_acc, grad_k, grad_v = inner
                logits, allowed = pair_logits(q_block, first_q, q_index, k_index)
                probs = jnp.where(allowed, jnp.exp(logits - norm_row[..., None]), 0.0)
                probs_low = probs.astype(jnp.bfloat16)
                k_block = cut_block(k_heads, k_index)
                v_block = cut_block(v_heads, k_index)
                d_probs = jnp.einsum(
                    "qjih,kjh->jiqk", g_block, v_block, preferred_element_type=jnp.float32
                )
                d_logits = (probs * (d_probs - delta_row[..., None])).astype(jnp.bfloat16)
                q_acc = q_acc + jnp.einsum(
                    "jiqk,kjh->qjih", d_logits, k_block, preferred_element_type=jnp.float32
                )
                k_part = jnp.einsum(
                    "jiqk,qjih->kjih", d_logits, q_block, preferred_element_type=jnp.float32
                )
                v_part = jnp.einsum(
                    "jiqk,qjih->kjih", probs_low, g_block, preferred_element_type=jnp.float32
                )
                at_row = k_index * span_len
                grad_k = lax.dynamic_update_slice_in_dim(
                    grad_k, cut_block(grad_k, k_index) + k_part, at_row, 0
                )
                grad_v = lax.dynamic_update_slice_in_dim(
                    grad_v, cut_block(grad_v, k_index) + v_part, at_row, 0
                )
                return (q_acc, grad_k, grad_v)

            return lax.cond(is_live(q_index, k_index), update, unchanged, inner)

        q_start = jnp.zeros((span_len, kv_local, q_per_kv, head_dim), jnp.float32)
        q_acc, grad_k, grad_v = lax.fori_loop(0, q_index + 1, visit_key, (q_start, grad_k, grad_v))
        grad_q = lax.dynamic_update_slice_in_dim(grad_q, q_acc, q_index * span_len, 0)
        return (grad_q, grad_k, grad_v)

    empty = jnp.zeros((tokens_here, kv_local, q_per_kv, head_dim), jnp.float32)
    grad_q, grad_k, grad_v = lax.fori_loop(0, blocks, back_row, (empty, empty, empty))
    return (grad_q * factor, grad_k * factor, grad_v)


def on_device(q_src, k_src, v_src, grad_src, doc_lengths, doc_groups, doc_offsets):
    grp_count = lax.axis_size("grp")
    sp_count = lax.axis_size("sp")
    unit_count = q_src.shape[0]
    slot_count = doc_lengths.shape[0]
    group_cap = slot_count // grp_count
    row_count = group_cap * grp_count
    unit_tok = grp_count * sp_count
    group_tok = row_count * sp_count
    head_dim = HEAD_DIM
    copies = max(1, sp_count // KV_HEADS)
    kv_local = max(1, KV_HEADS // sp_count)
    q_local = HEADS // sp_count
    q_per_kv = q_local // kv_local
    unit_ids = jnp.arange(unit_count, dtype=jnp.int32)
    starts = jnp.cumsum(doc_lengths) - doc_lengths
    inside = (
        (unit_ids[:, None] >= starts[None, :])
        & (unit_ids[:, None] < (starts + doc_lengths)[None, :])
    ).astype(jnp.int32)
    group_of = jnp.sum(inside * doc_groups[None, :], axis=1)
    place_of = jnp.sum(
        inside * (doc_offsets[None, :] + unit_ids[:, None] - starts[None, :]), axis=1
    )
    slot_of = group_of * group_cap + place_of
    slot_ids = jnp.arange(row_count, dtype=jnp.int32).reshape(grp_count, group_cap).T.reshape(-1)
    matches = (slot_of[None, :] == slot_ids[:, None]).astype(jnp.int32)
    source = jnp.sum(matches * unit_ids[None, :], axis=1)
    filled = jnp.sum(matches, axis=1) > 0

    def pack_rows(array):
        flat = array.reshape(unit_count, array.shape[-1])
        picked = jnp.take(flat, source, axis=0)
        picked = jnp.where(filled[:, None], picked, jnp.zeros_like(picked))
        return picked.reshape(group_cap, grp_count, array.shape[-1])

    arrived = (
        lax.all_to_all(pack_rows(q_src), "grp", split_axis=1, concat_axis=1, tiled=True),
        lax.all_to_all(pack_rows(k_src), "grp", split_axis=1, concat_axis=1, tiled=True),
        lax.all_to_all(pack_rows(v_src), "grp", split_axis=1, concat_axis=1, tiled=True),
        lax.all_to_all(pack_rows(grad_src), "grp", split_axis=1, concat_axis=1, tiled=True),
    )
    q_rows = arrived[0].reshape(row_count, 1, HEADS, head_dim)
    k_rows = arrived[1].reshape(row_count, KV_HEADS, head_dim)
    v_rows = arrived[2].reshape(row_count, KV_HEADS, head_dim)
    g_rows = arrived[3].reshape(row_count, 1, HEADS, head_dim)
    my_group = lax.axis_index("grp")
    unit_place = jnp.arange(group_cap, dtype=jnp.int32)
    member = (
        (doc_groups[None, :] == my_group)
        & (doc_lengths[None, :] > 0)
        & (doc_offsets[None, :] <= unit_place[:, None])
        & (unit_place[:, None] < (doc_offsets + doc_lengths)[None, :])
    ).astype(jnp.int32)
    first_unit = jnp.sum(member * doc_offsets[None, :], axis=1)
    occupied = jnp.sum(member, axis=1) > 0
    token_ids = jnp.arange(group_tok, dtype=jnp.int32)
    first_tok = jnp.where(
        jnp.repeat(occupied, unit_tok), jnp.repeat(first_unit * unit_tok, unit_tok), token_ids
    )
    k_wide = jnp.repeat(k_rows, copies, axis=1).reshape(row_count, 1, KV_HEADS * copies, head_dim)
    v_wide = jnp.repeat(v_rows, copies, axis=1).reshape(row_count, 1, KV_HEADS * copies, head_dim)
    q_back, g_back, k_back, v_back = (
        lax.all_to_all(q_rows, "sp", split_axis=2, concat_axis=1, tiled=True),
        lax.all_to_all(g_rows, "sp", split_axis=2, concat_axis=1, tiled=True),
        lax.all_to_all(k_wide, "sp", split_axis=2, concat_axis=1, tiled=True),
        lax.all_to_all(v_wide, "sp", split_axis=2, concat_axis=1, tiled=True),
    )
    k_heads = k_back.reshape(group_tok, kv_local, head_dim)
    v_heads = v_back.reshape(group_tok, kv_local, head_dim)
    q_heads = q_back.reshape(group_tok, kv_local, q_per_kv, head_dim)
    g_heads = g_back.reshape(group_tok, kv_local, q_per_kv, head_dim)
    grad_q, grad_k, grad_v = attend(q_heads, k_heads, v_heads, g_heads, first_tok)
    q_low = grad_q.astype(jnp.bfloat16).reshape(row_count, sp_count, q_local, head_dim)
    k_low = grad_k.astype(jnp.bfloat16)
    v_low = grad_v.astype(jnp.bfloat16)
    q_home, k_home, v_home = (
        lax.all_to_all(q_low, "sp", split_axis=1, concat_axis=2, tiled=True),
        lax.all_to_all(
            k_low.reshape(row_count, sp_count, q_local, head_dim),
            "sp",
            split_axis=1,
            concat_axis=2,
            tiled=True,
        ),
        lax.all_to_all(
            v_low.reshape(row_count, sp_count, q_local, head_dim),
            "sp",
            split_axis=1,
            concat_axis=2,
            tiled=True,
        ),
    )
    k_sum = halves_total(k_home.reshape(row_count, KV_HEADS, HEADS // KV_HEADS, head_dim))
    v_sum = halves_total(v_home.reshape(row_count, KV_HEADS, HEADS // KV_HEADS, head_dim))
    dk_out = k_sum.astype(jnp.bfloat16).reshape(1, row_count, 1, KV_HEADS * head_dim)
    dv_out = v_sum.astype(jnp.bfloat16).reshape(1, row_count, 1, KV_HEADS * head_dim)
    dq_out = q_home.reshape(1, row_count, 1, HEADS * head_dim)
    return (dq_out, dk_out, dv_out)


def solution(mesh):
    placed = (
        P(None, "grp", "sp", None),
        P(None, "grp", "sp", None),
        P(None, "grp", "sp", None),
        P(None, "grp", "sp", None),
        P(),
        P(),
        P(),
    )
    return jax.shard_map(
        on_device,
        mesh=mesh,
        in_specs=placed,
        out_specs=(
            P("grp", None, "sp", None),
            P("grp", None, "sp", None),
            P("grp", None, "sp", None),
        ),
        check_vma=False,
    )
```

profile of v0, /device:TPU:457, one launch (start us, length us, event | category | flops | bytes accessed | tf_op | source)
XLA Modules:
  0.0 1102.4 jit_solution(7298753183538963416)
XLA Ops:
  27.4 7.1 all-to-all-start.6
  39.0 8.8 all-to-all-done.6
  47.8 7.2 all-to-all-start
  57.2 44.9 %all-to-all-done = bf16[12,16,4096]{2,0,1:T(8,128)(2,1)} async-done(((bf16[12,16,4096]{2,0,1:T(8,128)(2,1)}), bf16[12,16,4096]{2,0,1:T(8,128)(2,1)}, u32[]{:S(2)}, u32[]{:S(2)}) %all-to-all-start) | async-done | bytes 1572896 | tf_op jit(solution)/shard_map/all_to_all | solution.py:204
  102.1 6.8 all-to-all-start.4
  109.3 46.8 %all-to-all-done.4 = bf16[12,16,4096]{2,0,1:T(8,128)(2,1)} async-done(((bf16[12,16,4096]{2,0,1:T(8,128)(2,1)}), bf16[12,16,4096]{2,0,1:T(8,128)(2,1)}, u32[]{:S(2)}, u32[]{:S(2)}) %all-to-all-start.4) | async-done | bytes 1572896 | tf_op jit(solution)/shard_map/all_to_all | solution.py:207
  157.7 9.7 all-to-all-start.7
  167.8 38.2 %all-to-all-done.7 = bf16[192,1,32,128]{3,0,1,2:T(8,128)(2,1)S(1)} async-done(((bf16[192,1,32,128]{3,0,1,2:T(8,128)(2,1)}), bf16[192,1,32,128]{3,0,1,2:T(8,128)(2,1)S(1)}, u32[]{:S(2)}, u32[]{:S(2)}) %all-to-all-start.7) | async-done | bytes 1572896 | tf_op jit(solution)/shard_map/all_to_all | solution.py:233
  218.0 33.2 %all-to-all-done.3 = bf16[192,1,32,128]{3,0,1,2:T(8,128)(2,1)S(1)} async-done(((bf16[192,1,32,128]{3,0,1,2:T(8,128)(2,1)}), bf16[192,1,32,128]{3,0,1,2:T(8,128)(2,1)S(1)}, u32[]{:S(2)}, u32[]{:S(2)}) %all-to-all-start.3) | async-done | bytes 1572896 | tf_op jit(solution)/shard_map/all_to_all | solution.py:232
  267.8 29.1 %all-to-all-done.1 = bf16[192,1,32,128]{3,0,1,2:T(8,128)(2,1)} async-done(((bf16[192,1,32,128]{3,0,1,2:T(8,128)(2,1)}), bf16[192,1,32,128]{3,0,1,2:T(8,128)(2,1)}, u32[]{:S(2)}, u32[]{:S(2)}) %all-to-all-start.1) | async-done | bytes 1572896 | tf_op jit(solution)/shard_map/all_to_all | solution.py:230
  307.2 191.2 %while.174 = (s32[]{:T(128)}, f32[12,1,1,512]{3,2,1,0:T(1,128)S(1)}, s32[12]{0:T(128)S(1)}, bf16[6144,1,1,128]{3,0,2,1:T(8,128)(2,1)}, s32[6144]{0:T(1024)S(1)},...) while((s32[]{:T(128)}, f32[12,1,1,512]{3,2,1,0:T(1,128)S(1)}, ...), condition=%wide.region_16.19_spmd.clone.clone, body=%wide.region_9.0_spmd.clone.clone.sunk | while | flops 70257176 | bytes 2685694 | solution.py:87
  331.7 8.9 while.179
  345.9 11.9 %while.179 = (s32[]{:T(128)}, f32[1,1,512]{2,1,0:T(1,128)S(1)}, f32[1,1,512]{2,1,0:T(1,128)S(1)}, s32[]{:T(128)}, s32[1]{0:T(128)}, /*index=5*/s32[512]{0:T(512)...) while((s32[]{:T(128)}, f32[1,1,512]{2,1,0:T(1,128)S(1)}, ...), condition=%wide.region_15.17_spmd.clone, body=%wide.region_10.16_spmd.clone.sunk | while | flops 70256656 | bytes 2406753 | solution.py:84
  363.0 14.9 %while.179 = (s32[]{:T(128)}, f32[1,1,512]{2,1,0:T(1,128)S(1)}, f32[1,1,512]{2,1,0:T(1,128)S(1)}, s32[]{:T(128)}, s32[1]{0:T(128)}, /*index=5*/s32[512]{0:T(512)...) while((s32[]{:T(128)}, f32[1,1,512]{2,1,0:T(1,128)S(1)}, ...), condition=%wide.region_15.17_spmd.clone, body=%wide.region_10.16_spmd.clone.sunk | while | flops 70256656 | bytes 2406753 | solution.py:84
  394.9 7.3 while.179
  407.5 10.3 while.179
  423.0 13.3 %while.179 = (s32[]{:T(128)}, f32[1,1,512]{2,1,0:T(1,128)S(1)}, f32[1,1,512]{2,1,0:T(1,128)S(1)}, s32[]{:T(128)}, s32[1]{0:T(128)}, /*index=5*/s32[512]{0:T(512)...) while((s32[]{:T(128)}, f32[1,1,512]{2,1,0:T(1,128)S(1)}, ...), condition=%wide.region_15.17_spmd.clone, body=%wide.region_10.16_spmd.clone.sunk | while | flops 70256656 | bytes 2406753 | solution.py:84
  441.5 16.3 %while.179 = (s32[]{:T(128)}, f32[1,1,512]{2,1,0:T(1,128)S(1)}, f32[1,1,512]{2,1,0:T(1,128)S(1)}, s32[]{:T(128)}, s32[1]{0:T(128)}, /*index=5*/s32[512]{0:T(512)...) while((s32[]{:T(128)}, f32[1,1,512]{2,1,0:T(1,128)S(1)}, ...), condition=%wide.region_15.17_spmd.clone, body=%wide.region_10.16_spmd.clone.sunk | while | flops 70256656 | bytes 2406753 | solution.py:84
  462.9 19.2 %while.179 = (s32[]{:T(128)}, f32[1,1,512]{2,1,0:T(1,128)S(1)}, f32[1,1,512]{2,1,0:T(1,128)S(1)}, s32[]{:T(128)}, s32[1]{0:T(128)}, /*index=5*/s32[512]{0:T(512)...) while((s32[]{:T(128)}, f32[1,1,512]{2,1,0:T(1,128)S(1)}, ...), condition=%wide.region_15.17_spmd.clone, body=%wide.region_10.16_spmd.clone.sunk | while | flops 70256656 | bytes 2406753 | solution.py:84
  487.4 11.0 while.179
  500.6 195.1 %while.176 = (s32[]{:T(128)}, f32[12,1,1,512]{3,2,1,0:T(1,128)S(1)}, s32[12]{0:T(128)S(1)}, bf16[6144,1,1,128]{3,0,2,1:T(8,128)(2,1)}, s32[6144]{0:T(1024)S(1)},...) while((s32[]{:T(128)}, f32[12,1,1,512]{3,2,1,0:T(1,128)S(1)}, ...), condition=%wide.region_22.25_spmd.clone.clone, body=%wide.region_17.24_spmd.clone.clone.sunk | while | flops 136315408 | bytes 1869574 | solution.py:114
  527.4 8.5 while.180
  542.3 11.4 %while.180 = (s32[]{:T(128)}, f32[1,1,512,128]{3,2,1,0:T(8,128)S(1)}, s32[]{:T(128)}, s32[1]{0:T(128)}, s32[512]{0:T(512)S(1)}, /*index=5*/s32[]{:T(128)}, s32[5...) while((s32[]{:T(128)}, ...), condition=%wide.region_21.23_spmd.clone, body=%wide.region_18.22_spmd.clone.sunk | while | flops 136119296 | bytes 935245 | solution.py:108
  560.1 14.2 %while.180 = (s32[]{:T(128)}, f32[1,1,512,128]{3,2,1,0:T(8,128)S(1)}, s32[]{:T(128)}, s32[1]{0:T(128)}, s32[512]{0:T(512)S(1)}, /*index=5*/s32[]{:T(128)}, s32[5...) while((s32[]{:T(128)}, ...), condition=%wide.region_21.23_spmd.clone, body=%wide.region_18.22_spmd.clone.sunk | while | flops 136119296 | bytes 935245 | solution.py:108
  605.8 9.2 while.180
  621.4 12.0 %while.180 = (s32[]{:T(128)}, f32[1,1,512,128]{3,2,1,0:T(8,128)S(1)}, s32[]{:T(128)}, s32[1]{0:T(128)}, s32[512]{0:T(512)S(1)}, /*index=5*/s32[]{:T(128)}, s32[5...) while((s32[]{:T(128)}, ...), condition=%wide.region_21.23_spmd.clone, body=%wide.region_18.22_spmd.clone.sunk | while | flops 136119296 | bytes 935245 | solution.py:108
  639.8 14.9 %while.180 = (s32[]{:T(128)}, f32[1,1,512,128]{3,2,1,0:T(8,128)S(1)}, s32[]{:T(128)}, s32[1]{0:T(128)}, s32[512]{0:T(512)S(1)}, /*index=5*/s32[]{:T(128)}, s32[5...) while((s32[]{:T(128)}, ...), condition=%wide.region_21.23_spmd.clone, body=%wide.region_18.22_spmd.clone.sunk | while | flops 136119296 | bytes 935245 | solution.py:108
  661.2 17.7 %while.180 = (s32[]{:T(128)}, f32[1,1,512,128]{3,2,1,0:T(8,128)S(1)}, s32[]{:T(128)}, s32[1]{0:T(128)}, s32[512]{0:T(512)S(1)}, /*index=5*/s32[]{:T(128)}, s32[5...) while((s32[]{:T(128)}, ...), condition=%wide.region_21.23_spmd.clone, body=%wide.region_18.22_spmd.clone.sunk | while | flops 136119296 | bytes 935245 | solution.py:108
  685.3 9.2 while.180
  701.3 305.3 %while.178 = (s32[]{:T(128)}, f32[6144,1,1,128]{3,0,2,1:T(8,128)}, f32[6144,1,1,128]{3,0,2,1:T(8,128)}, f32[6144,1,1,128]{3,0,2,1:T(8,128)}, bf16[6144,1,1,128]{...) while((s32[]{:T(128)}, f32[6144,1,1,128]{3,0,2,1:T(8,128)}, ...), condition=%wide.region_28.31_spmd.clone.clone, body=%wide.region_23.30_spmd.clone.clone.sunk | while | flops 338363392 | bytes 9077620 | solution.py:163
  703.1 7.5 while.181
  703.8 6.8 conditional.9
  713.2 15.0 %while.181 = (s32[]{:T(128)}, f32[512,1,1,128]{0,3,2,1:T(8,128)S(1)}, f32[6144,1,1,128]{3,0,2,1:T(8,128)}, f32[6144,1,1,128]{3,0,2,1:T(8,128)}, s32[]{:T(128)}, ...) while((s32[]{:T(128)}, ...), condition=%wide.region_27.29_spmd.clone, body=%wide.region_24.28_spmd.clone.sunk | while | flops 338363392 | bytes 7227857 | solution.py:158
  730.8 22.5 %while.181 = (s32[]{:T(128)}, f32[512,1,1,128]{0,3,2,1:T(8,128)S(1)}, f32[6144,1,1,128]{3,0,2,1:T(8,128)}, f32[6144,1,1,128]{3,0,2,1:T(8,128)}, s32[]{:T(128)}, ...) while((s32[]{:T(128)}, ...), condition=%wide.region_27.29_spmd.clone, body=%wide.region_24.28_spmd.clone.sunk | while | flops 338363392 | bytes 7227857 | solution.py:158
  739.0 6.8 conditional.9
  746.5 6.8 conditional.9
  756.0 30.0 %while.181 = (s32[]{:T(128)}, f32[512,1,1,128]{0,3,2,1:T(8,128)S(1)}, f32[6144,1,1,128]{3,0,2,1:T(8,128)}, f32[6144,1,1,128]{3,0,2,1:T(8,128)}, s32[]{:T(128)}, ...) while((s32[]{:T(128)}, ...), condition=%wide.region_27.29_spmd.clone, body=%wide.region_24.28_spmd.clone.sunk | while | flops 338363392 | bytes 7227857 | solution.py:158
  771.7 6.8 conditional.9
  788.6 37.5 %while.181 = (s32[]{:T(128)}, f32[512,1,1,128]{0,3,2,1:T(8,128)S(1)}, f32[6144,1,1,128]{3,0,2,1:T(8,128)}, f32[6144,1,1,128]{3,0,2,1:T(8,128)}, s32[]{:T(128)}, ...) while((s32[]{:T(128)}, ...), condition=%wide.region_27.29_spmd.clone, body=%wide.region_24.28_spmd.clone.sunk | while | flops 338363392 | bytes 7227857 | solution.py:158
  804.3 6.8 conditional.9
  828.7 11.1 %while.181 = (s32[]{:T(128)}, f32[512,1,1,128]{0,3,2,1:T(8,128)S(1)}, f32[6144,1,1,128]{3,0,2,1:T(8,128)}, f32[6144,1,1,128]{3,0,2,1:T(8,128)}, s32[]{:T(128)}, ...) while((s32[]{:T(128)}, ...), condition=%wide.region_27.29_spmd.clone, body=%wide.region_24.28_spmd.clone.sunk | while | flops 338363392 | bytes 7227857 | solution.py:158
  842.4 11.9 %while.181 = (s32[]{:T(128)}, f32[512,1,1,128]{0,3,2,1:T(8,128)S(1)}, f32[6144,1,1,128]{3,0,2,1:T(8,128)}, f32[6144,1,1,128]{3,0,2,1:T(8,128)}, s32[]{:T(128)}, ...) while((s32[]{:T(128)}, ...), condition=%wide.region_27.29_spmd.clone, body=%wide.region_24.28_spmd.clone.sunk | while | flops 338363392 | bytes 7227857 | solution.py:158
  847.5 6.8 conditional.9
  857.0 19.4 %while.181 = (s32[]{:T(128)}, f32[512,1,1,128]{0,3,2,1:T(8,128)S(1)}, f32[6144,1,1,128]{3,0,2,1:T(8,128)}, f32[6144,1,1,128]{3,0,2,1:T(8,128)}, s32[]{:T(128)}, ...) while((s32[]{:T(128)}, ...), condition=%wide.region_27.29_spmd.clone, body=%wide.region_24.28_spmd.clone.sunk | while | flops 338363392 | bytes 7227857 | solution.py:158
  862.0 6.8 conditional.9
  869.6 6.8 conditional.9
  879.0 26.9 %while.181 = (s32[]{:T(128)}, f32[512,1,1,128]{0,3,2,1:T(8,128)S(1)}, f32[6144,1,1,128]{3,0,2,1:T(8,128)}, f32[6144,1,1,128]{3,0,2,1:T(8,128)}, s32[]{:T(128)}, ...) while((s32[]{:T(128)}, ...), condition=%wide.region_27.29_spmd.clone, body=%wide.region_24.28_spmd.clone.sunk | while | flops 338363392 | bytes 7227857 | solution.py:158
  884.1 6.8 conditional.9
  899.1 6.8 conditional.9
  908.5 34.4 %while.181 = (s32[]{:T(128)}, f32[512,1,1,128]{0,3,2,1:T(8,128)S(1)}, f32[6144,1,1,128]{3,0,2,1:T(8,128)}, f32[6144,1,1,128]{3,0,2,1:T(8,128)}, s32[]{:T(128)}, ...) while((s32[]{:T(128)}, ...), condition=%wide.region_27.29_spmd.clone, body=%wide.region_24.28_spmd.clone.sunk | while | flops 338363392 | bytes 7227857 | solution.py:158
  913.6 6.8 conditional.9
  921.2 6.8 conditional.9
  928.7 6.8 conditional.9
  936.2 6.8 conditional.9
  945.6 42.0 %while.181 = (s32[]{:T(128)}, f32[512,1,1,128]{0,3,2,1:T(8,128)S(1)}, f32[6144,1,1,128]{3,0,2,1:T(8,128)}, f32[6144,1,1,128]{3,0,2,1:T(8,128)}, s32[]{:T(128)}, ...) while((s32[]{:T(128)}, ...), condition=%wide.region_27.29_spmd.clone, body=%wide.region_24.28_spmd.clone.sunk | while | flops 338363392 | bytes 7227857 | solution.py:158
  950.7 6.8 conditional.9
  965.7 6.8 conditional.9
  973.2 6.8 conditional.9
  980.8 6.8 conditional.9
  990.2 15.5 %while.181 = (s32[]{:T(128)}, f32[512,1,1,128]{0,3,2,1:T(8,128)S(1)}, f32[6144,1,1,128]{3,0,2,1:T(8,128)}, f32[6144,1,1,128]{3,0,2,1:T(8,128)}, s32[]{:T(128)}, ...) while((s32[]{:T(128)}, ...), condition=%wide.region_27.29_spmd.clone, body=%wide.region_24.28_spmd.clone.sunk | while | flops 338363392 | bytes 7227857 | solution.py:158
  1010.4 9.2 all-to-all-start.10
  1023.5 19.6 %all-to-all-done.10 = bf16[192,32,1,128]{3,0,2,1:T(8,128)(2,1)S(1)} async-done(((bf16[192,32,1,128]{3,0,2,1:T(8,128)(2,1)}), bf16[192,32,1,128]{3,0,2,1:T(8,128)(2,1)S(1)}, u32[]{:S(2)}, u32[]{:S(2)}) %all-to-all-start.10) | async-done | bytes 1572896 | tf_op jit(solution)/shard_map/all_to_all | solution.py:252
  1051.6 19.6 %all-to-all-done.8 = bf16[192,32,1,128]{3,0,2,1:T(8,128)(2,1)S(1)} async-done(((bf16[192,32,1,128]{3,0,2,1:T(8,128)(2,1)}), bf16[192,32,1,128]{3,0,2,1:T(8,128)(2,1)S(1)}, u32[]{:S(2)}, u32[]{:S(2)}) %all-to-all-start.8) | async-done | bytes 1572896 | tf_op jit(solution)/shard_map/all_to_all | solution.py:244
  1082.5 16.9 %all-to-all-done.9 = bf16[192,32,1,128]{3,0,2,1:T(8,128)(2,1)} async-done(((bf16[192,32,1,128]{3,0,2,1:T(8,128)(2,1)}), bf16[192,32,1,128]{3,0,2,1:T(8,128)(2,1)}, u32[]{:S(2)}, u32[]{:S(2)}) %all-to-all-start.9) | async-done | bytes 1572896 | tf_op jit(solution)/shard_map/all_to_all | solution.py:245
  (1077 shorter events, 808.6 us)
Async XLA Ops:
  0.6 13.8 %copy-start = (bf16[128,1,1,4096]{3,0,2,1:T(8,128)(2,1)S(1)}, bf16[128,1,1,4096]{3,0,2,1:T(8,128)(2,1)}, u32[]{:S(2)}) copy-start(bf16[128,1,1,4096]{3,0,2,1:T(8,128)(2,1)} %param.32) | copy-start | bytes 3145732
  4.0 2.3 copy-start.3
  8.6 18.0 %all-to-all-start.2 = ((bf16[12,16,1024]{2,0,1:T(8,128)(2,1)}), bf16[12,16,1024]{2,0,1:T(8,128)(2,1)S(1)}, u32[]{:S(2)}, u32[]{:S(2)}) async-start(bf16[12,16,1024]{2,0,1:T(8,128)(2,1)} %copy.102), calls=%async_computation.2 | async-start | bytes 1048576 | tf_op jit(solution)/shard_map/all_to_all | solution.py:205
  14.5 2.7 copy-start.2
  26.6 0.8 copy-start.6
  27.4 20.4 %all-to-all-start.6 = ((bf16[12,16,1024]{2,0,1:T(8,128)(2,1)}), bf16[12,16,1024]{2,0,1:T(8,128)(2,1)S(1)}, u32[]{:S(2)}, u32[]{:S(2)}) async-start(bf16[12,16,1024]{2,0,1:T(8,128)(2,1)} %copy.110), calls=%async_computation.6 | async-start | bytes 1048576 | tf_op jit(solution)/shard_map/all_to_all | solution.py:206
  47.8 54.4 %all-to-all-start = ((bf16[12,16,4096]{2,0,1:T(8,128)(2,1)}), bf16[12,16,4096]{2,0,1:T(8,128)(2,1)}, u32[]{:S(2)}, u32[]{:S(2)}) async-start(bf16[12,16,4096]{2,0,1:T(8,128)(2,1)} %copy.98), calls=%async_computation | async-start | bytes 4194304 | tf_op jit(solution)/shard_map/all_to_all | solution.py:204
  102.1 54.0 %all-to-all-start.4 = ((bf16[12,16,4096]{2,0,1:T(8,128)(2,1)}), bf16[12,16,4096]{2,0,1:T(8,128)(2,1)}, u32[]{:S(2)}, u32[]{:S(2)}) async-start(bf16[12,16,4096]{2,0,1:T(8,128)(2,1)} %copy.106), calls=%async_computation.4 | async-start | bytes 4194304 | tf_op jit(solution)/shard_map/all_to_all | solution.py:207
  157.7 9.7 copy-start.7
  157.7 48.3 %all-to-all-start.7 = ((bf16[192,1,32,128]{3,0,1,2:T(8,128)(2,1)}), bf16[192,1,32,128]{3,0,1,2:T(8,128)(2,1)S(1)}, u32[]{:S(2)}, u32[]{:S(2)}) async-start(bf16[192,1,32,128]{3,0,1,2:T(8,128)(2,1)} %bitcast.49), calls=%async_computation.7 | async-start | bytes 3145728 | tf_op jit(solution)/shard_map/all_to_all | solution.py:233
  207.6 43.6 %all-to-all-start.3 = ((bf16[192,1,32,128]{3,0,1,2:T(8,128)(2,1)}), bf16[192,1,32,128]{3,0,1,2:T(8,128)(2,1)S(1)}, u32[]{:S(2)}, u32[]{:S(2)}) async-start(bf16[192,1,32,128]{3,0,1,2:T(8,128)(2,1)} %bitcast.238), calls=%async_computation.3 | async-start | bytes 3145728 | tf_op jit(solution)/shard_map/all_to_all | solution.py:232
  218.0 41.1 %copy-start.9 = (s32[192]{0:T(256)S(1)}, s32[192]{0:T(256)}, u32[]{:S(2)}) copy-start(s32[192]{0:T(256)} %param.33) | copy-start | bytes 2308
  218.0 41.1 %copy-start.10 = (s32[192]{0:T(256)S(1)}, s32[192]{0:T(256)}, u32[]{:S(2)}) copy-start(s32[192]{0:T(256)} %param.34) | copy-start | bytes 2308
  218.0 41.1 %copy-start.8 = (s32[192]{0:T(256)S(1)}, s32[192]{0:T(256)}, u32[]{:S(2)}) copy-start(s32[192]{0:T(256)} %param.35) | copy-start | bytes 2308
  251.2 1.2 copy-start.4
  252.3 44.6 %all-to-all-start.1 = ((bf16[192,1,32,128]{3,0,1,2:T(8,128)(2,1)}), bf16[192,1,32,128]{3,0,1,2:T(8,128)(2,1)}, u32[]{:S(2)}, u32[]{:S(2)}) async-start(bf16[192,1,32,128]{3,0,1,2:T(8,128)(2,1)} %copy.100), calls=%async_computation.1 | async-start | bytes 3145728 | tf_op jit(solution)/shard_map/all_to_all | solution.py:230
  264.3 1.4 copy-start.5
  296.9 201.5 %all-to-all-start.5 = ((bf16[192,1,32,128]{3,0,1,2:T(8,128)(2,1)}), bf16[192,1,32,128]{3,0,1,2:T(8,128)(2,1)S(1)}, u32[]{:S(2)}, u32[]{:S(2)}) async-start(bf16[192,1,32,128]{3,0,1,2:T(8,128)(2,1)} %copy.108), calls=%async_computation.5 | async-start | bytes 3145728 | tf_op jit(solution)/shard_map/all_to_all | solution.py:231
  1010.4 32.7 %all-to-all-start.10 = ((bf16[192,32,1,128]{3,0,2,1:T(8,128)(2,1)}), bf16[192,32,1,128]{3,0,2,1:T(8,128)(2,1)S(1)}, u32[]{:S(2)}, u32[]{:S(2)}) async-start(bf16[192,32,1,128]{3,0,2,1:T(8,128)(2,1)} %copy.121), calls=%async_computation.10 | async-start | bytes 3145728 | tf_op jit(solution)/shard_map/all_to_all | solution.py:252
  1043.1 28.1 %all-to-all-start.8 = ((bf16[192,32,1,128]{3,0,2,1:T(8,128)(2,1)}), bf16[192,32,1,128]{3,0,2,1:T(8,128)(2,1)S(1)}, u32[]{:S(2)}, u32[]{:S(2)}) async-start(bf16[192,32,1,128]{3,0,2,1:T(8,128)(2,1)} %copy.117), calls=%async_computation.8 | async-start | bytes 3145728 | tf_op jit(solution)/shard_map/all_to_all | solution.py:244
  1071.2 28.2 %all-to-all-start.9 = ((bf16[192,32,1,128]{3,0,2,1:T(8,128)(2,1)}), bf16[192,32,1,128]{3,0,2,1:T(8,128)(2,1)}, u32[]{:S(2)}, u32[]{:S(2)}) async-start(bf16[192,32,1,128]{3,0,2,1:T(8,128)(2,1)} %copy.119), calls=%async_computation.9 | async-start | bytes 3145728 | tf_op jit(solution)/shard_map/all_to_all | solution.py:245
  1099.4 3.1 copy-start.1
where the time goes:
time: 1110 us; the launch traced here: 1100 us
  matrix products  309 us (28%)
  loops' own time  273 us (25%)
  waiting for transfers between devices  264 us (24%)
  local copies, waits for them, and re-layouts  142 us (13%)
  starting transfers between devices  73.5 us (7%)
  other arithmetic  40 us (4%)
    dot_general x64, matrix products, pair_logits(): jnp.einsum('qjih,kjh->jiqk', q_block, k_block, preferred_element_type=jnp...  84.6 us
    dot_general x32, matrix products, update(): jnp.einsum('jiqk,qjih->kjih', probs_low, g_block, preferred_element_type=...  62.8 us
    dot_general x32, matrix products, update(): jnp.einsum('jiqk,qjih->kjih', d_logits, q_block, preferred_element_type=j...  62.5 us
    another operation x12, loops' own time, row_norm(): row_high, row_mass = lax.fori_loop(0, q_index + 1, visit_key, initial)  55.8 us
    another operation x12, loops' own time, back_row(): lax.fori_loop(0, q_index + 1, visit_key, (q_start, grad_k, grad_v))  55.7 us
    dot_general x32, matrix products, update(): jnp.einsum('jiqk,kjh->jiqh', weights, v_block, preferred_element_type=jnp...  51.6 us
    all_to_all x1, waiting for transfers between devices, on_device(): lax.all_to_all(pack_rows(grad_src), 'grp', split_axis=1, concat_axis=1, t...  46.8 us
    all_to_all x1, waiting for transfers between devices, on_device(): lax.all_to_all(pack_rows(q_src), 'grp', split_axis=1, concat_axis=1, tile...  44.9 us
  transfers between devices with their start and end apart: 11, of which 10 were waited for; matrix products, arithmetic and copies ran while one was open for 11% of the time, Pallas kernels for 0%

commit v1 on v0

v1 whole, which is shorter than its diff:
```python
import functools, math
import jax, jax.numpy as jnp
from jax import lax
from jax.experimental import pallas as pl
from jax.experimental.pallas import tpu as pltpu
from jax.sharding import Mesh, PartitionSpec as P

HEADS = 32
KV_HEADS = 8
HEAD_DIM = 128

CAPB=12
NT=(((1,),(1,)),((),()))
TN=(((0,),(0,)),((),()))
NN=(((1,),(0,)),((),()))
f32=jnp.float32; bf16=jnp.bfloat16

def dot(a,b,dims):
    return lax.dot_general(a,b,dims,preferred_element_type=f32)

def attn_kernel(first_ref, r_ref, kv_ref, dq_ref, dkv_ref, qg, s_scr, p_scr, dk_acc, dv_acc, dq_acc, *, WS, ngrp, nsp, hd):
    i=pl.program_id(0)
    cap=CAPB
    unit=ngrp*nsp
    c2=math.log2(math.e)/math.sqrt(hd)
    xs=kv_ref.shape[0]; tq=unit//xs
    rows=2*cap
    @pl.when(i==0)
    def _():
        n=ngrp*rows
        ri=lax.broadcasted_iota(jnp.int32,(n,n),0); ci=lax.broadcasted_iota(jnp.int32,(n,n),1)
        perm=jnp.where((ri//ngrp==ci%rows)&(ri%ngrp==ci//rows),1.0,0.0).astype(bf16)
        def one(s,_):
            blk=r_ref[:,s].reshape(n,hd)
            o=dot(perm,blk,NN).astype(bf16)
            qg[:,pl.ds(pl.multiple_of(s*ngrp,ngrp),ngrp),:]=o.reshape(rows,ngrp,hd)
            return 0
        lax.fori_loop(0,nsp,one,0)
    f=first_ref[i]
    at=pl.multiple_of(i*ngrp,ngrp)
    @pl.when(f<0)
    def _():
        z=jnp.zeros((nsp,ngrp,hd),bf16)
        dq_ref[:,pl.ds(at,ngrp),:]=z
        dkv_ref[:,pl.ds(at,ngrp),:]=z
        dkv_ref[:,pl.ds(pl.multiple_of(cap*ngrp+at,ngrp),ngrp),:]=z
    @pl.when(f>=0)
    def _():
        q=qg[i]; g=qg[cap+i]
        def kvb(row):
            return kv_ref[:,row].reshape(unit,hd)
        def pos(axis,base,shape):
            p=lax.broadcasted_iota(jnp.int32,shape,axis)+base
            return (p%ngrp)*nsp+p//ngrp
        def score(j,slot,st,masked):
            m,l,d=st
            kj=kvb(j); vj=kvb(cap+j)
            ss=[]
            mx=m
            for w in range(0,unit,WS):
                s=dot(kj[w:w+WS],q,NT)
                if masked:
                    s=jnp.where(pos(0,w,(WS,unit))<=pos(1,0,(WS,unit)),s,-1e30)
                s_scr[slot,w:w+WS,:]=s
                mx=jnp.maximum(mx,jnp.max(s,axis=0,keepdims=True))
            al=jnp.exp2((m-mx)*c2)
            l=l*al; d=d*al
            for w in range(0,unit,WS):
                dp=dot(vj[w:w+WS],g,NT)
                p_scr[slot,w:w+WS,:]=dp
                e=jnp.exp2((s_scr[slot,w:w+WS,:]-mx)*c2)
                l=l+jnp.sum(e,axis=0,keepdims=True)
                d=d+jnp.sum(e*dp,axis=0,keepdims=True)
            return mx,l,d
        st=(jnp.full((1,unit),-1e30,f32),jnp.zeros((1,unit),f32),jnp.zeros((1,unit),f32))
        st=score(i,i-f,st,True)
        st=lax.fori_loop(f,i,lambda j,s: score(j,j-f,s,False),st)
        m,l,d=st
        L=m*c2+jnp.log2(l)
        delta=d/l
        def back(j,slot,first):
            kj=kvb(j)
            acc=None
            for w in range(0,unit,WS):
                p=jnp.exp2(s_scr[slot,w:w+WS,:]*c2-L)
                ds=(p*(p_scr[slot,w:w+WS,:]-delta)).astype(bf16)
                dv=dot(p.astype(bf16),g,NN)
                dk=dot(ds,q,NN)
                t=dot(ds,kj[w:w+WS],TN)
                acc=t if acc is None else acc+t
                if first:
                    dv_acc[j,w:w+WS,:]=dv; dk_acc[j,w:w+WS,:]=dk
                else:
                    dv_acc[j,w:w+WS,:]+=dv; dk_acc[j,w:w+WS,:]+=dk
            if first: dq_acc[...]=acc
            else: dq_acc[...]+=acc
        back(i,i-f,True)
        def bl(j,_):
            back(j,j-f,False); return 0
        lax.fori_loop(f,i,bl,0)
        sc=1.0/math.sqrt(hd)
        dq_ref[:,pl.ds(at,ngrp),:]=(dq_acc[...]*sc).astype(bf16).reshape(nsp,ngrp,hd)
        nxt=jnp.where(i==cap-1,cap,first_ref[jnp.minimum(i+1,cap-1)])
        @pl.when(jnp.logical_or(nxt<0,nxt>i))
        def _():
            def put(j,_):
                aj=pl.multiple_of(j*ngrp,ngrp)
                dkv_ref[:,pl.ds(aj,ngrp),:]=(dk_acc[j]*sc).astype(bf16).reshape(nsp,ngrp,hd)
                dkv_ref[:,pl.ds(pl.multiple_of(cap*ngrp+aj,ngrp),ngrp),:]=dv_acc[j].astype(bf16).reshape(nsp,ngrp,hd)
                return 0
            lax.fori_loop(f,i+1,put,0)

def attention(first, r, kv, WS=128):
    ngrp,nsp,rows,hd=r.shape
    cap=rows//2; unit=ngrp*nsp
    full=lambda shape: pl.BlockSpec(shape, lambda i,*_: (0,)*len(shape))
    return pl.pallas_call(
        functools.partial(attn_kernel,WS=WS,ngrp=ngrp,nsp=nsp,hd=hd),
        out_shape=(jax.ShapeDtypeStruct((nsp,cap*ngrp,hd),bf16),jax.ShapeDtypeStruct((nsp,2*cap*ngrp,hd),bf16)),
        grid_spec=pltpu.PrefetchScalarGridSpec(
            num_scalar_prefetch=1, grid=(cap,),
            in_specs=[full(r.shape),full(kv.shape)],
            out_specs=(full((nsp,cap*ngrp,hd)),full((nsp,2*cap*ngrp,hd))),
            scratch_shapes=[pltpu.VMEM((rows,unit,hd),bf16),pltpu.VMEM((5,unit,unit),f32),pltpu.VMEM((5,unit,unit),f32),
                pltpu.VMEM((cap,unit,hd),f32),pltpu.VMEM((cap,unit,hd),f32),pltpu.VMEM((unit,hd),f32)]),
        compiler_params=pltpu.CompilerParams(vmem_limit_bytes=56*2**20,dimension_semantics=("arbitrary",)),
        name="attention",
    )(first,r,kv)


def pack_kernel(want_ref, a_ref, b_ref, out_ref):
    rows = want_ref.shape[0]
    units = a_ref.shape[0]
    groups, wide, _, per, width = out_ref.shape
    both = jnp.concatenate([a_ref[...], b_ref[...]], axis=0)
    column = lax.broadcasted_iota(jnp.int32, (rows, 2 * units), 1)
    pick = jnp.where(column == want_ref[...], 1.0, 0.0).astype(bf16)
    moved = dot(pick, both, NN).astype(bf16)
    for x in range(wide):
        out_ref[:, x, 0] = moved[:, x * width:(x + 1) * width].reshape(groups, per, width)


def pack(want, a, b, groups, wide):
    units, columns = a.shape
    rows = want.shape[0]
    steps = columns // (wide * HEAD_DIM)
    step_in = pl.BlockSpec((units, wide * HEAD_DIM), lambda y: (0, y))
    return pl.pallas_call(
        pack_kernel,
        out_shape=jax.ShapeDtypeStruct((groups, wide, steps, rows // groups, HEAD_DIM), bf16),
        grid=(steps,),
        in_specs=[pl.BlockSpec((rows, 1), lambda y: (0, 0)), step_in, step_in],
        out_specs=pl.BlockSpec((groups, wide, 1, rows // groups, HEAD_DIM), lambda y: (0, 0, y, 0, 0)),
        compiler_params=pltpu.CompilerParams(vmem_limit_bytes=32 * 2**20),
        name="pack",
    )(want, a, b)


def plan(doc_lengths, doc_groups, doc_offsets, units, groups, cap):
    starts = jnp.cumsum(doc_lengths) - doc_lengths
    place = jnp.arange(groups * cap, dtype=jnp.int32)
    low = doc_groups * cap + doc_offsets
    inside = (place[:, None] >= low[None, :]) & (place[:, None] < (low + doc_lengths)[None, :])
    source = jnp.sum(jnp.where(inside, (starts - low)[None, :] + place[:, None] + 1, 0), axis=1) - 1
    first = jnp.sum(jnp.where(inside, doc_offsets[None, :] + 1, 0), axis=1) - 1
    return source.reshape(groups, cap), first.reshape(groups, cap)


def on_device(q_src, k_src, v_src, grad_src, doc_lengths, doc_groups, doc_offsets):
    groups, n_x, n_y = lax.axis_size("grp"), lax.axis_size("x"), lax.axis_size("y")
    n_sp = n_x * n_y
    units = q_src.shape[0]
    cap = doc_lengths.shape[0] // groups
    source, first = plan(doc_lengths, doc_groups, doc_offsets, units, groups, cap)
    first_mine = lax.dynamic_index_in_dim(first, lax.axis_index("grp"), 0, keepdims=False)
    want = jnp.concatenate([source, jnp.where(source >= 0, source + units, -1)], axis=1).reshape(-1, 1)

    flat = lambda array: array.reshape(units, array.shape[-1])
    kv_out = pack(want, flat(k_src), flat(v_src), groups, 1)
    qg_out = pack(want, flat(q_src), flat(grad_src), groups, n_x)

    kv_in = lax.all_to_all(kv_out.reshape(groups * n_y, 2 * cap, HEAD_DIM), ("grp", "y"), 0, 0, tiled=True)
    kv_in = kv_in.reshape(groups, n_y, 2 * cap, HEAD_DIM).transpose(2, 1, 0, 3)
    kv_all = lax.all_gather(kv_in.reshape(2 * cap, n_y * groups, HEAD_DIM), "x", axis=0)
    qg_in = lax.all_to_all(qg_out.reshape(groups * n_sp, 2 * cap, HEAD_DIM), ("grp", "x", "y"), 0, 0, tiled=True)
    dq, dkv = attention(first_mine, qg_in.reshape(groups, n_sp, 2 * cap, HEAD_DIM), kv_all)

    dq_home = lax.all_to_all(dq, ("x", "y"), 0, 0, tiled=True)
    dkv_sum = lax.psum_scatter(dkv.reshape(n_x, n_y, 2 * cap * groups, HEAD_DIM), "x", scatter_dimension=0)
    dkv_home = lax.all_to_all(dkv_sum, "y", 0, 0, tiled=True)
    rows = cap * groups
    dq_out = dq_home.reshape(n_x, n_y, rows, HEAD_DIM).transpose(2, 1, 0, 3).reshape(1, rows, 1, HEADS * HEAD_DIM)
    dk_out = dkv_home[:, :rows].transpose(1, 0, 2).reshape(1, rows, 1, KV_HEADS * HEAD_DIM)
    dv_out = dkv_home[:, rows:].transpose(1, 0, 2).reshape(1, rows, 1, KV_HEADS * HEAD_DIM)
    return dq_out, dk_out, dv_out


def solution(mesh):
    groups = mesh.shape["grp"]
    split = Mesh(mesh.devices.reshape(groups, HEADS // KV_HEADS, KV_HEADS), ("grp", "x", "y"))
    placed = P(None, "grp", ("x", "y"), None)
    out = P("grp", None, ("x", "y"), None)
    return jax.shard_map(
        on_device,
        mesh=split,
        in_specs=(placed,) * 4 + (P(),) * 3,
        out_specs=(out,) * 3,
        check_vma=False,
    )
```

time: 1110 us -> 278 us (0.25)
  the two profiles are of different devices: /device:TPU:457 before, /device:TPU:193 now
where the time goes in v1:
time: 278 us; the launch traced here: 277 us
  waiting for transfers between devices  126 us (45%)
  Pallas kernels  43.1 us (16%)
  blocking collectives  39.5 us (14%)
  starting transfers between devices  34.9 us (13%)
  local copies, waits for them, and re-layouts  17.4 us (6%)
  between operations  14.2 us (5%)
    all_to_all x1, waiting for transfers between devices, on_device(): lax.all_to_all(qg_out.reshape(groups * n_sp, 2 * cap, HEAD_DIM), ('grp',...  70.5 us
    all_to_all x1, blocking collectives, on_device(): dq_home = lax.all_to_all(dq, ('x', 'y'), 0, 0, tiled=True)  39.5 us
    pallas_call x1, Pallas kernels, attention(): pl.pallas_call(functools.partial(attn_kernel, WS=WS, ngrp=ngrp, nsp=nsp,...  34.2 us
    all_to_all x1, waiting for transfers between devices, on_device(): dkv_home = lax.all_to_all(dkv_sum, 'y', 0, 0, tiled=True)  20.1 us
    reduce_scatter x1, waiting for transfers between devices, on_device(): lax.psum_scatter(dkv.reshape(n_x, n_y, 2 * cap * groups, HEAD_DIM), 'x',...  17.7 us
    all_to_all x1, waiting for transfers between devices, on_device(): lax.all_to_all(kv_out.reshape(groups * n_y, 2 * cap, HEAD_DIM), ('grp', '...  17.7 us
    all_to_all x1, starting transfers between devices, on_device(): lax.all_to_all(kv_out.reshape(groups * n_y, 2 * cap, HEAD_DIM), ('grp', '...  15.3 us
    all_to_all x1, starting transfers between devices, on_device(): lax.all_to_all(qg_out.reshape(groups * n_sp, 2 * cap, HEAD_DIM), ('grp',...  14 us
  transfers between devices with their start and end apart: 5, of which 4 were waited for; matrix products, arithmetic and copies ran while one was open for 2% of the time, Pallas kernels for 2%

profile of v1, /device:TPU:193, one launch (start us, length us, event | category | flops | bytes accessed | tf_op | source)
XLA Modules:
  0.0 277.3 jit_solution(2801738135428385435)
XLA Ops:
  7.2 0.0 copy-start.1
  7.2 0.0 copy-start
  7.2 0.8 pad_bitcast_fusion
  8.0 0.3 reduce-window.9
  8.3 0.1 slice.16
  8.4 0.1 slice_reduce_fusion
  8.6 0.1 add_bitcast_fusion
  8.6 0.7 fusion.1
  9.3 0.7 subtract_subtract_fusion
  10.0 0.2 select_reduce_fusion
  10.2 0.1 sub.21
  10.3 0.1 add.66
  10.4 0.1 pad_add_fusion
  10.5 0.1 reshape.93.want_ref
  10.6 0.0 copy-start.2
  10.6 0.9 copy-done.2
  11.6 0.0 copy-start.3
  11.6 0.9 copy-done.3
  12.5 4.0 %pack.3 = bf16[16,1,8,24,128]{4,3,2,1,0:T(8,128)(2,1)} custom-call(s32[384,1]{1,0:T(8,128)S(1)} %reshape.93.want_ref, bf16[128,1024]{1,0:T(8,128)(2,1)S(1)} %bitcast.28, bf16[128,1024]{1,0:T(8,128)(2,1)S(1)} %bitcast.29), custom_call_target="tpu_custom_call" | custom-call | tf_op jit(solution)/shard_map/pack/pallas_call | solution.py:148
  16.5 15.3 %all-to-all-start.1 = ((bf16[128,24,128]{2,1,0:T(8,128)(2,1)}), bf16[128,24,128]{2,1,0:T(8,128)(2,1)S(1)}, u32[]{:S(2)}, u32[]{:S(2)}) async-start(bf16[128,24,128]{2,1,0:T(8,128)(2,1)} %bitcast.9), calls=%async_computation.1 | async-start | bytes 1572864 | tf_op jit(solution)/shard_map/all_to_all | solution.py:182
  31.8 0.0 copy-done.1
  31.8 0.0 copy-done
  31.8 5.0 %pack.2 = bf16[16,4,8,24,128]{4,3,2,1,0:T(8,128)(2,1)} custom-call(s32[384,1]{1,0:T(8,128)S(1)} %reshape.93.want_ref, bf16[128,4096]{1,0:T(8,128)(2,1)S(1)} %bitcast.26, bf16[128,4096]{1,0:T(8,128)(2,1)S(1)} %bitcast.27), custom_call_target="tpu_custom_call" | custom-call | tf_op jit(solution)/shard_map/pack/pallas_call | solution.py:148
  36.8 17.7 %all-to-all-done.1 = bf16[128,24,128]{2,1,0:T(8,128)(2,1)S(1)} async-done(((bf16[128,24,128]{2,1,0:T(8,128)(2,1)}), bf16[128,24,128]{2,1,0:T(8,128)(2,1)S(1)}, u32[]{:S(2)}, u32[]{:S(2)}) %all-to-all-start.1) | async-done | bytes 786464 | tf_op jit(solution)/shard_map/all_to_all | solution.py:182
  54.4 0.0 copy-start.5
  54.4 0.9 copy-done.5
  55.3 14.0 %all-to-all-start = ((bf16[512,24,128]{2,1,0:T(8,128)(2,1)}), bf16[512,24,128]{2,1,0:T(8,128)(2,1)S(1)}, u32[]{:S(2)}, u32[]{:S(2)}) async-start(bf16[512,24,128]{2,1,0:T(8,128)(2,1)} %bitcast.5), calls=%async_computation | async-start | bytes 6291456 | tf_op jit(solution)/shard_map/all_to_all | solution.py:185
  69.3 0.0 all-gather.2.cloned.1.call-start
  69.4 2.5 copy.32
  71.9 0.0 all-gather.2.cloned.1.call-update
  71.9 0.0 reduce-scatter.2.cloned.1.call-start
  72.0 0.1 sub.17
  72.0 0.5 dynamic-slice_bitcast_fusion.first_ref
  72.6 70.5 %all-to-all-done = bf16[512,24,128]{2,1,0:T(8,128)(2,1)S(1)} async-done(((bf16[512,24,128]{2,1,0:T(8,128)(2,1)}), bf16[512,24,128]{2,1,0:T(8,128)(2,1)S(1)}, u32[]{:S(2)}, u32[]{:S(2)}) %all-to-all-start) | async-done | bytes 3145760 | tf_op jit(solution)/shard_map/all_to_all | solution.py:185
  143.1 0.0 copy-start.4
  143.1 0.0 all-gather.2.cloned.1.call-done.kv_ref
  143.1 1.7 copy-done.4
  144.8 34.2 %attention.1 = (bf16[32,192,128]{2,1,0:T(8,128)(2,1)}, bf16[32,384,128]{2,1,0:T(8,128)(2,1)}) custom-call(s32[12]{0:T(128)} %dynamic-slice_bitcast_fusion.first_ref, bf16[16,32,24,128]{3,2,1,0:T(8,128)(2,1)} %bitcast.30, bf16[4,24,128,128]{3,2,1,0:T(8,128)(2,1)} %all-gather.2.cloned.1.call-done.kv_ref), custom_call_target="tpu_custom_call" | custom-call | tf_op jit(solution)/shard_map/attention/pallas_call | solution.py:117
  179.0 0.0 copy-start.6
  179.0 0.0 reduce-scatter.2.cloned.1.call-update
  179.1 1.4 copy-done.6
  180.4 39.5 %all_to_all.20 = bf16[32,192,128]{2,1,0:T(8,128)(2,1)S(1)} all-to-all(bf16[32,192,128]{2,1,0:T(8,128)(2,1)S(1)} %copy-done.6), channel_id=1, replica_groups=mesh['grp'=16,'x'=4,'y'=8] {'x','y'}, dimensions={0} | all-to-all | bytes 3145728 | tf_op jit(solution)/shard_map/all_to_all | solution.py:188
  220.0 17.7 %reduce-scatter.2.cloned.1.call-done = bf16[1,8,384,128]{3,2,1,0:T(8,128)(2,1)} async-done(((bf16[4,8,384,128]{3,2,1,0:T(8,128)(2,1)}), bf16[1,8,384,128]{3,2,1,0:T(8,128)(2,1)}) %reduce-scatter.2.cloned.1.call-update) | async-done | bytes 786448 | tf_op jit(solution)/shard_map/reduce_scatter | solution.py:189
  237.7 5.6 %all-to-all-start.3 = ((bf16[8,384,128]{2,1,0:T(8,128)(2,1)}), bf16[8,384,128]{2,1,0:T(8,128)(2,1)}, u32[]{:S(2)}, u32[]{:S(2)}) async-start(bf16[8,384,128]{2,1,0:T(8,128)(2,1)} %bitcast.35), calls=%async_computation.4 | async-start | bytes 1572864 | tf_op jit(solution)/shard_map/all_to_all | solution.py:190
  243.3 1.2 copy.33
  244.5 2.4 reshape.89
  246.9 20.1 %all-to-all-done.3 = bf16[8,384,128]{2,1,0:T(8,128)(2,1)} async-done(((bf16[8,384,128]{2,1,0:T(8,128)(2,1)}), bf16[8,384,128]{2,1,0:T(8,128)(2,1)}, u32[]{:S(2)}, u32[]{:S(2)}) %all-to-all-start.3) | async-done | bytes 786464 | tf_op jit(solution)/shard_map/all_to_all | solution.py:190
  267.0 1.2 slice_bitcast_fusion
  268.1 0.3 copy.35
  268.4 0.9 reshape.92
  269.3 0.3 copy.34
  269.6 0.9 reshape.91
  (3 shorter events, 0.0 us)
Async XLA Ops:
  7.2 24.6 %copy-start.1 = (bf16[128,1,1,4096]{3,0,2,1:T(8,128)(2,1)S(1)}, bf16[128,1,1,4096]{3,0,2,1:T(8,128)(2,1)}, u32[]{:S(2)}) copy-start(bf16[128,1,1,4096]{3,0,2,1:T(8,128)(2,1)} %param.10) | copy-start | bytes 3145732
  7.2 24.6 %copy-start = (bf16[128,1,1,4096]{3,0,2,1:T(8,128)(2,1)S(1)}, bf16[128,1,1,4096]{3,0,2,1:T(8,128)(2,1)}, u32[]{:S(2)}) copy-start(bf16[128,1,1,4096]{3,0,2,1:T(8,128)(2,1)} %param.7) | copy-start | bytes 3145732
  10.6 1.0 copy-start.2
  11.6 0.9 copy-start.3
  16.5 38.0 %all-to-all-start.1 = ((bf16[128,24,128]{2,1,0:T(8,128)(2,1)}), bf16[128,24,128]{2,1,0:T(8,128)(2,1)S(1)}, u32[]{:S(2)}, u32[]{:S(2)}) async-start(bf16[128,24,128]{2,1,0:T(8,128)(2,1)} %bitcast.9), calls=%async_computation.1 | async-start | bytes 1572864 | tf_op jit(solution)/shard_map/all_to_all | solution.py:182
  54.4 0.9 copy-start.5
  55.3 87.8 %all-to-all-start = ((bf16[512,24,128]{2,1,0:T(8,128)(2,1)}), bf16[512,24,128]{2,1,0:T(8,128)(2,1)S(1)}, u32[]{:S(2)}, u32[]{:S(2)}) async-start(bf16[512,24,128]{2,1,0:T(8,128)(2,1)} %bitcast.5), calls=%async_computation | async-start | bytes 6291456 | tf_op jit(solution)/shard_map/all_to_all | solution.py:185
  69.3 73.8 %all-gather.2.cloned.1.call-start = ((), (), s32[]{:S(2)}) async-start(), calls=%async_computation.5 | async-start | bytes 3932160 | tf_op jit(solution)/shard_map/all_gather | solution.py:184
  71.9 165.8 %reduce-scatter.2.cloned.1.call-start = ((), (), s32[]{:S(2)}) async-start(), calls=%async_computation.6 | async-start | bytes 3932160 | tf_op jit(solution)/shard_map/reduce_scatter | solution.py:189
  143.1 1.7 copy-start.4
  179.0 1.4 copy-start.6
  237.7 29.3 %all-to-all-start.3 = ((bf16[8,384,128]{2,1,0:T(8,128)(2,1)}), bf16[8,384,128]{2,1,0:T(8,128)(2,1)}, u32[]{:S(2)}, u32[]{:S(2)}) async-start(bf16[8,384,128]{2,1,0:T(8,128)(2,1)} %bitcast.35), calls=%async_computation.4 | async-start | bytes 1572864 | tf_op jit(solution)/shard_map/all_to_all | solution.py:190
Sparse Core Ops, SparseCore 0:
  72.2 68.4 all-gather.1
  179.2 58.4 reduce-scatter.1

commit v2 on v1

v2 whole, which is shorter than its diff:
```python
import functools
import math

import jax
import jax.numpy as jnp
from jax import lax
from jax.experimental import pallas as pl
from jax.experimental.pallas import tpu as pltpu
from jax.sharding import Mesh, PartitionSpec as P

HEADS = 32
KV_HEADS = 8
HEAD_DIM = 128
MAXDOC = 5
EARLY = 4
NN = (((1,), (0,)), ((), ()))
NT = (((1,), (1,)), ((), ()))
TN = (((0,), (0,)), ((), ()))
f32 = jnp.float32
bf16 = jnp.bfloat16
NEG_FILL = -1e30


def dot(a, b, dims):
    return lax.dot_general(a, b, dims, preferred_element_type=f32)


def attention_kernel(begin, count, cap, n_x, has_carry, dqt, *refs):
    first_ref, where_ref, in_ref = refs[:3]
    k_refs, v_refs = refs[3:3 + n_x], refs[3 + n_x:3 + 2 * n_x]
    refs = refs[3 + 2 * n_x:]
    if has_carry:
        k_carry, v_carry, dq_ref = refs[:3]
        dk_refs, dv_refs = refs[3:3 + n_x], refs[3 + n_x:3 + 2 * n_x]
        queries, s_keep, p_keep, k_acc, v_acc, q_acc = refs[3 + 2 * n_x:]
    else:
        dq_ref, k_acc, v_acc, queries, s_keep, p_keep, q_acc = refs
    groups, n_y, rows, head_dim = in_ref.shape
    heads = n_x
    part = groups * n_y
    span = heads * part
    per = 2 * count
    factor = 1.0 / math.sqrt(head_dim)
    power = math.log2(math.e) * factor
    my_x = where_ref[0]

    mixed = groups * per
    row = lax.broadcasted_iota(jnp.int32, (mixed, mixed), 0)
    col = lax.broadcasted_iota(jnp.int32, (mixed, mixed), 1)
    turn = jnp.where((row // groups == col % per) & (row % groups == col // per), 1.0, 0.0).astype(bf16)

    def sort_y(y, _):
        taken = jnp.concatenate(
            [in_ref[:, y, h * per:(h + 1) * per, :].reshape(mixed, head_dim) for h in range(heads)], axis=1)
        turned = dot(turn, taken, NN).astype(bf16)
        for h in range(heads):
            at = pl.multiple_of(h * part + y * groups, groups)
            queries[:, pl.ds(at, groups), :] = (
                turned[:, h * head_dim:(h + 1) * head_dim].reshape(per, groups, head_dim))
        return 0

    lax.fori_loop(0, n_y, sort_y, 0)

    def put(block):
        at = pl.multiple_of(block * groups, groups)
        for x in range(n_x):
            dk_refs[x][:, pl.ds(at, groups), :] = (k_acc[x, block] * factor).astype(bf16).reshape(n_y, groups, head_dim)
            dv_refs[x][:, pl.ds(at, groups), :] = v_acc[x, block].astype(bf16).reshape(n_y, groups, head_dim)

    if has_carry:
        k_acc[:, :begin] = k_carry[...]
        v_acc[:, :begin] = v_carry[...]
        low = first_ref[begin]
        low = jnp.where(low < 0, begin, jnp.minimum(low, begin))
        lax.fori_loop(0, low, lambda block, _: (put(block), 0)[1], 0)

    key_row = lax.broadcasted_iota(jnp.int32, (part, span), 0)
    query_col = lax.broadcasted_iota(jnp.int32, (part, span), 1) % part
    key_pos = (key_row % groups) * (n_x * n_y) + key_row // groups
    query_pos = (query_col % groups) * (n_x * n_y) + query_col // groups + my_x * n_y

    def one_block(block, _):
        low = first_ref[block]
        local = block - begin
        at = pl.multiple_of(local * groups, groups)

        @pl.when(low < 0)
        def _():
            dq_ref[:, pl.ds(at, groups), :] = jnp.zeros((n_y, groups, heads * head_dim), bf16)
            zero = jnp.zeros((part, head_dim), f32)
            for x in range(n_x):
                k_acc[x, block] = zero
                v_acc[x, block] = zero
            if has_carry:
                put(block)

        @pl.when(low >= 0)
        def _():
            q = queries[local]
            g = queries[count + local]

            def score(key, stats, masked):
                high, mass, mean = stats
                slot = key - low
                top = high
                for x in range(n_x):
                    s = dot(k_refs[x][key], q, NT)
                    if masked:
                        x_of = lax.rem(my_x + x, n_x) * n_y
                        s = jnp.where(key_pos + x_of <= query_pos, s, NEG_FILL)
                    s_keep[slot, x] = s
                    top = jnp.maximum(top, jnp.max(s, axis=0, keepdims=True))
                shrink = jnp.exp2((high - top) * power)
                mass = mass * shrink
                mean = mean * shrink
                for x in range(n_x):
                    dp = dot(v_refs[x][key], g, NT)
                    p_keep[slot, x] = dp
                    e = jnp.exp2((s_keep[slot, x] - top) * power)
                    mass = mass + jnp.sum(e, axis=0, keepdims=True)
                    mean = mean + jnp.sum(e * dp, axis=0, keepdims=True)
                return top, mass, mean

            none = jnp.zeros((1, span), f32)
            stats = score(block, (none + NEG_FILL, none, none), True)
            stats = lax.fori_loop(low, block, lambda key, stats: score(key, stats, False), stats)
            high, mass, mean = stats
            norm = high * power + jnp.log2(mass)
            delta = mean / mass

            def back(key, fresh):
                slot = key - low
                total = None
                for x in range(n_x):
                    p = jnp.exp2(s_keep[slot, x] * power - norm)
                    ds = (p * (p_keep[slot, x] - delta)).astype(bf16)
                    dv = dot(p.astype(bf16), g, NN)
                    dk = dot(ds, q, NN)
                    if dqt:
                        dq = dot(k_refs[x][key], ds, TN)
                    else:
                        dq = dot(ds, k_refs[x][key], TN)
                    total = dq if total is None else total + dq
                    if fresh:
                        v_acc[x, key] = dv
                        k_acc[x, key] = dk
                    else:
                        v_acc[x, key] += dv
                        k_acc[x, key] += dk
                if fresh:
                    q_acc[...] = total
                else:
                    q_acc[...] += total

            back(block, True)
            lax.fori_loop(low, block, lambda key, _: (back(key, False), 0)[1], 0)
            for h in range(heads):
                if dqt:
                    mine = (q_acc[:, h * part:(h + 1) * part] * factor).T.astype(bf16)
                else:
                    mine = (q_acc[h * part:(h + 1) * part, :] * factor).astype(bf16)
                dq_ref[:, pl.ds(at, groups), h * head_dim:(h + 1) * head_dim] = mine.reshape(n_y, groups, head_dim)

            if has_carry:
                after = first_ref[jnp.minimum(block + 1, cap - 1)]

                @pl.when((block == cap - 1) | (after < 0) | (after > block))
                def _():
                    lax.fori_loop(low, block + 1, lambda key, _: (put(key), 0)[1], 0)
        return 0

    lax.fori_loop(begin, begin + count, one_block, 0)


def attention(first, my_x, packed, keys, values, begin, count, carry=None, dqt=False):
    groups, n_y, rows, head_dim = packed.shape
    n_x = len(keys)
    cap = first.shape[0]
    part = groups * n_y
    span = n_x * part
    vmem = pl.BlockSpec(memory_space=pltpu.VMEM)
    smem = pl.BlockSpec(memory_space=pltpu.SMEM)
    shape = jax.ShapeDtypeStruct
    dq = shape((n_y, count * groups, n_x * head_dim), bf16)
    slots = MAXDOC if carry is not None else min(MAXDOC, count)
    scratch = [
        pltpu.VMEM((2 * count, span, head_dim), bf16),
        pltpu.VMEM((slots, n_x, part, span), f32),
        pltpu.VMEM((slots, n_x, part, span), f32),
    ]
    sums = (n_x, begin + count, part, head_dim)
    total = [pltpu.VMEM((head_dim, span) if dqt else (span, head_dim), f32)]
    if carry is None:
        out = (dq, shape(sums, f32), shape(sums, f32))
        carry = ()
        scratch = scratch + total
    else:
        out = (dq,) + (shape((n_y, cap * groups, head_dim), bf16),) * (2 * n_x)
        scratch = scratch + [pltpu.VMEM(sums, f32)] * 2 + total
    pairs = count * 2
    return pl.pallas_call(
        functools.partial(attention_kernel, begin, count, cap, n_x, bool(carry), dqt),
        out_shape=out,
        in_specs=[smem, smem] + [vmem] * (1 + 2 * n_x + len(carry)),
        out_specs=(vmem,) * len(out),
        scratch_shapes=scratch,
        compiler_params=pltpu.CompilerParams(vmem_limit_bytes=48 * 2**20),
        cost_estimate=pl.CostEstimate(
            flops=pairs * 10 * span * span * head_dim, bytes_accessed=8 * 2**20, transcendentals=pairs * 2 * span * span),
        name="attention",
    )(first, my_x, packed, *keys, *values, *carry)


def pack_kernel(begin, count, cap, with_kv, *refs):
    lens_ref, groups_ref, offsets_ref, q_ref, g_ref = refs[:5]
    if with_kv:
        k_ref, v_ref, out_ref, pick, pick_kv = refs[5:]
    else:
        out_ref, pick = refs[5:]
    n_grp = out_ref.shape[0]
    units = q_ref.shape[0]
    head_dim = out_ref.shape[3]
    per = 2 * count

    @pl.when(pl.program_id(0) == 0)
    def _():
        lens = lens_ref[...]
        docs = lens.shape[1]
        before = lax.broadcasted_iota(jnp.int32, (docs, docs), 0) < lax.broadcasted_iota(jnp.int32, (docs, docs), 1)
        many = jnp.broadcast_to(lens, (16, docs)).astype(f32).astype(bf16)
        start = dot(many, jnp.where(before, 1.0, 0.0).astype(bf16), NN)[:1].astype(jnp.int32)
        low = groups_ref[...] * cap + offsets_ref[...]

        def choose(first, blocks, into):
            rows = n_grp * 2 * blocks
            row = lax.broadcasted_iota(jnp.int32, (rows, docs), 0)
            place = row // (2 * blocks) * cap + first + row % blocks
            inside = (place >= low) & (place < low + lens)
            source = jnp.sum(jnp.where(inside, start - low + place + 1, 0), axis=1, keepdims=True) - 1
            kind = lax.broadcasted_iota(jnp.int32, (rows, 1), 0) // blocks % 2
            wanted = jnp.where(source >= 0, source + kind * units, -1)
            column = lax.broadcasted_iota(jnp.int32, (rows, 2 * units), 1)
            into[...] = jnp.where(column == wanted, 1.0, 0.0).astype(bf16)

        choose(begin, count, pick)
        if with_kv:
            choose(0, cap, pick_kv)

    moved = dot(pick[...], jnp.concatenate([q_ref[...], g_ref[...]], axis=0), NN)
    heads = moved.shape[1] // head_dim
    for h in range(heads):
        slab = moved[:, h * head_dim:(h + 1) * head_dim].reshape(n_grp, per, head_dim)
        out_ref[:, 0, h * per:(h + 1) * per, :] = slab.astype(bf16)
    if with_kv:
        both = dot(pick_kv[...], jnp.concatenate([k_ref[...], v_ref[...]], axis=0), NN)
        out_ref[:, 0, heads * per:, :] = both.reshape(n_grp, 2 * cap, head_dim).astype(bf16)


def pack(tables, q, g, kv, n_grp, n_y, begin, count, cap):
    units = q.shape[0]
    heads = q.shape[1] // (n_y * HEAD_DIM)
    rows = heads * 2 * count + (2 * cap if kv else 0)
    table = pl.BlockSpec((1, tables[0].shape[1]), lambda y: (0, 0))
    wide = pl.BlockSpec((units, heads * HEAD_DIM), lambda y: (0, y))
    thin = pl.BlockSpec((units, HEAD_DIM), lambda y: (0, y))
    scratch = [pltpu.VMEM((n_grp * 2 * count, 2 * units), bf16)]
    if kv:
        scratch.append(pltpu.VMEM((n_grp * 2 * cap, 2 * units), bf16))
    return pl.pallas_call(
        functools.partial(pack_kernel, begin, count, cap, bool(kv)),
        out_shape=jax.ShapeDtypeStruct((n_grp, n_y, rows, HEAD_DIM), bf16),
        grid=(n_y,),
        in_specs=[table] * 3 + [wide] * 2 + [thin] * len(kv),
        out_specs=pl.BlockSpec((n_grp, 1, rows, HEAD_DIM), lambda y: (0, y, 0, 0)),
        scratch_shapes=scratch,
        compiler_params=pltpu.CompilerParams(vmem_limit_bytes=24 * 2**20),
        cost_estimate=pl.CostEstimate(flops=2 * 10**9, bytes_accessed=6 * 2**20, transcendentals=0),
        name="pack",
    )(*tables, q, g, *kv)


def add_kernel(*refs):
    out_ref = refs[-1]
    rows = out_ref.shape[1] // 2
    for half in range(2):
        a, b, c = refs[3 * half:3 * half + 3]
        total = a[...].astype(f32) + b[...].astype(f32) + c[...].astype(f32)
        out_ref[:, half * rows:(half + 1) * rows, :] = total.astype(bf16)


def add_up(dk_parts, dv_parts):
    n_y, rows, head_dim = dk_parts[0].shape
    vmem = pl.BlockSpec(memory_space=pltpu.VMEM)
    return pl.pallas_call(
        add_kernel,
        out_shape=jax.ShapeDtypeStruct((n_y, 2 * rows, head_dim), bf16),
        in_specs=[vmem] * 6,
        out_specs=vmem,
        compiler_params=pltpu.CompilerParams(vmem_limit_bytes=16 * 2**20),
        name="add_up",
    )(*dk_parts, *dv_parts)


def lay_kernel(pieces, *refs):
    sources = 1 + max(piece[0] for piece in pieces)
    for source, row, rows, target, at in pieces:
        taken, out_ref = refs[source], refs[sources + target]
        n_y, _, width = taken.shape
        for y in range(n_y):
            out_ref[at:at + rows, y * width:(y + 1) * width] = taken[y, row:row + rows, :]


def lay_out(arrays, pieces, shapes):
    vmem = pl.BlockSpec(memory_space=pltpu.VMEM)
    return pl.pallas_call(
        functools.partial(lay_kernel, pieces),
        out_shape=tuple(jax.ShapeDtypeStruct(shape, bf16) for shape in shapes),
        in_specs=[vmem] * len(arrays),
        out_specs=(vmem,) * len(shapes),
        compiler_params=pltpu.CompilerParams(vmem_limit_bytes=16 * 2**20),
        name="lay_out",
    )(*arrays)


def first_blocks(doc_lengths, doc_groups, doc_offsets, cap):
    place = jnp.arange(cap, dtype=jnp.int32)[:, None]
    here = (doc_groups == lax.axis_index("grp"))[None, :]
    member = here & (doc_offsets[None, :] <= place) & (place < (doc_offsets + doc_lengths)[None, :])
    return jnp.sum(jnp.where(member, doc_offsets[None, :] + 1, 0), axis=1) - 1


def step(array, by):
    n_x = lax.axis_size("x")
    return lax.ppermute(array, "x", [(i, (i + by) % n_x) for i in range(n_x)])


def on_device(q_src, k_src, v_src, grad_src, doc_lengths, doc_groups, doc_offsets):
    n_grp, n_x, n_y = lax.axis_size("grp"), lax.axis_size("x"), lax.axis_size("y")
    units = q_src.shape[0]
    docs = doc_lengths.shape[0]
    cap = docs // n_grp
    split = EARLY
    tables = tuple(table.reshape(1, docs) for table in (doc_lengths, doc_groups, doc_offsets))
    q, k, v, g = (array.reshape(units, array.shape[-1]) for array in (q_src, k_src, v_src, grad_src))

    def exchange(message):
        rows = message.shape[2]
        home = lax.all_to_all(message.reshape(n_grp * n_y, rows, HEAD_DIM), ("grp", "y"), 0, 0, tiled=True)
        return home.reshape(n_grp, n_y, rows, HEAD_DIM)

    early = exchange(pack(tables, q, g, (k, v), n_grp, n_y, 0, split, cap))
    late = exchange(pack(tables, q, g, (), n_grp, n_y, split, cap - split, cap))

    at = n_x * 2 * split
    k0, v0 = (
        early[:, :, at + i * cap:at + (i + 1) * cap].transpose(2, 1, 0, 3).reshape(cap, n_y * n_grp, HEAD_DIM)
        for i in range(2)
    )
    k3, v1 = step(k0, 1), step(v0, -1)
    v3, k1 = step(v0, 1), step(k0, -1)
    k2, v2 = step(k3, 1), step(v1, -1)
    keys, values = (k0, k1, k2, k3), (v0, v1, v2, v3)

    first = first_blocks(doc_lengths, doc_groups, doc_offsets, cap)
    my_x = lax.axis_index("x").astype(jnp.int32).reshape(1)
    dq_early, k_sums, v_sums = attention(first, my_x, early, keys, values, 0, split)
    dq_late, *grads = attention(first, my_x, late, keys, values, split, cap - split, (k_sums, v_sums))
    dk, dv = grads[:n_x], grads[n_x:]

    dq_early = lax.all_to_all(dq_early, "y", 0, 0, tiled=True)
    dq_late = lax.all_to_all(dq_late, "y", 0, 0, tiled=True)

    def joined(mine, came):
        return (mine.astype(f32) + came.astype(f32)).astype(bf16)

    k_far, v_far = step(dk[2], 1), step(dv[2], -1)
    v_up, k_down = step(dv[1], 1), step(dk[3], -1)
    k_up, v_down = step(joined(dk[1], k_far), 1), step(joined(dv[3], v_far), -1)
    sums = add_up((dk[0], k_up, k_down), (dv[0], v_up, v_down))
    sums = lax.all_to_all(sums, "y", 0, 0, tiled=True)

    rows, near = cap * n_grp, split * n_grp
    (dq_out,) = lay_out(
        (dq_early, dq_late), ((0, 0, near, 0, 0), (1, 0, rows - near, 0, near)), ((rows, HEADS * HEAD_DIM),))
    dk_out, dv_out = lay_out((sums,), ((0, 0, rows, 0, 0), (0, rows, rows, 1, 0)), ((rows, KV_HEADS * HEAD_DIM),) * 2)
    return tuple(array.reshape(1, rows, 1, array.shape[-1]) for array in (dq_out, dk_out, dv_out))


def solution(mesh):
    groups = mesh.shape["grp"]
    split = Mesh(mesh.devices.reshape(groups, HEADS // KV_HEADS, KV_HEADS), ("grp", "x", "y"))
    placed = P(None, "grp", ("x", "y"), None)
    out = P("grp", None, ("x", "y"), None)
    return jax.shard_map(
        on_device,
        mesh=split,
        in_specs=(placed,) * 4 + (P(),) * 3,
        out_specs=(out,) * 3,
        check_vma=False,
    )
```

time: 278 us -> 238 us (0.86)
  waiting for transfers between devices: 126 us -> 79 us
  starting transfers between devices: 34.9 us -> 79.7 us
  blocking collectives: 39.5 us -> 0 us
  Pallas kernels: 43.1 us -> 59.7 us
  between operations: 14.2 us -> 0.97 us
    all_to_all x3 -> x5, waiting for transfers between devices: 108 us -> 58.1 us  [the longest x2 44.4 us: exchange(): lax.all_to_all(message.reshape(n_grp * n_y, rows, HEAD_DIM), ('grp', 'y')...]
    all_to_all x1 -> x0, blocking collectives: 39.5 us -> none  [on_device(): dq_home = lax.all_to_all(dq, ('x', 'y'), 0, 0, tiled=True)]
    ppermute x0 -> x12, starting transfers between devices: none -> 36.5 us  [step(): return lax.ppermute(array, 'x', [(i, (i + by) % n_x) for i in range(n_x)])]
    ppermute x0 -> x12, waiting for transfers between devices: none -> 20.9 us  [step(): return lax.ppermute(array, 'x', [(i, (i + by) % n_x) for i in range(n_x)])]
    reduce_scatter x1 -> x0, waiting for transfers between devices: 17.7 us -> none  [on_device(): lax.psum_scatter(dkv.reshape(n_x, n_y, 2 * cap * groups, HEAD_DIM), 'x',...]
    pallas_call x3 -> x7, Pallas kernels: 43.1 us -> 59.7 us  [the longest x2 46.7 us: attention(): pl.pallas_call(functools.partial(attention_kernel, begin, count, cap, n_x...]
    unnamed x14 -> x56, local copies, waits for them, and re-layouts: 5.85 us -> 15.4 us
    all_to_all x3 -> x5, starting transfers between devices: 34.9 us -> 43.2 us  [the longest x2 25.5 us: exchange(): lax.all_to_all(message.reshape(n_grp * n_y, rows, HEAD_DIM), ('grp', 'y')...]
  transfers between devices with their start and end apart: 5 -> 17, of which waited for: 4 -> 10; matrix products, arithmetic and copies ran while one was open for 2% -> 1% of each run, Pallas kernels for 2% -> 23%
where the time goes in v2:
time: 238 us; the launch traced here: 237 us
  starting transfers between devices  79.7 us (33%)
  waiting for transfers between devices  79 us (33%)
  Pallas kernels  59.7 us (25%)
  local copies, waits for them, and re-layouts  17.4 us (7%)
    pallas_call x2, Pallas kernels, attention(): pl.pallas_call(functools.partial(attention_kernel, begin, count, cap, n_x...  46.7 us
    all_to_all x2, waiting for transfers between devices, exchange(): lax.all_to_all(message.reshape(n_grp * n_y, rows, HEAD_DIM), ('grp', 'y')...  44.4 us
    ppermute x12, starting transfers between devices, step(): return lax.ppermute(array, 'x', [(i, (i + by) % n_x) for i in range(n_x)])  36.5 us
    all_to_all x2, starting transfers between devices, exchange(): lax.all_to_all(message.reshape(n_grp * n_y, rows, HEAD_DIM), ('grp', 'y')...  25.5 us
    ppermute x12, waiting for transfers between devices, step(): return lax.ppermute(array, 'x', [(i, (i + by) % n_x) for i in range(n_x)])  20.9 us
    unnamed x56, local copies, waits for them, and re-layouts  15.4 us
    all_to_all x1, waiting for transfers between devices, on_device(): sums = lax.all_to_all(sums, 'y', 0, 0, tiled=True)  13.7 us
    pallas_call x2, Pallas kernels, pack(): pl.pallas_call(functools.partial(pack_kernel, begin, count, cap, bool(kv)...  9.48 us
  transfers between devices with their start and end apart: 17, of which 10 were waited for; matrix products, arithmetic and copies ran while one was open for 1% of the time, Pallas kernels for 23%

profile of v2, /device:TPU:193, one launch (start us, length us, event | category | flops | bytes accessed | tf_op | source)
XLA Modules:
  0.0 237.1 jit_solution(11162468273335299061)
XLA Ops:
  0.6 0.0 copy-start
  0.6 0.7 copy-done
  1.3 0.7 copy-done.2
  2.0 0.7 copy-done.4
  2.7 1.2 copy-done.6
  3.9 1.2 copy-done.8
  5.1 0.9 copy-done.24
  6.1 0.9 copy-done.25
  7.0 4.9 %pack.2 = bf16[16,8,56,128]{3,2,1,0:T(8,128)(2,1)} custom-call(s32[1,192]{1,0:T(1,128)S(1)} %bitcast.33, s32[1,192]{1,0:T(1,128)S(1)} %bitcast.31, s32[1,192]{1,0:T(1,128)S(1)} %bitcast.29, bf16[128,4096]{1,0:T(8,128)(2,1)S(1)} %bitcast.35, bf16[128,4096]{1,0:T(8,128)(2,1)S(1)} %bitcast.37, bf16[128,1024]{1,0:T(8,128)(2,1)S(1)} %bitcast.39, ...), custom_call_target="tpu_custom_call" | custom-call | flops 2000000000 | bytes 6291456 | tf_op jit(solution)/shard_map/pack/pallas_call | solution.py:269
  12.0 0.0 copy-start.9
  12.0 15.8 %all-to-all-start = ((bf16[128,56,128]{2,1,0:T(8,128)(2,1)}), bf16[128,56,128]{2,1,0:T(8,128)(2,1)}, u32[]{:S(2)}, u32[]{:S(2)}) async-start(bf16[128,56,128]{2,1,0:T(8,128)(2,1)} %bitcast.8), calls=%async_computation | async-start | bytes 3670016 | tf_op jit(solution)/shard_map/all_to_all | solution.py:348
  27.9 4.5 %pack.3 = bf16[16,8,64,128]{3,2,1,0:T(8,128)(2,1)} custom-call(s32[1,192]{1,0:T(1,128)S(1)} %bitcast.34, s32[1,192]{1,0:T(1,128)S(1)} %bitcast.32, s32[1,192]{1,0:T(1,128)S(1)} %bitcast.30, bf16[128,4096]{1,0:T(8,128)(2,1)S(1)} %bitcast.36, bf16[128,4096]{1,0:T(8,128)(2,1)S(1)} %bitcast.38), custom_call_target="tpu_custom_call" | custom-call | flops 2000000000 | bytes 6291456 | tf_op jit(solution)/shard_map/pack/pallas_call | solution.py:269
  32.4 40.1 %all-to-all-done = bf16[128,56,128]{2,1,0:T(8,128)(2,1)} async-done(((bf16[128,56,128]{2,1,0:T(8,128)(2,1)}), bf16[128,56,128]{2,1,0:T(8,128)(2,1)}, u32[]{:S(2)}, u32[]{:S(2)}) %all-to-all-start) | async-done | bytes 1835040 | tf_op jit(solution)/shard_map/all_to_all | solution.py:348
  72.6 9.6 %all-to-all-start.2 = ((bf16[128,64,128]{2,1,0:T(8,128)(2,1)}), bf16[128,64,128]{2,1,0:T(8,128)(2,1)}, u32[]{:S(2)}, u32[]{:S(2)}) async-start(bf16[128,64,128]{2,1,0:T(8,128)(2,1)} %bitcast.14), calls=%async_computation.2 | async-start | bytes 4194304 | tf_op jit(solution)/shard_map/all_to_all | solution.py:348
  82.2 1.5 slice_bitcast_fusion
  83.7 0.3 copy.13
  84.0 0.3 copy.12
  84.2 3.1 %collective-permute-start.1 = (bf16[12,128,128]{2,1,0:T(8,128)(2,1)S(1)}, bf16[12,128,128]{2,1,0:T(8,128)(2,1)S(1)}, u32[]{:S(2)}, u32[]{:S(2)}) collective-permute-start(bf16[12,128,128]{2,1,0:T(8,128)(2,1)S(1)} %bitcast.25), channel_id=1, source_target_pairs={{0,8},{8,16},{16,24},{24,0},{1,9},{9,17},{17,25},{25,1},{2,10},{10... | collective-permute-start | bytes 1179656 | tf_op jit(solution)/shard_map/ppermute | solution.py:334
  87.4 3.4 %collective-permute-start.3 = (bf16[12,128,128]{2,1,0:T(8,128)(2,1)S(1)}, bf16[12,128,128]{2,1,0:T(8,128)(2,1)S(1)}, u32[]{:S(2)}, u32[]{:S(2)}) collective-permute-start(bf16[12,128,128]{2,1,0:T(8,128)(2,1)S(1)} %bitcast.21), channel_id=1, source_target_pairs={{0,24},{8,0},{16,8},{24,16},{1,25},{9,1},{17,9},{25,17},{2,26},{10... | collective-permute-start | bytes 1179656 | tf_op jit(solution)/shard_map/ppermute | solution.py:334
  90.8 3.2 %collective-permute-start = (bf16[12,128,128]{2,1,0:T(8,128)(2,1)S(1)}, bf16[12,128,128]{2,1,0:T(8,128)(2,1)S(1)}, u32[]{:S(2)}, u32[]{:S(2)}) collective-permute-start(bf16[12,128,128]{2,1,0:T(8,128)(2,1)S(1)} %bitcast.26), channel_id=1, source_target_pairs={{0,24},{8,0},{16,8},{24,16},{1,25},{9,1},{17,9},{25,17},{2,26},{10... | collective-permute-start | bytes 1179656 | tf_op jit(solution)/shard_map/ppermute | solution.py:334
  93.9 2.1 collective-permute-start.5
  96.1 1.8 collective-permute-done.1.refs_6_
  97.8 1.9 collective-permute-start.2
  99.7 0.0 collective-permute-done.3.refs_8_
  99.7 4.6 %collective-permute-start.4 = (bf16[12,128,128]{2,1,0:T(8,128)(2,1)S(1)}, bf16[12,128,128]{2,1,0:T(8,128)(2,1)S(1)}, u32[]{:S(2)}, u32[]{:S(2)}) collective-permute-start(bf16[12,128,128]{2,1,0:T(8,128)(2,1)S(1)} %collective-permute-done.3.refs_8_), channel_id=1, source_target_pairs={{0,24},{8,0},{16,8},{24,16},{1,25},{9,1},{17,9},{25,17},{2,26},{10... | collective-permute-start | bytes 1179656 | tf_op jit(solution)/shard_map/ppermute | solution.py:334
  104.3 0.1 select_reduce_fusion
  104.5 3.4 %collective-permute-done.refs_4_ = bf16[12,128,128]{2,1,0:T(8,128)(2,1)S(1)} collective-permute-done((bf16[12,128,128]{2,1,0:T(8,128)(2,1)S(1)}, bf16[12,128,128]{2,1,0:T(8,128)(2,1)S(1)}, u32[]{:S(2)}, u32[]{:S(2)}) %collective-permute-start) | collective-permute-done | bytes 393248 | tf_op jit(solution)/shard_map/ppermute | solution.py:334
  107.8 7.2 %collective-permute-done.2.refs_5_ = bf16[12,128,128]{2,1,0:T(8,128)(2,1)S(1)} collective-permute-done((bf16[12,128,128]{2,1,0:T(8,128)(2,1)S(1)}, bf16[12,128,128]{2,1,0:T(8,128)(2,1)S(1)}, u32[]{:S(2)}, u32[]{:S(2)}) %collective-permute-start.2) | collective-permute-done | bytes 393248 | tf_op jit(solution)/shard_map/ppermute | solution.py:334
  115.0 1.2 collective-permute-done.4.refs_9_
  116.3 9.8 %attention.2 = (bf16[8,64,512]{2,1,0:T(8,128)(2,1)}, f32[4,4,128,128]{3,2,1,0:T(8,128)S(1)}, f32[4,4,128,128]{3,2,1,0:T(8,128)S(1)}) custom-call(s32[12]{0:T(128)S(1)} %broadcast_add_fusion.1.refs_0_, s32[1]{0:T(128)} %bitcast.refs_1_, bf16[16,8,56,128]{3,2,1,0:T(8,128)(2,1)} %bitcast.9.refs_2_, bf16[12,128,128]{2,1,0:T(8,128)(2,1)S(1)} %bitcast.27, ...), custom_call_target="tpu_custom_call" | custom-call | flops 2684354560 | bytes 8388608 | tf_op jit(solution)/shard_map/attention/pallas_call | solution.py:201
  126.1 0.0 copy-start.26
  126.1 1.0 copy-done.26
  127.0 1.0 copy-done.27
  128.0 4.2 %all-to-all-done.2 = bf16[128,64,128]{2,1,0:T(8,128)(2,1)} async-done(((bf16[128,64,128]{2,1,0:T(8,128)(2,1)}), bf16[128,64,128]{2,1,0:T(8,128)(2,1)}, u32[]{:S(2)}, u32[]{:S(2)}) %all-to-all-start.2) | async-done | bytes 2097184 | tf_op jit(solution)/shard_map/all_to_all | solution.py:348
  132.3 4.3 %all-to-all-start.1 = ((bf16[8,64,512]{2,1,0:T(8,128)(2,1)}), bf16[8,64,512]{2,1,0:T(8,128)(2,1)S(1)}, u32[]{:S(2)}, u32[]{:S(2)}) async-start(bf16[8,64,512]{2,1,0:T(8,128)(2,1)} %get-tuple-element.17), calls=%async_computation.1 | async-start | bytes 1048576 | tf_op jit(solution)/shard_map/all_to_all | solution.py:370
  136.6 1.0 copy-done.11
  137.6 1.0 copy-done.13
  138.6 1.0 copy-done.18
  139.6 1.0 copy-done.21
  140.5 36.9 %attention.3 = (bf16[8,128,512]{2,1,0:T(8,128)(2,1)}, bf16[8,192,128]{2,1,0:T(8,128)(2,1)S(1)}, bf16[8,192,128]{2,1,0:T(8,128)(2,1)S(1)}, bf16[8,192,128]{2,1,0:...) custom-call(s32[12]{0:T(128)S(1)} %broadcast_add_fusion.1.refs_0_, ...), custom_call_target="tpu_custom_call" | custom-call | flops 5368709120 | bytes 8388608 | tf_op jit(solution)/shard_map/attention/pallas_call | solution.py:201
  177.4 0.7 copy-done.15
  178.2 0.7 copy-done.19
  178.9 0.8 copy-done.22
  179.7 0.7 copy-done.23
  180.4 0.0 all-to-all-done.1.refs_0_
  180.4 6.8 %all-to-all-start.3 = ((bf16[8,128,512]{2,1,0:T(8,128)(2,1)}), bf16[8,128,512]{2,1,0:T(8,128)(2,1)S(1)}, u32[]{:S(2)}, u32[]{:S(2)}) async-start(bf16[8,128,512]{2,1,0:T(8,128)(2,1)} %get-tuple-element.20), calls=%async_computation.3 | async-start | bytes 2097152 | tf_op jit(solution)/shard_map/all_to_all | solution.py:371
  187.2 3.1 %collective-permute-start.6 = (bf16[8,192,128]{2,1,0:T(8,128)(2,1)}, bf16[8,192,128]{2,1,0:T(8,128)(2,1)S(1)}, u32[]{:S(2)}, u32[]{:S(2)}) collective-permute-start(bf16[8,192,128]{2,1,0:T(8,128)(2,1)} %copy-done.23), channel_id=1, source_target_pairs={{0,8},{8,16},{16,24},{24,0},{1,9},{9,17},{17,25},{25,1},{2,10},{10... | collective-permute-start | bytes 1179656 | tf_op jit(solution)/shard_map/ppermute | solution.py:334
  190.3 3.4 %collective-permute-start.10 = (bf16[8,192,128]{2,1,0:T(8,128)(2,1)}, bf16[8,192,128]{2,1,0:T(8,128)(2,1)S(1)}, u32[]{:S(2)}, u32[]{:S(2)}) collective-permute-start(bf16[8,192,128]{2,1,0:T(8,128)(2,1)} %copy-done.22), channel_id=1, source_target_pairs={{0,24},{8,0},{16,8},{24,16},{1,25},{9,1},{17,9},{25,17},{2,26},{10... | collective-permute-start | bytes 1179656 | tf_op jit(solution)/shard_map/ppermute | solution.py:334
  193.7 3.2 %collective-permute-start.8 = (bf16[8,192,128]{2,1,0:T(8,128)(2,1)}, bf16[8,192,128]{2,1,0:T(8,128)(2,1)S(1)}, u32[]{:S(2)}, u32[]{:S(2)}) collective-permute-start(bf16[8,192,128]{2,1,0:T(8,128)(2,1)} %copy-done.19), channel_id=1, source_target_pairs={{0,24},{8,0},{16,8},{24,16},{1,25},{9,1},{17,9},{25,17},{2,26},{10... | collective-permute-start | bytes 1179656 | tf_op jit(solution)/shard_map/ppermute | solution.py:334
  196.9 2.1 collective-permute-start.9
  199.0 2.7 %collective-permute-done.6 = bf16[8,192,128]{2,1,0:T(8,128)(2,1)S(1)} collective-permute-done((bf16[8,192,128]{2,1,0:T(8,128)(2,1)}, bf16[8,192,128]{2,1,0:T(8,128)(2,1)S(1)}, u32[]{:S(2)}, u32[]{:S(2)}) %collective-permute-start.6) | collective-permute-done | bytes 393248 | tf_op jit(solution)/shard_map/ppermute | solution.py:334
  201.7 0.1 add_convert_fusion.1
  201.8 1.9 collective-permute-start.7
  203.8 0.0 collective-permute-done.10
  203.8 0.1 add_convert_fusion
  203.9 4.6 %collective-permute-start.11 = (bf16[8,192,128]{2,1,0:T(8,128)(2,1)S(1)}, bf16[8,192,128]{2,1,0:T(8,128)(2,1)S(1)}, u32[]{:S(2)}, u32[]{:S(2)}) collective-permute-start(bf16[8,192,128]{2,1,0:T(8,128)(2,1)S(1)} %add_convert_fusion), channel_id=1, source_target_pairs={{0,24},{8,0},{16,8},{24,16},{1,25},{9,1},{17,9},{25,17},{2,26},{10... | collective-permute-start | bytes 1179656 | tf_op jit(solution)/shard_map/ppermute | solution.py:334
  208.5 0.0 collective-permute-done.9.refs_4_
  208.5 3.1 %collective-permute-done.7.refs_1_ = bf16[8,192,128]{2,1,0:T(8,128)(2,1)S(1)} collective-permute-done((bf16[8,192,128]{2,1,0:T(8,128)(2,1)S(1)}, bf16[8,192,128]{2,1,0:T(8,128)(2,1)S(1)}, u32[]{:S(2)}, u32[]{:S(2)}) %collective-permute-start.7) | collective-permute-done | bytes 393248 | tf_op jit(solution)/shard_map/ppermute | solution.py:334
  211.6 1.6 collective-permute-done.11.refs_5_
  213.2 1.2 add_up.1
  214.4 6.6 %all-to-all-start.4 = ((bf16[8,384,128]{2,1,0:T(8,128)(2,1)}), bf16[8,384,128]{2,1,0:T(8,128)(2,1)S(1)}, u32[]{:S(2)}, u32[]{:S(2)}) async-start(bf16[8,384,128]{2,1,0:T(8,128)(2,1)} %add_up.1), calls=%async_computation.4 | async-start | bytes 1572864 | tf_op jit(solution)/shard_map/all_to_all | solution.py:380
  221.0 1.2 lay_out.2
  222.3 13.7 %all-to-all-done.4.refs_0_ = bf16[8,384,128]{2,1,0:T(8,128)(2,1)S(1)} async-done(((bf16[8,384,128]{2,1,0:T(8,128)(2,1)}), bf16[8,384,128]{2,1,0:T(8,128)(2,1)S(1)}, u32[]{:S(2)}, u32[]{:S(2)}) %all-to-all-start.4) | async-done | bytes 786464 | tf_op jit(solution)/shard_map/all_to_all | solution.py:380
  236.0 1.1 lay_out.3
  (42 shorter events, 0.1 us)
Async XLA Ops:
  0.6 0.7 copy-start
  1.3 0.7 copy-start.2
  2.0 0.7 copy-start.4
  2.7 1.2 copy-start.6
  3.9 1.2 copy-start.8
  5.1 0.9 copy-start.24
  6.1 0.9 copy-start.25
  12.0 15.9 %copy-start.1 = (s32[192]{0:T(256)S(1)}, s32[192]{0:T(256)}, u32[]{:S(2)}) copy-start(s32[192]{0:T(256)} %param.13) | copy-start | bytes 2308
  12.0 15.9 %copy-start.3 = (s32[192]{0:T(256)S(1)}, s32[192]{0:T(256)}, u32[]{:S(2)}) copy-start(s32[192]{0:T(256)} %param.12) | copy-start | bytes 2308
  12.0 15.9 %copy-start.5 = (s32[192]{0:T(256)S(1)}, s32[192]{0:T(256)}, u32[]{:S(2)}) copy-start(s32[192]{0:T(256)} %param.11) | copy-start | bytes 2308
  12.0 15.9 %copy-start.7 = (bf16[128,1,1,4096]{3,0,2,1:T(8,128)(2,1)S(1)}, bf16[128,1,1,4096]{3,0,2,1:T(8,128)(2,1)}, u32[]{:S(2)}) copy-start(bf16[128,1,1,4096]{3,0,2,1:T(8,128)(2,1)} %param.7) | copy-start | bytes 3145732
  12.0 15.9 %copy-start.9 = (bf16[128,1,1,4096]{3,0,2,1:T(8,128)(2,1)S(1)}, bf16[128,1,1,4096]{3,0,2,1:T(8,128)(2,1)}, u32[]{:S(2)}) copy-start(bf16[128,1,1,4096]{3,0,2,1:T(8,128)(2,1)} %param.10) | copy-start | bytes 3145732
  12.0 60.6 %all-to-all-start = ((bf16[128,56,128]{2,1,0:T(8,128)(2,1)}), bf16[128,56,128]{2,1,0:T(8,128)(2,1)}, u32[]{:S(2)}, u32[]{:S(2)}) async-start(bf16[128,56,128]{2,1,0:T(8,128)(2,1)} %bitcast.8), calls=%async_computation | async-start | bytes 3670016 | tf_op jit(solution)/shard_map/all_to_all | solution.py:348
  72.6 59.7 %all-to-all-start.2 = ((bf16[128,64,128]{2,1,0:T(8,128)(2,1)}), bf16[128,64,128]{2,1,0:T(8,128)(2,1)}, u32[]{:S(2)}, u32[]{:S(2)}) async-start(bf16[128,64,128]{2,1,0:T(8,128)(2,1)} %bitcast.14), calls=%async_computation.2 | async-start | bytes 4194304 | tf_op jit(solution)/shard_map/all_to_all | solution.py:348
  84.2 13.6 %collective-permute-start.1 = (bf16[12,128,128]{2,1,0:T(8,128)(2,1)S(1)}, bf16[12,128,128]{2,1,0:T(8,128)(2,1)S(1)}, u32[]{:S(2)}, u32[]{:S(2)}) collective-permute-start(bf16[12,128,128]{2,1,0:T(8,128)(2,1)S(1)} %bitcast.25), channel_id=1, source_target_pairs={{0,8},{8,16},{16,24},{24,0},{1,9},{9,17},{17,25},{25,1},{2,10},{10... | collective-permute-start | bytes 1179656 | tf_op jit(solution)/shard_map/ppermute | solution.py:334
  87.4 12.4 %collective-permute-start.3 = (bf16[12,128,128]{2,1,0:T(8,128)(2,1)S(1)}, bf16[12,128,128]{2,1,0:T(8,128)(2,1)S(1)}, u32[]{:S(2)}, u32[]{:S(2)}) collective-permute-start(bf16[12,128,128]{2,1,0:T(8,128)(2,1)S(1)} %bitcast.21), channel_id=1, source_target_pairs={{0,24},{8,0},{16,8},{24,16},{1,25},{9,1},{17,9},{25,17},{2,26},{10... | collective-permute-start | bytes 1179656 | tf_op jit(solution)/shard_map/ppermute | solution.py:334
  90.8 17.1 %collective-permute-start = (bf16[12,128,128]{2,1,0:T(8,128)(2,1)S(1)}, bf16[12,128,128]{2,1,0:T(8,128)(2,1)S(1)}, u32[]{:S(2)}, u32[]{:S(2)}) collective-permute-start(bf16[12,128,128]{2,1,0:T(8,128)(2,1)S(1)} %bitcast.26), channel_id=1, source_target_pairs={{0,24},{8,0},{16,8},{24,16},{1,25},{9,1},{17,9},{25,17},{2,26},{10... | collective-permute-start | bytes 1179656 | tf_op jit(solution)/shard_map/ppermute | solution.py:334
  93.9 13.9 %collective-permute-start.5 = (bf16[12,128,128]{2,1,0:T(8,128)(2,1)S(1)}, bf16[12,128,128]{2,1,0:T(8,128)(2,1)S(1)}, u32[]{:S(2)}, u32[]{:S(2)}) collective-permute-start(bf16[12,128,128]{2,1,0:T(8,128)(2,1)S(1)} %bitcast.22), channel_id=1, source_target_pairs={{0,8},{8,16},{16,24},{24,0},{1,9},{9,17},{17,25},{25,1},{2,10},{10... | collective-permute-start | bytes 1179656 | tf_op jit(solution)/shard_map/ppermute | solution.py:334
  97.8 17.2 %collective-permute-start.2 = (bf16[12,128,128]{2,1,0:T(8,128)(2,1)S(1)}, bf16[12,128,128]{2,1,0:T(8,128)(2,1)S(1)}, u32[]{:S(2)}, u32[]{:S(2)}) collective-permute-start(bf16[12,128,128]{2,1,0:T(8,128)(2,1)S(1)} %collective-permute-done.1.refs_6_), channel_id=1, source_target_pairs={{0,8},{8,16},{16,24},{24,0},{1,9},{9,17},{17,25},{25,1},{2,10},{10... | collective-permute-start | bytes 1179656 | tf_op jit(solution)/shard_map/ppermute | solution.py:334
  99.7 26.3 %copy-start.10 = (bf16[12,128,128]{2,1,0:T(8,128)(2,1)}, bf16[12,128,128]{2,1,0:T(8,128)(2,1)S(1)}, u32[]{:S(2)}) copy-start(bf16[12,128,128]{2,1,0:T(8,128)(2,1)S(1)} %collective-permute-done.3.refs_8_) | copy-start | bytes 1179652
  99.7 16.5 %collective-permute-start.4 = (bf16[12,128,128]{2,1,0:T(8,128)(2,1)S(1)}, bf16[12,128,128]{2,1,0:T(8,128)(2,1)S(1)}, u32[]{:S(2)}, u32[]{:S(2)}) collective-permute-start(bf16[12,128,128]{2,1,0:T(8,128)(2,1)S(1)} %collective-permute-done.3.refs_8_), channel_id=1, source_target_pairs={{0,24},{8,0},{16,8},{24,16},{1,25},{9,1},{17,9},{25,17},{2,26},{10... | collective-permute-start | bytes 1179656 | tf_op jit(solution)/shard_map/ppermute | solution.py:334
  107.8 18.2 %copy-start.12 = (bf16[12,128,128]{2,1,0:T(8,128)(2,1)}, bf16[12,128,128]{2,1,0:T(8,128)(2,1)S(1)}, u32[]{:S(2)}) copy-start(bf16[12,128,128]{2,1,0:T(8,128)(2,1)S(1)} %collective-permute-done.refs_4_) | copy-start | bytes 1179652
  107.8 18.2 %copy-start.14 = (bf16[12,128,128]{2,1,0:T(8,128)(2,1)}, bf16[12,128,128]{2,1,0:T(8,128)(2,1)S(1)}, u32[]{:S(2)}) copy-start(bf16[12,128,128]{2,1,0:T(8,128)(2,1)S(1)} %collective-permute-done.5.refs_10_) | copy-start | bytes 1179652
  115.0 11.0 %copy-start.17 = (bf16[12,128,128]{2,1,0:T(8,128)(2,1)}, bf16[12,128,128]{2,1,0:T(8,128)(2,1)S(1)}, u32[]{:S(2)}) copy-start(bf16[12,128,128]{2,1,0:T(8,128)(2,1)S(1)} %collective-permute-done.2.refs_5_) | copy-start | bytes 1179652
  116.2 9.8 %copy-start.20 = (bf16[12,128,128]{2,1,0:T(8,128)(2,1)}, bf16[12,128,128]{2,1,0:T(8,128)(2,1)S(1)}, u32[]{:S(2)}) copy-start(bf16[12,128,128]{2,1,0:T(8,128)(2,1)S(1)} %collective-permute-done.4.refs_9_) | copy-start | bytes 1179652
  126.1 1.0 copy-start.26
  127.0 1.0 copy-start.27
  132.3 48.1 %all-to-all-start.1 = ((bf16[8,64,512]{2,1,0:T(8,128)(2,1)}), bf16[8,64,512]{2,1,0:T(8,128)(2,1)S(1)}, u32[]{:S(2)}, u32[]{:S(2)}) async-start(bf16[8,64,512]{2,1,0:T(8,128)(2,1)} %get-tuple-element.17), calls=%async_computation.1 | async-start | bytes 1048576 | tf_op jit(solution)/shard_map/all_to_all | solution.py:370
  136.6 1.0 copy-start.11
  137.6 1.0 copy-start.13
  138.6 1.0 copy-start.18
  139.5 1.0 copy-start.21
  177.4 0.7 copy-start.15
  178.2 0.7 copy-start.19
  178.9 0.8 copy-start.22
  179.7 0.7 copy-start.23
  180.4 16.5 %copy-start.16 = (bf16[8,192,128]{2,1,0:T(8,128)(2,1)S(1)}, bf16[8,192,128]{2,1,0:T(8,128)(2,1)}, u32[]{:S(2)}) copy-start(bf16[8,192,128]{2,1,0:T(8,128)(2,1)} %copy-done.15) | copy-start | bytes 1179652
  180.4 33.9 %all-to-all-start.3 = ((bf16[8,128,512]{2,1,0:T(8,128)(2,1)}), bf16[8,128,512]{2,1,0:T(8,128)(2,1)S(1)}, u32[]{:S(2)}, u32[]{:S(2)}) async-start(bf16[8,128,512]{2,1,0:T(8,128)(2,1)} %get-tuple-element.20), calls=%async_computation.3 | async-start | bytes 2097152 | tf_op jit(solution)/shard_map/all_to_all | solution.py:371
  187.2 14.5 %collective-permute-start.6 = (bf16[8,192,128]{2,1,0:T(8,128)(2,1)}, bf16[8,192,128]{2,1,0:T(8,128)(2,1)S(1)}, u32[]{:S(2)}, u32[]{:S(2)}) collective-permute-start(bf16[8,192,128]{2,1,0:T(8,128)(2,1)} %copy-done.23), channel_id=1, source_target_pairs={{0,8},{8,16},{16,24},{24,0},{1,9},{9,17},{17,25},{25,1},{2,10},{10... | collective-permute-start | bytes 1179656 | tf_op jit(solution)/shard_map/ppermute | solution.py:334
  190.3 13.4 %collective-permute-start.10 = (bf16[8,192,128]{2,1,0:T(8,128)(2,1)}, bf16[8,192,128]{2,1,0:T(8,128)(2,1)S(1)}, u32[]{:S(2)}, u32[]{:S(2)}) collective-permute-start(bf16[8,192,128]{2,1,0:T(8,128)(2,1)} %copy-done.22), channel_id=1, source_target_pairs={{0,24},{8,0},{16,8},{24,16},{1,25},{9,1},{17,9},{25,17},{2,26},{10... | collective-permute-start | bytes 1179656 | tf_op jit(solution)/shard_map/ppermute | solution.py:334
  193.7 14.8 %collective-permute-start.8 = (bf16[8,192,128]{2,1,0:T(8,128)(2,1)}, bf16[8,192,128]{2,1,0:T(8,128)(2,1)S(1)}, u32[]{:S(2)}, u32[]{:S(2)}) collective-permute-start(bf16[8,192,128]{2,1,0:T(8,128)(2,1)} %copy-done.19), channel_id=1, source_target_pairs={{0,24},{8,0},{16,8},{24,16},{1,25},{9,1},{17,9},{25,17},{2,26},{10... | collective-permute-start | bytes 1179656 | tf_op jit(solution)/shard_map/ppermute | solution.py:334
  196.9 11.6 %collective-permute-start.9 = (bf16[8,192,128]{2,1,0:T(8,128)(2,1)S(1)}, bf16[8,192,128]{2,1,0:T(8,128)(2,1)S(1)}, u32[]{:S(2)}, u32[]{:S(2)}) collective-permute-start(bf16[8,192,128]{2,1,0:T(8,128)(2,1)S(1)} %copy-done.16), channel_id=1, source_target_pairs={{0,8},{8,16},{16,24},{24,0},{1,9},{9,17},{17,25},{25,1},{2,10},{10... | collective-permute-start | bytes 1179656 | tf_op jit(solution)/shard_map/ppermute | solution.py:334
  201.8 9.7 %collective-permute-start.7 = (bf16[8,192,128]{2,1,0:T(8,128)(2,1)S(1)}, bf16[8,192,128]{2,1,0:T(8,128)(2,1)S(1)}, u32[]{:S(2)}, u32[]{:S(2)}) collective-permute-start(bf16[8,192,128]{2,1,0:T(8,128)(2,1)S(1)} %add_convert_fusion.1), channel_id=1, source_target_pairs={{0,8},{8,16},{16,24},{24,0},{1,9},{9,17},{17,25},{25,1},{2,10},{10... | collective-permute-start | bytes 1179656 | tf_op jit(solution)/shard_map/ppermute | solution.py:334
  203.9 9.3 %collective-permute-start.11 = (bf16[8,192,128]{2,1,0:T(8,128)(2,1)S(1)}, bf16[8,192,128]{2,1,0:T(8,128)(2,1)S(1)}, u32[]{:S(2)}, u32[]{:S(2)}) collective-permute-start(bf16[8,192,128]{2,1,0:T(8,128)(2,1)S(1)} %add_convert_fusion), channel_id=1, source_target_pairs={{0,24},{8,0},{16,8},{24,16},{1,25},{9,1},{17,9},{25,17},{2,26},{10... | collective-permute-start | bytes 1179656 | tf_op jit(solution)/shard_map/ppermute | solution.py:334
  214.4 21.6 %all-to-all-start.4 = ((bf16[8,384,128]{2,1,0:T(8,128)(2,1)}), bf16[8,384,128]{2,1,0:T(8,128)(2,1)S(1)}, u32[]{:S(2)}, u32[]{:S(2)}) async-start(bf16[8,384,128]{2,1,0:T(8,128)(2,1)} %add_up.1), calls=%async_computation.4 | async-start | bytes 1572864 | tf_op jit(solution)/shard_map/all_to_all | solution.py:380

commit v3 on v2

--- a/solution.py
+++ b/solution.py
@@ -13,6 +13,7 @@
 HEAD_DIM = 128
 MAXDOC = 5
 EARLY = 4
+LIMIT = 60
 NN = (((1,), (0,)), ((), ()))
 NT = (((1,), (1,)), ((), ()))
 TN = (((0,), (0,)), ((), ()))
@@ -25,16 +26,15 @@
     return lax.dot_general(a, b, dims, preferred_element_type=f32)
 
 
-def attention_kernel(begin, count, cap, n_x, has_carry, dqt, *refs):
-    first_ref, where_ref, in_ref = refs[:3]
-    k_refs, v_refs = refs[3:3 + n_x], refs[3 + n_x:3 + 2 * n_x]
-    refs = refs[3 + 2 * n_x:]
+def attention_kernel(begin, count, cap, n_x, has_carry, *refs):
+    first_ref, where_ref, in_ref, own, right, left, far_k, far_v = refs[:8]
+    k_from = ((own, 0), (right, 0), (far_k, 0), (left, 0))
+    v_from = ((own, cap), (right, cap), (far_v, 0), (left, cap))
     if has_carry:
-        k_carry, v_carry, dq_ref = refs[:3]
-        dk_refs, dv_refs = refs[3:3 + n_x], refs[3 + n_x:3 + 2 * n_x]
-        queries, s_keep, p_keep, k_acc, v_acc, q_acc = refs[3 + 2 * n_x:]
+        k_carry, v_carry, dq_ref, out_own, out_up, out_down, out_k, out_v = refs[8:16]
+        queries, s_keep, p_keep, k_acc, v_acc, q_acc = refs[16:]
     else:
-        dq_ref, k_acc, v_acc, queries, s_keep, p_keep, q_acc = refs
+        dq_ref, k_acc, v_acc, queries, s_keep, p_keep, q_acc = refs[8:]
     groups, n_y, rows, head_dim = in_ref.shape
     heads = n_x
     part = groups * n_y
@@ -43,6 +43,14 @@
     factor = 1.0 / math.sqrt(head_dim)
     power = math.log2(math.e) * factor
     my_x = where_ref[0]
+
+    def key_part(x, block):
+        source, row = k_from[x]
+        return source[row + block]
+
+    def value_part(x, block):
+        source, row = v_from[x]
+        return source[row + block]
 
     mixed = groups * per
     row = lax.broadcasted_iota(jnp.int32, (mixed, mixed), 0)
@@ -63,9 +71,14 @@
 
     def put(block):
         at = pl.multiple_of(block * groups, groups)
+        second = pl.multiple_of(at + cap * groups, groups)
+        k_to = ((out_own, at), (out_k, at), (out_up, at), (out_down, at))
+        v_to = ((out_own, second), (out_up, second), (out_down, second), (out_v, at))
         for x in range(n_x):
-            dk_refs[x][:, pl.ds(at, groups), :] = (k_acc[x, block] * factor).astype(bf16).reshape(n_y, groups, head_dim)
-            dv_refs[x][:, pl.ds(at, groups), :] = v_acc[x, block].astype(bf16).reshape(n_y, groups, head_dim)
+            target, row = k_to[x]
+            target[:, pl.ds(row, groups), :] = (k_acc[x, block] * factor).astype(bf16).reshape(n_y, groups, head_dim)
+            target, row = v_to[x]
+            target[:, pl.ds(row, groups), :] = v_acc[x, block].astype(bf16).reshape(n_y, groups, head_dim)
 
     if has_carry:
         k_acc[:, :begin] = k_carry[...]
@@ -104,7 +117,7 @@
                 slot = key - low
                 top = high
                 for x in range(n_x):
-                    s = dot(k_refs[x][key], q, NT)
+                    s = dot(key_part(x, key), q, NT)
                     if masked:
                         x_of = lax.rem(my_x + x, n_x) * n_y
                         s = jnp.where(key_pos + x_of <= query_pos, s, NEG_FILL)
@@ -114,7 +127,7 @@
                 mass = mass * shrink
                 mean = mean * shrink
                 for x in range(n_x):
-                    dp = dot(v_refs[x][key], g, NT)
+                    dp = dot(value_part(x, key), g, NT)
                     p_keep[slot, x] = dp
                     e = jnp.exp2((s_keep[slot, x] - top) * power)
                     mass = mass + jnp.sum(e, axis=0, keepdims=True)
@@ -136,10 +149,7 @@
                     ds = (p * (p_keep[slot, x] - delta)).astype(bf16)
                     dv = dot(p.astype(bf16), g, NN)
                     dk = dot(ds, q, NN)
-                    if dqt:
-                        dq = dot(k_refs[x][key], ds, TN)
-                    else:
-                        dq = dot(ds, k_refs[x][key], TN)
+                    dq = dot(ds, key_part(x, key), TN)
                     total = dq if total is None else total + dq
                     if fresh:
                         v_acc[x, key] = dv
@@ -155,10 +165,7 @@
             back(block, True)
             lax.fori_loop(low, block, lambda key, _: (back(key, False), 0)[1], 0)
             for h in range(heads):
-                if dqt:
-                    mine = (q_acc[:, h * part:(h + 1) * part] * factor).T.astype(bf16)
-                else:
-                    mine = (q_acc[h * part:(h + 1) * part, :] * factor).astype(bf16)
+                mine = (q_acc[h * part:(h + 1) * part, :] * factor).astype(bf16)
                 dq_ref[:, pl.ds(at, groups), h * head_dim:(h + 1) * head_dim] = mine.reshape(n_y, groups, head_dim)
 
             if has_carry:
@@ -172,9 +179,9 @@
     lax.fori_loop(begin, begin + count, one_block, 0)
 
 
-def attention(first, my_x, packed, keys, values, begin, count, carry=None, dqt=False):
+def attention(first, my_x, packed, keys, begin, count, limit, carry=None):
     groups, n_y, rows, head_dim = packed.shape
-    n_x = len(keys)
+    n_x = HEADS // KV_HEADS
     cap = first.shape[0]
     part = groups * n_y
     span = n_x * part
@@ -189,26 +196,27 @@
         pltpu.VMEM((slots, n_x, part, span), f32),
     ]
     sums = (n_x, begin + count, part, head_dim)
-    total = [pltpu.VMEM((head_dim, span) if dqt else (span, head_dim), f32)]
+    total = [pltpu.VMEM((span, head_dim), f32)]
     if carry is None:
         out = (dq, shape(sums, f32), shape(sums, f32))
         carry = ()
         scratch = scratch + total
     else:
-        out = (dq,) + (shape((n_y, cap * groups, head_dim), bf16),) * (2 * n_x)
+        one = cap * groups
+        out = (dq,) + tuple(shape((n_y, rows, head_dim), bf16) for rows in (2 * one, 2 * one, 2 * one, one, one))
         scratch = scratch + [pltpu.VMEM(sums, f32)] * 2 + total
     pairs = count * 2
     return pl.pallas_call(
-        functools.partial(attention_kernel, begin, count, cap, n_x, bool(carry), dqt),
+        functools.partial(attention_kernel, begin, count, cap, n_x, bool(carry)),
         out_shape=out,
-        in_specs=[smem, smem] + [vmem] * (1 + 2 * n_x + len(carry)),
+        in_specs=[smem, smem] + [vmem] * (1 + len(keys) + len(carry)),
         out_specs=(vmem,) * len(out),
         scratch_shapes=scratch,
-        compiler_params=pltpu.CompilerParams(vmem_limit_bytes=48 * 2**20),
+        compiler_params=pltpu.CompilerParams(vmem_limit_bytes=limit * 2**20),
         cost_estimate=pl.CostEstimate(
             flops=pairs * 10 * span * span * head_dim, bytes_accessed=8 * 2**20, transcendentals=pairs * 2 * span * span),
         name="attention",
-    )(first, my_x, packed, *keys, *values, *carry)
+    )(first, my_x, packed, *keys, *carry)
 
 
 def pack_kernel(begin, count, cap, with_kv, *refs):
@@ -273,32 +281,31 @@
         in_specs=[table] * 3 + [wide] * 2 + [thin] * len(kv),
         out_specs=pl.BlockSpec((n_grp, 1, rows, HEAD_DIM), lambda y: (0, y, 0, 0)),
         scratch_shapes=scratch,
-        compiler_params=pltpu.CompilerParams(vmem_limit_bytes=24 * 2**20),
+        compiler_params=pltpu.CompilerParams(vmem_limit_bytes=LIMIT * 2**20),
         cost_estimate=pl.CostEstimate(flops=2 * 10**9, bytes_accessed=6 * 2**20, transcendentals=0),
         name="pack",
     )(*tables, q, g, *kv)
 
 
-def add_kernel(*refs):
-    out_ref = refs[-1]
-    rows = out_ref.shape[1] // 2
-    for half in range(2):
-        a, b, c = refs[3 * half:3 * half + 3]
-        total = a[...].astype(f32) + b[...].astype(f32) + c[...].astype(f32)
-        out_ref[:, half * rows:(half + 1) * rows, :] = total.astype(bf16)
-
-
-def add_up(dk_parts, dv_parts):
-    n_y, rows, head_dim = dk_parts[0].shape
+def add_kernel(own_ref, up_ref, down_ref, k_ref, v_ref, out_ref):
+    rows = k_ref.shape[1]
+    low, high = slice(0, rows), slice(rows, 2 * rows)
+    dk = own_ref[:, low].astype(f32) + down_ref[:, low].astype(f32) + k_ref[...].astype(f32)
+    dv = own_ref[:, high].astype(f32) + up_ref[:, high].astype(f32) + v_ref[...].astype(f32)
+    out_ref[:, low] = dk.astype(bf16)
+    out_ref[:, high] = dv.astype(bf16)
+
+
+def add_up(*parts):
     vmem = pl.BlockSpec(memory_space=pltpu.VMEM)
     return pl.pallas_call(
         add_kernel,
-        out_shape=jax.ShapeDtypeStruct((n_y, 2 * rows, head_dim), bf16),
-        in_specs=[vmem] * 6,
+        out_shape=jax.ShapeDtypeStruct(parts[0].shape, bf16),
+        in_specs=[vmem] * len(parts),
         out_specs=vmem,
         compiler_params=pltpu.CompilerParams(vmem_limit_bytes=16 * 2**20),
         name="add_up",
-    )(*dk_parts, *dv_parts)
+    )(*parts)
 
 
 def lay_kernel(pieces, *refs):
@@ -352,20 +359,14 @@
     late = exchange(pack(tables, q, g, (), n_grp, n_y, split, cap - split, cap))
 
     at = n_x * 2 * split
-    k0, v0 = (
-        early[:, :, at + i * cap:at + (i + 1) * cap].transpose(2, 1, 0, 3).reshape(cap, n_y * n_grp, HEAD_DIM)
-        for i in range(2)
-    )
-    k3, v1 = step(k0, 1), step(v0, -1)
-    v3, k1 = step(v0, 1), step(k0, -1)
-    k2, v2 = step(k3, 1), step(v1, -1)
-    keys, values = (k0, k1, k2, k3), (v0, v1, v2, v3)
+    own = early[:, :, at:at + 2 * cap].transpose(2, 1, 0, 3).reshape(2 * cap, n_y * n_grp, HEAD_DIM)
+    left, right = step(own, 1), step(own, -1)
+    keys = (own, right, left, step(left[:cap], 1), step(right[cap:], -1))
 
     first = first_blocks(doc_lengths, doc_groups, doc_offsets, cap)
     my_x = lax.axis_index("x").astype(jnp.int32).reshape(1)
-    dq_early, k_sums, v_sums = attention(first, my_x, early, keys, values, 0, split)
-    dq_late, *grads = attention(first, my_x, late, keys, values, split, cap - split, (k_sums, v_sums))
-    dk, dv = grads[:n_x], grads[n_x:]
+    dq_early, k_sums, v_sums = attention(first, my_x, early, keys, 0, split, 60)
+    dq_late, own, up, down, dk, dv = attention(first, my_x, late, keys, split, cap - split, 60, (k_sums, v_sums))
 
     dq_early = lax.all_to_all(dq_early, "y", 0, 0, tiled=True)
     dq_late = lax.all_to_all(dq_late, "y", 0, 0, tiled=True)
@@ -373,13 +374,13 @@
     def joined(mine, came):
         return (mine.astype(f32) + came.astype(f32)).astype(bf16)
 
-    k_far, v_far = step(dk[2], 1), step(dv[2], -1)
-    v_up, k_down = step(dv[1], 1), step(dk[3], -1)
-    k_up, v_down = step(joined(dk[1], k_far), 1), step(joined(dv[3], v_far), -1)
-    sums = add_up((dk[0], k_up, k_down), (dv[0], v_up, v_down))
+    rows = cap * n_grp
+    up, down = step(up, 1), step(down, -1)
+    k_in, v_in = step(joined(dk, up[:, :rows]), 1), step(joined(dv, down[:, rows:]), -1)
+    sums = add_up(own, up, down, k_in, v_in)
     sums = lax.all_to_all(sums, "y", 0, 0, tiled=True)
 
-    rows, near = cap * n_grp, split * n_grp
+    near = split * n_grp
     (dq_out,) = lay_out(
         (dq_early, dq_late), ((0, 0, near, 0, 0), (1, 0, rows - near, 0, near)), ((rows, HEADS * HEAD_DIM),))
     dk_out, dv_out = lay_out((sums,), ((0, 0, rows, 0, 0), (0, rows, rows, 1, 0)), ((rows, KV_HEADS * HEAD_DIM),) * 2)

time: 238 us -> 232 us (0.975)
  the two profiles are of different devices: /device:TPU:193 before, /device:TPU:6 now
where the time goes in v3:
time: 232 us; the launch traced here: 231 us
  waiting for transfers between devices  97.1 us (42%)
  starting transfers between devices  70 us (30%)
  Pallas kernels  61.9 us (27%)
    pallas_call x2, Pallas kernels, attention(): pl.pallas_call(functools.partial(attention_kernel, begin, count, cap, n_x...  44.3 us
    ppermute x8, waiting for transfers between devices, step(): return lax.ppermute(array, 'x', [(i, (i + by) % n_x) for i in range(n_x)])  41.1 us
    all_to_all x2, waiting for transfers between devices, exchange(): lax.all_to_all(message.reshape(n_grp * n_y, rows, HEAD_DIM), ('grp', 'y')...  41.1 us
    all_to_all x2, starting transfers between devices, exchange(): lax.all_to_all(message.reshape(n_grp * n_y, rows, HEAD_DIM), ('grp', 'y')...  25.9 us
    ppermute x8, starting transfers between devices, step(): return lax.ppermute(array, 'x', [(i, (i + by) % n_x) for i in range(n_x)])  23.4 us
    all_to_all x1, waiting for transfers between devices, on_device(): sums = lax.all_to_all(sums, 'y', 0, 0, tiled=True)  14.9 us
    pallas_call x2, Pallas kernels, pack(): pl.pallas_call(functools.partial(pack_kernel, begin, count, cap, bool(kv)...  14.1 us
    all_to_all x1, starting transfers between devices, on_device(): dq_late = lax.all_to_all(dq_late, 'y', 0, 0, tiled=True)  7.35 us
  transfers between devices with their start and end apart: 13, of which 9 were waited for; matrix products, arithmetic and copies ran while one was open for 1% of the time, Pallas kernels for 23%

profile of v3, /device:TPU:6, one launch (start us, length us, event | category | flops | bytes accessed | tf_op | source)
XLA Modules:
  0.0 231.5 jit_solution(14458281645968181068)
XLA Ops:
  0.6 7.2 %pack.2 = bf16[16,8,56,128]{3,2,1,0:T(8,128)(2,1)} custom-call(s32[1,192]{1,0:T(1,128)} %bitcast.31, s32[1,192]{1,0:T(1,128)} %bitcast.29, s32[1,192]{1,0:T(1,128)} %bitcast.27, bf16[128,4096]{1,0:T(8,128)(2,1)} %bitcast.33, bf16[128,4096]{1,0:T(8,128)(2,1)} %bitcast.35, bf16[128,1024]{1,0:T(8,128)(2,1)} %bitcast.39, bf16[128,1024]{1,0:T(8,128)(2,1)} %bitcast.40), custom_call_target="tpu_custom_call" | custom-call | flops 2000000000 | bytes 6291456 | tf_op jit(solution)/shard_map/pack/pallas_call | solution.py:277
  7.8 17.8 %all-to-all-start = ((bf16[128,56,128]{2,1,0:T(8,128)(2,1)}), bf16[128,56,128]{2,1,0:T(8,128)(2,1)S(1)}, u32[]{:S(2)}, u32[]{:S(2)}) async-start(bf16[128,56,128]{2,1,0:T(8,128)(2,1)} %bitcast.21), calls=%async_computation | async-start | bytes 3670016 | tf_op jit(solution)/shard_map/all_to_all | solution.py:355
  25.7 6.9 %pack.3 = bf16[16,8,64,128]{3,2,1,0:T(8,128)(2,1)} custom-call(s32[1,192]{1,0:T(1,128)} %bitcast.32, s32[1,192]{1,0:T(1,128)} %bitcast.30, s32[1,192]{1,0:T(1,128)} %bitcast.28, bf16[128,4096]{1,0:T(8,128)(2,1)} %bitcast.34, bf16[128,4096]{1,0:T(8,128)(2,1)} %bitcast.36), custom_call_target="tpu_custom_call" | custom-call | flops 2000000000 | bytes 6291456 | tf_op jit(solution)/shard_map/pack/pallas_call | solution.py:277
  32.6 39.7 %all-to-all-done = bf16[128,56,128]{2,1,0:T(8,128)(2,1)S(1)} async-done(((bf16[128,56,128]{2,1,0:T(8,128)(2,1)}), bf16[128,56,128]{2,1,0:T(8,128)(2,1)S(1)}, u32[]{:S(2)}, u32[]{:S(2)}) %all-to-all-start) | async-done | bytes 1835040 | tf_op jit(solution)/shard_map/all_to_all | solution.py:355
  72.3 0.0 copy-start.1
  72.3 8.1 %all-to-all-start.2 = ((bf16[128,64,128]{2,1,0:T(8,128)(2,1)}), bf16[128,64,128]{2,1,0:T(8,128)(2,1)}, u32[]{:S(2)}, u32[]{:S(2)}) async-start(bf16[128,64,128]{2,1,0:T(8,128)(2,1)} %bitcast.20), calls=%async_computation.2 | async-start | bytes 4194304 | tf_op jit(solution)/shard_map/all_to_all | solution.py:355
  80.4 0.0 copy-start.7
  80.4 0.0 copy-start.9
  80.4 0.0 copy-done.1
  80.4 0.1 slice_bitcast_fusion
  80.5 0.0 copy-start.8
  80.5 0.5 copy.11
  81.0 0.0 copy-start.2
  81.0 2.4 %collective-permute-start.1 = (bf16[24,128,128]{2,1,0:T(8,128)(2,1)S(1)}, bf16[24,128,128]{2,1,0:T(8,128)(2,1)S(1)}, u32[]{:S(2)}, u32[]{:S(2)}) collective-permute-start(bf16[24,128,128]{2,1,0:T(8,128)(2,1)S(1)} %bitcast.23), channel_id=1, source_target_pairs={{0,8},{8,16},{16,24},{24,0},{1,9},{9,17},{17,25},{25,1},{2,10},{10... | collective-permute-start | bytes 2359304 | tf_op jit(solution)/shard_map/ppermute | solution.py:341
  83.4 3.5 %collective-permute-start = (bf16[24,128,128]{2,1,0:T(8,128)(2,1)S(1)}, bf16[24,128,128]{2,1,0:T(8,128)(2,1)S(1)}, u32[]{:S(2)}, u32[]{:S(2)}) collective-permute-start(bf16[24,128,128]{2,1,0:T(8,128)(2,1)S(1)} %bitcast.24), channel_id=1, source_target_pairs={{0,24},{8,0},{16,8},{24,16},{1,25},{9,1},{17,9},{25,17},{2,26},{10... | collective-permute-start | bytes 2359304 | tf_op jit(solution)/shard_map/ppermute | solution.py:341
  86.9 0.0 copy-done.7
  86.9 0.0 copy-done.9
  86.9 15.0 %collective-permute-done.1.refs_5_ = bf16[24,128,128]{2,1,0:T(8,128)(2,1)S(1)} collective-permute-done((bf16[24,128,128]{2,1,0:T(8,128)(2,1)S(1)}, bf16[24,128,128]{2,1,0:T(8,128)(2,1)S(1)}, u32[]{:S(2)}, u32[]{:S(2)}) %collective-permute-start.1) | collective-permute-done | bytes 786464 | tf_op jit(solution)/shard_map/ppermute | solution.py:341
  101.9 0.0 copy-start.5
  101.9 3.6 %collective-permute-start.2 = (bf16[12,128,128]{2,1,0:T(8,128)(2,1)S(1)}, bf16[12,128,128]{2,1,0:T(8,128)(2,1)}, u32[]{:S(2)}, u32[]{:S(2)}) collective-permute-start(bf16[12,128,128]{2,1,0:T(8,128)(2,1)S(1)} %slice.21), channel_id=1, source_target_pairs={{0,8},{8,16},{16,24},{24,0},{1,9},{9,17},{17,25},{25,1},{2,10},{10... | collective-permute-start | bytes 1179656 | tf_op jit(solution)/shard_map/ppermute | solution.py:341
  105.5 0.0 collective-permute-done.refs_4_
  105.6 0.0 copy-start.6
  105.6 2.2 collective-permute-start.3
  107.9 0.0 copy-done.8
  107.9 0.1 select_reduce_fusion
  108.0 0.6 broadcast_add_fusion.1.refs_0_
  108.6 5.1 %collective-permute-done.2.refs_6_ = bf16[12,128,128]{2,1,0:T(8,128)(2,1)} collective-permute-done((bf16[12,128,128]{2,1,0:T(8,128)(2,1)S(1)}, bf16[12,128,128]{2,1,0:T(8,128)(2,1)}, u32[]{:S(2)}, u32[]{:S(2)}) %collective-permute-start.2) | collective-permute-done | bytes 393248 | tf_op jit(solution)/shard_map/ppermute | solution.py:341
  113.7 4.6 %collective-permute-done.3.refs_7_ = bf16[12,128,128]{2,1,0:T(8,128)(2,1)} collective-permute-done((bf16[12,128,128]{2,1,0:T(8,128)(2,1)S(1)}, bf16[12,128,128]{2,1,0:T(8,128)(2,1)}, u32[]{:S(2)}, u32[]{:S(2)}) %collective-permute-start.3) | collective-permute-done | bytes 393248 | tf_op jit(solution)/shard_map/ppermute | solution.py:341
  118.3 0.0 copy-done.2
  118.3 0.0 copy-done.5
  118.3 0.0 copy-done.6
  118.3 12.3 %attention.2 = (bf16[8,64,512]{2,1,0:T(8,128)(2,1)}, f32[4,4,128,128]{3,2,1,0:T(8,128)}, f32[4,4,128,128]{3,2,1,0:T(8,128)}) custom-call(s32[12]{0:T(128)} %broadcast_add_fusion.1.refs_0_, s32[1]{0:T(128)} %bitcast.refs_1_, bf16[16,8,56,128]{3,2,1,0:T(8,128)(2,1)} %bitcast.19, bf16[24,128,128]{2,1,0:T(8,128)(2,1)} %bitcast.25, ...), custom_call_target="tpu_custom_call" | custom-call | flops 2684354560 | bytes 8388608 | tf_op jit(solution)/shard_map/attention/pallas_call | solution.py:209
  130.6 1.4 all-to-all-done.2
  132.0 6.1 %all-to-all-start.1 = ((bf16[8,64,512]{2,1,0:T(8,128)(2,1)}), bf16[8,64,512]{2,1,0:T(8,128)(2,1)S(1)}, u32[]{:S(2)}, u32[]{:S(2)}) async-start(bf16[8,64,512]{2,1,0:T(8,128)(2,1)} %get-tuple-element.14), calls=%async_computation.1 | async-start | bytes 1048576 | tf_op jit(solution)/shard_map/all_to_all | solution.py:371
  138.2 31.9 %attention.3 = (bf16[8,128,512]{2,1,0:T(8,128)(2,1)}, bf16[8,384,128]{2,1,0:T(8,128)(2,1)}, bf16[8,384,128]{2,1,0:T(8,128)(2,1)}, bf16[8,384,128]{2,1,0:T(8,128)...) custom-call(s32[12]{0:T(128)} %broadcast_add_fusion.1.refs_0_, s32[1]{0:T(128)} %bitcast.refs_1_, ...), custom_call_target="tpu_custom_call" | custom-call | flops 5368709120 | bytes 8388608 | tf_op jit(solution)/shard_map/attention/pallas_call | solution.py:209
  170.1 0.0 copy-start.4
  170.1 0.0 copy-start.3
  170.1 0.0 all-to-all-done.1.refs_0_
  170.1 0.0 copy-start
  170.1 7.4 %all-to-all-start.3 = ((bf16[8,128,512]{2,1,0:T(8,128)(2,1)}), bf16[8,128,512]{2,1,0:T(8,128)(2,1)S(1)}, u32[]{:S(2)}, u32[]{:S(2)}) async-start(bf16[8,128,512]{2,1,0:T(8,128)(2,1)} %get-tuple-element.17), calls=%async_computation.3 | async-start | bytes 2097152 | tf_op jit(solution)/shard_map/all_to_all | solution.py:372
  177.5 1.9 collective-permute-start.4
  179.4 3.9 %collective-permute-start.5 = (bf16[8,384,128]{2,1,0:T(8,128)(2,1)}, bf16[8,384,128]{2,1,0:T(8,128)(2,1)S(1)}, u32[]{:S(2)}, u32[]{:S(2)}) collective-permute-start(bf16[8,384,128]{2,1,0:T(8,128)(2,1)} %get-tuple-element.20), channel_id=1, source_target_pairs={{0,24},{8,0},{16,8},{24,16},{1,25},{9,1},{17,9},{25,17},{2,26},{10... | collective-permute-start | bytes 2359304 | tf_op jit(solution)/shard_map/ppermute | solution.py:341
  183.3 8.2 %collective-permute-done.4.up_ref = bf16[8,384,128]{2,1,0:T(8,128)(2,1)S(1)} collective-permute-done((bf16[8,384,128]{2,1,0:T(8,128)(2,1)}, bf16[8,384,128]{2,1,0:T(8,128)(2,1)S(1)}, u32[]{:S(2)}, u32[]{:S(2)}) %collective-permute-start.4) | collective-permute-done | bytes 786464 | tf_op jit(solution)/shard_map/ppermute | solution.py:341
  191.6 0.0 copy-done.4
  191.6 0.1 add_convert_fusion.1
  191.7 3.1 %collective-permute-start.6 = (bf16[8,192,128]{2,1,0:T(8,128)(2,1)S(1)}, bf16[8,192,128]{2,1,0:T(8,128)(2,1)S(1)}, u32[]{:S(2)}, u32[]{:S(2)}) collective-permute-start(bf16[8,192,128]{2,1,0:T(8,128)(2,1)S(1)} %add_convert_fusion.1), channel_id=1, source_target_pairs={{0,8},{8,16},{16,24},{24,0},{1,9},{9,17},{17,25},{25,1},{2,10},{10... | collective-permute-start | bytes 1179656 | tf_op jit(solution)/shard_map/ppermute | solution.py:341
  194.8 0.0 collective-permute-done.5.down_ref
  194.8 0.0 copy-done.3
  194.9 0.1 add_convert_fusion
  195.0 2.7 %collective-permute-start.7 = (bf16[8,192,128]{2,1,0:T(8,128)(2,1)S(1)}, bf16[8,192,128]{2,1,0:T(8,128)(2,1)S(1)}, u32[]{:S(2)}, u32[]{:S(2)}) collective-permute-start(bf16[8,192,128]{2,1,0:T(8,128)(2,1)S(1)} %add_convert_fusion), channel_id=1, source_target_pairs={{0,24},{8,0},{16,8},{24,16},{1,25},{9,1},{17,9},{25,17},{2,26},{10... | collective-permute-start | bytes 1179656 | tf_op jit(solution)/shard_map/ppermute | solution.py:341
  197.7 3.7 %collective-permute-done.6.k_ref = bf16[8,192,128]{2,1,0:T(8,128)(2,1)S(1)} collective-permute-done((bf16[8,192,128]{2,1,0:T(8,128)(2,1)S(1)}, bf16[8,192,128]{2,1,0:T(8,128)(2,1)S(1)}, u32[]{:S(2)}, u32[]{:S(2)}) %collective-permute-start.6) | collective-permute-done | bytes 393248 | tf_op jit(solution)/shard_map/ppermute | solution.py:341
  201.4 4.5 %collective-permute-done.7.v_ref = bf16[8,192,128]{2,1,0:T(8,128)(2,1)S(1)} collective-permute-done((bf16[8,192,128]{2,1,0:T(8,128)(2,1)S(1)}, bf16[8,192,128]{2,1,0:T(8,128)(2,1)S(1)}, u32[]{:S(2)}, u32[]{:S(2)}) %collective-permute-start.7) | collective-permute-done | bytes 393248 | tf_op jit(solution)/shard_map/ppermute | solution.py:341
  205.9 0.0 copy-done
  205.9 1.2 add_up.1
  207.0 0.0 all-to-all-done.3.refs_1_
  207.0 7.2 %all-to-all-start.4 = ((bf16[8,384,128]{2,1,0:T(8,128)(2,1)}), bf16[8,384,128]{2,1,0:T(8,128)(2,1)S(1)}, u32[]{:S(2)}, u32[]{:S(2)}) async-start(bf16[8,384,128]{2,1,0:T(8,128)(2,1)} %add_up.1), calls=%async_computation.4 | async-start | bytes 1572864 | tf_op jit(solution)/shard_map/all_to_all | solution.py:381
  214.2 1.2 lay_out.2
  215.5 14.9 %all-to-all-done.4.refs_0_ = bf16[8,384,128]{2,1,0:T(8,128)(2,1)S(1)} async-done(((bf16[8,384,128]{2,1,0:T(8,128)(2,1)}), bf16[8,384,128]{2,1,0:T(8,128)(2,1)S(1)}, u32[]{:S(2)}, u32[]{:S(2)}) %all-to-all-start.4) | async-done | bytes 786464 | tf_op jit(solution)/shard_map/all_to_all | solution.py:381
  230.4 1.1 lay_out.3
  (4 shorter events, 0.1 us)
Async XLA Ops:
  7.8 64.4 %all-to-all-start = ((bf16[128,56,128]{2,1,0:T(8,128)(2,1)}), bf16[128,56,128]{2,1,0:T(8,128)(2,1)S(1)}, u32[]{:S(2)}, u32[]{:S(2)}) async-start(bf16[128,56,128]{2,1,0:T(8,128)(2,1)} %bitcast.21), calls=%async_computation | async-start | bytes 3670016 | tf_op jit(solution)/shard_map/all_to_all | solution.py:355
  72.3 8.1 %copy-start.1 = (bf16[128,56,128]{2,1,0:T(8,128)(2,1)}, bf16[128,56,128]{2,1,0:T(8,128)(2,1)S(1)}, u32[]{:S(2)}) copy-start(bf16[128,56,128]{2,1,0:T(8,128)(2,1)S(1)} %all-to-all-done) | copy-start | bytes 5505028
  72.3 59.8 %all-to-all-start.2 = ((bf16[128,64,128]{2,1,0:T(8,128)(2,1)}), bf16[128,64,128]{2,1,0:T(8,128)(2,1)}, u32[]{:S(2)}, u32[]{:S(2)}) async-start(bf16[128,64,128]{2,1,0:T(8,128)(2,1)} %bitcast.20), calls=%async_computation.2 | async-start | bytes 4194304 | tf_op jit(solution)/shard_map/all_to_all | solution.py:355
  80.4 6.5 %copy-start.7 = (s32[192]{0:T(256)S(1)}, s32[192]{0:T(256)}, u32[]{:S(2)}) copy-start(s32[192]{0:T(256)} %param.13) | copy-start | bytes 2308
  80.4 6.5 %copy-start.9 = (s32[192]{0:T(256)S(1)}, s32[192]{0:T(256)}, u32[]{:S(2)}) copy-start(s32[192]{0:T(256)} %param.11) | copy-start | bytes 2308
  80.5 27.4 %copy-start.8 = (s32[192]{0:T(256)S(1)}, s32[192]{0:T(256)}, u32[]{:S(2)}) copy-start(s32[192]{0:T(256)} %param.12) | copy-start | bytes 2308
  81.0 37.3 %copy-start.2 = (bf16[24,8,16,128]{3,2,1,0:T(8,128)(2,1)}, bf16[24,8,16,128]{3,2,1,0:T(8,128)(2,1)S(1)}, u32[]{:S(2)}) copy-start(bf16[24,8,16,128]{3,2,1,0:T(8,128)(2,1)S(1)} %copy.11) | copy-start | bytes 2359300
  81.0 20.9 %collective-permute-start.1 = (bf16[24,128,128]{2,1,0:T(8,128)(2,1)S(1)}, bf16[24,128,128]{2,1,0:T(8,128)(2,1)S(1)}, u32[]{:S(2)}, u32[]{:S(2)}) collective-permute-start(bf16[24,128,128]{2,1,0:T(8,128)(2,1)S(1)} %bitcast.23), channel_id=1, source_target_pairs={{0,8},{8,16},{16,24},{24,0},{1,9},{9,17},{17,25},{25,1},{2,10},{10... | collective-permute-start | bytes 2359304 | tf_op jit(solution)/shard_map/ppermute | solution.py:341
  83.4 22.1 %collective-permute-start = (bf16[24,128,128]{2,1,0:T(8,128)(2,1)S(1)}, bf16[24,128,128]{2,1,0:T(8,128)(2,1)S(1)}, u32[]{:S(2)}, u32[]{:S(2)}) collective-permute-start(bf16[24,128,128]{2,1,0:T(8,128)(2,1)S(1)} %bitcast.24), channel_id=1, source_target_pairs={{0,24},{8,0},{16,8},{24,16},{1,25},{9,1},{17,9},{25,17},{2,26},{10... | collective-permute-start | bytes 2359304 | tf_op jit(solution)/shard_map/ppermute | solution.py:341
  101.9 16.4 %copy-start.5 = (bf16[24,128,128]{2,1,0:T(8,128)(2,1)}, bf16[24,128,128]{2,1,0:T(8,128)(2,1)S(1)}, u32[]{:S(2)}) copy-start(bf16[24,128,128]{2,1,0:T(8,128)(2,1)S(1)} %collective-permute-done.1.refs_5_) | copy-start | bytes 2359300
  101.9 11.8 %collective-permute-start.2 = (bf16[12,128,128]{2,1,0:T(8,128)(2,1)S(1)}, bf16[12,128,128]{2,1,0:T(8,128)(2,1)}, u32[]{:S(2)}, u32[]{:S(2)}) collective-permute-start(bf16[12,128,128]{2,1,0:T(8,128)(2,1)S(1)} %slice.21), channel_id=1, source_target_pairs={{0,8},{8,16},{16,24},{24,0},{1,9},{9,17},{17,25},{25,1},{2,10},{10... | collective-permute-start | bytes 1179656 | tf_op jit(solution)/shard_map/ppermute | solution.py:341
  105.6 12.7 %copy-start.6 = (bf16[24,128,128]{2,1,0:T(8,128)(2,1)}, bf16[24,128,128]{2,1,0:T(8,128)(2,1)S(1)}, u32[]{:S(2)}) copy-start(bf16[24,128,128]{2,1,0:T(8,128)(2,1)S(1)} %collective-permute-done.refs_4_) | copy-start | bytes 2359300
  105.6 12.7 %collective-permute-start.3 = (bf16[12,128,128]{2,1,0:T(8,128)(2,1)S(1)}, bf16[12,128,128]{2,1,0:T(8,128)(2,1)}, u32[]{:S(2)}, u32[]{:S(2)}) collective-permute-start(bf16[12,128,128]{2,1,0:T(8,128)(2,1)S(1)} %slice.22), channel_id=1, source_target_pairs={{0,24},{8,0},{16,8},{24,16},{1,25},{9,1},{17,9},{25,17},{2,26},{10... | collective-permute-start | bytes 1179656 | tf_op jit(solution)/shard_map/ppermute | solution.py:341
  132.0 38.1 %all-to-all-start.1 = ((bf16[8,64,512]{2,1,0:T(8,128)(2,1)}), bf16[8,64,512]{2,1,0:T(8,128)(2,1)S(1)}, u32[]{:S(2)}, u32[]{:S(2)}) async-start(bf16[8,64,512]{2,1,0:T(8,128)(2,1)} %get-tuple-element.14), calls=%async_computation.1 | async-start | bytes 1048576 | tf_op jit(solution)/shard_map/all_to_all | solution.py:371
  170.1 21.5 %copy-start.4 = (bf16[8,192,128]{2,1,0:T(8,128)(2,1)S(1)}, bf16[8,192,128]{2,1,0:T(8,128)(2,1)}, u32[]{:S(2)}) copy-start(bf16[8,192,128]{2,1,0:T(8,128)(2,1)} %get-tuple-element.21) | copy-start | bytes 1179652
  170.1 24.7 %copy-start.3 = (bf16[8,192,128]{2,1,0:T(8,128)(2,1)S(1)}, bf16[8,192,128]{2,1,0:T(8,128)(2,1)}, u32[]{:S(2)}) copy-start(bf16[8,192,128]{2,1,0:T(8,128)(2,1)} %get-tuple-element.22) | copy-start | bytes 1179652
  170.1 35.7 %copy-start = (bf16[8,384,128]{2,1,0:T(8,128)(2,1)S(1)}, bf16[8,384,128]{2,1,0:T(8,128)(2,1)}, u32[]{:S(2)}) copy-start(bf16[8,384,128]{2,1,0:T(8,128)(2,1)} %get-tuple-element.18.own_ref) | copy-start | bytes 2359300
  170.1 36.9 %all-to-all-start.3 = ((bf16[8,128,512]{2,1,0:T(8,128)(2,1)}), bf16[8,128,512]{2,1,0:T(8,128)(2,1)S(1)}, u32[]{:S(2)}, u32[]{:S(2)}) async-start(bf16[8,128,512]{2,1,0:T(8,128)(2,1)} %get-tuple-element.17), calls=%async_computation.3 | async-start | bytes 2097152 | tf_op jit(solution)/shard_map/all_to_all | solution.py:372
  177.5 14.1 %collective-permute-start.4 = (bf16[8,384,128]{2,1,0:T(8,128)(2,1)}, bf16[8,384,128]{2,1,0:T(8,128)(2,1)S(1)}, u32[]{:S(2)}, u32[]{:S(2)}) collective-permute-start(bf16[8,384,128]{2,1,0:T(8,128)(2,1)} %get-tuple-element.19), channel_id=1, source_target_pairs={{0,8},{8,16},{16,24},{24,0},{1,9},{9,17},{17,25},{25,1},{2,10},{10... | collective-permute-start | bytes 2359304 | tf_op jit(solution)/shard_map/ppermute | solution.py:341
  179.4 15.4 %collective-permute-start.5 = (bf16[8,384,128]{2,1,0:T(8,128)(2,1)}, bf16[8,384,128]{2,1,0:T(8,128)(2,1)S(1)}, u32[]{:S(2)}, u32[]{:S(2)}) collective-permute-start(bf16[8,384,128]{2,1,0:T(8,128)(2,1)} %get-tuple-element.20), channel_id=1, source_target_pairs={{0,24},{8,0},{16,8},{24,16},{1,25},{9,1},{17,9},{25,17},{2,26},{10... | collective-permute-start | bytes 2359304 | tf_op jit(solution)/shard_map/ppermute | solution.py:341
  191.7 9.7 %collective-permute-start.6 = (bf16[8,192,128]{2,1,0:T(8,128)(2,1)S(1)}, bf16[8,192,128]{2,1,0:T(8,128)(2,1)S(1)}, u32[]{:S(2)}, u32[]{:S(2)}) collective-permute-start(bf16[8,192,128]{2,1,0:T(8,128)(2,1)S(1)} %add_convert_fusion.1), channel_id=1, source_target_pairs={{0,8},{8,16},{16,24},{24,0},{1,9},{9,17},{17,25},{25,1},{2,10},{10... | collective-permute-start | bytes 1179656 | tf_op jit(solution)/shard_map/ppermute | solution.py:341
  195.0 10.9 %collective-permute-start.7 = (bf16[8,192,128]{2,1,0:T(8,128)(2,1)S(1)}, bf16[8,192,128]{2,1,0:T(8,128)(2,1)S(1)}, u32[]{:S(2)}, u32[]{:S(2)}) collective-permute-start(bf16[8,192,128]{2,1,0:T(8,128)(2,1)S(1)} %add_convert_fusion), channel_id=1, source_target_pairs={{0,24},{8,0},{16,8},{24,16},{1,25},{9,1},{17,9},{25,17},{2,26},{10... | collective-permute-start | bytes 1179656 | tf_op jit(solution)/shard_map/ppermute | solution.py:341
  207.0 23.4 %all-to-all-start.4 = ((bf16[8,384,128]{2,1,0:T(8,128)(2,1)}), bf16[8,384,128]{2,1,0:T(8,128)(2,1)S(1)}, u32[]{:S(2)}, u32[]{:S(2)}) async-start(bf16[8,384,128]{2,1,0:T(8,128)(2,1)} %add_up.1), calls=%async_computation.4 | async-start | bytes 1572864 | tf_op jit(solution)/shard_map/all_to_all | solution.py:381

commit v4 on v2

--- a/solution.py
+++ b/solution.py
@@ -12,7 +12,8 @@
 KV_HEADS = 8
 HEAD_DIM = 128
 MAXDOC = 5
-EARLY = 4
+EARLY = 5
+QUAD = 4
 NN = (((1,), (0,)), ((), ()))
 NT = (((1,), (1,)), ((), ()))
 TN = (((0,), (0,)), ((), ()))
@@ -25,41 +26,74 @@
     return lax.dot_general(a, b, dims, preferred_element_type=f32)
 
 
-def attention_kernel(begin, count, cap, n_x, has_carry, dqt, *refs):
+def attention_kernel(begin, count, cap, early, n_x, has_carry, *refs):
     first_ref, where_ref, in_ref = refs[:3]
-    k_refs, v_refs = refs[3:3 + n_x], refs[3 + n_x:3 + 2 * n_x]
-    refs = refs[3 + 2 * n_x:]
+    near = refs[3:8]
     if has_carry:
-        k_carry, v_carry, dq_ref = refs[:3]
-        dk_refs, dv_refs = refs[3:3 + n_x], refs[3 + n_x:3 + 2 * n_x]
-        queries, s_keep, p_keep, k_acc, v_acc, q_acc = refs[3 + 2 * n_x:]
+        late_ref, k_carry, v_carry, dq_ref = refs[8:12]
+        dk_refs, dv_refs = refs[12:12 + n_x], refs[12 + n_x:12 + 2 * n_x]
+        refs = refs[12 + 2 * n_x:]
+        queries, keys, values, s_keep, p_keep, q_acc, sem, k_acc, v_acc = refs
     else:
-        dq_ref, k_acc, v_acc, queries, s_keep, p_keep, q_acc = refs
-    groups, n_y, rows, head_dim = in_ref.shape
+        dq_ref, k_acc, v_acc, queries, keys, values, s_keep, p_keep, q_acc, sem = refs[8:]
+    groups, n_y, _, head_dim = in_ref.shape
     heads = n_x
     part = groups * n_y
     span = heads * part
-    per = 2 * count
+    rest = cap - early
     factor = 1.0 / math.sqrt(head_dim)
     power = math.log2(math.e) * factor
     my_x = where_ref[0]
 
+    moves = []
+    own, right, left, far_k, far_v = near
+    for slot, k_from, k_row, v_from, v_row in (
+        (0, own, 0, own, early), (1, right, 0, right, early), (2, far_k, 0, far_v, 0), (3, left, 0, left, early)):
+        moves.append((k_from.at[pl.ds(k_row, early)], keys.at[slot, pl.ds(0, early)]))
+        moves.append((v_from.at[pl.ds(v_row, early)], values.at[slot, pl.ds(0, early)]))
+    if has_carry:
+        for slot in range(n_x):
+            x = lax.rem(my_x + slot, n_x)
+            moves.append((late_ref.at[x, pl.ds(0, rest)], keys.at[slot, pl.ds(early, rest)]))
+            moves.append((late_ref.at[x, pl.ds(rest, rest)], values.at[slot, pl.ds(early, rest)]))
+        moves.append((k_carry, k_acc.at[:, pl.ds(0, early)]))
+        moves.append((v_carry, v_acc.at[:, pl.ds(0, early)]))
+    copies = [pltpu.make_async_copy(source, target, sem.at[i]) for i, (source, target) in enumerate(moves)]
+    for copy in copies:
+        copy.start()
+
+    per = 2 * QUAD
     mixed = groups * per
     row = lax.broadcasted_iota(jnp.int32, (mixed, mixed), 0)
     col = lax.broadcasted_iota(jnp.int32, (mixed, mixed), 1)
     turn = jnp.where((row // groups == col % per) & (row % groups == col // per), 1.0, 0.0).astype(bf16)
+    quads, ones = count // QUAD, count % QUAD
 
     def sort_y(y, _):
-        taken = jnp.concatenate(
-            [in_ref[:, y, h * per:(h + 1) * per, :].reshape(mixed, head_dim) for h in range(heads)], axis=1)
-        turned = dot(turn, taken, NN).astype(bf16)
-        for h in range(heads):
-            at = pl.multiple_of(h * part + y * groups, groups)
-            queries[:, pl.ds(at, groups), :] = (
-                turned[:, h * head_dim:(h + 1) * head_dim].reshape(per, groups, head_dim))
+        def turned(starts):
+            taken = jnp.concatenate(
+                [in_ref[:, y, start:start + per, :].reshape(mixed, head_dim) for start in starts], axis=1)
+            out = dot(turn, taken, NN).astype(bf16)
+            return [out[:, i * head_dim:(i + 1) * head_dim].reshape(per, groups, head_dim) for i in range(len(starts))]
+
+        at = [pl.ds(pl.multiple_of(h * part + y * groups, groups), groups) for h in range(heads)]
+        for j in range(quads):
+            slabs = turned([(j * heads + h) * per for h in range(heads)])
+            for h in range(heads):
+                for kind in range(2):
+                    to = kind * count + j * QUAD
+                    queries[to:to + QUAD, at[h], :] = slabs[h][kind * QUAD:(kind + 1) * QUAD]
+        if ones:
+            slabs = turned([(quads * heads + i) * per for i in range(ones)])
+            for i in range(ones):
+                for h in range(heads):
+                    for kind in range(2):
+                        queries[kind * count + quads * QUAD + i, at[h], :] = slabs[i][2 * h + kind]
         return 0
 
     lax.fori_loop(0, n_y, sort_y, 0)
+    for copy in copies:
+        copy.wait()
 
     def put(block):
         at = pl.multiple_of(block * groups, groups)
@@ -68,8 +102,6 @@
             dv_refs[x][:, pl.ds(at, groups), :] = v_acc[x, block].astype(bf16).reshape(n_y, groups, head_dim)
 
     if has_carry:
-        k_acc[:, :begin] = k_carry[...]
-        v_acc[:, :begin] = v_carry[...]
         low = first_ref[begin]
         low = jnp.where(low < 0, begin, jnp.minimum(low, begin))
         lax.fori_loop(0, low, lambda block, _: (put(block), 0)[1], 0)
@@ -104,7 +136,7 @@
                 slot = key - low
                 top = high
                 for x in range(n_x):
-                    s = dot(k_refs[x][key], q, NT)
+                    s = dot(keys[x, key], q, NT)
                     if masked:
                         x_of = lax.rem(my_x + x, n_x) * n_y
                         s = jnp.where(key_pos + x_of <= query_pos, s, NEG_FILL)
@@ -114,7 +146,7 @@
                 mass = mass * shrink
                 mean = mean * shrink
                 for x in range(n_x):
-                    dp = dot(v_refs[x][key], g, NT)
+                    dp = dot(values[x, key], g, NT)
                     p_keep[slot, x] = dp
                     e = jnp.exp2((s_keep[slot, x] - top) * power)
                     mass = mass + jnp.sum(e, axis=0, keepdims=True)
@@ -136,10 +168,7 @@
                     ds = (p * (p_keep[slot, x] - delta)).astype(bf16)
                     dv = dot(p.astype(bf16), g, NN)
                     dk = dot(ds, q, NN)
-                    if dqt:
-                        dq = dot(k_refs[x][key], ds, TN)
-                    else:
-                        dq = dot(ds, k_refs[x][key], TN)
+                    dq = dot(ds, keys[x, key], TN)
                     total = dq if total is None else total + dq
                     if fresh:
                         v_acc[x, key] = dv
@@ -155,10 +184,7 @@
             back(block, True)
             lax.fori_loop(low, block, lambda key, _: (back(key, False), 0)[1], 0)
             for h in range(heads):
-                if dqt:
-                    mine = (q_acc[:, h * part:(h + 1) * part] * factor).T.astype(bf16)
-                else:
-                    mine = (q_acc[h * part:(h + 1) * part, :] * factor).astype(bf16)
+                mine = (q_acc[h * part:(h + 1) * part, :] * factor).astype(bf16)
                 dq_ref[:, pl.ds(at, groups), h * head_dim:(h + 1) * head_dim] = mine.reshape(n_y, groups, head_dim)
 
             if has_carry:
@@ -172,55 +198,62 @@
     lax.fori_loop(begin, begin + count, one_block, 0)
 
 
-def attention(first, my_x, packed, keys, values, begin, count, carry=None, dqt=False):
-    groups, n_y, rows, head_dim = packed.shape
-    n_x = len(keys)
+def attention(first, my_x, packed, near, begin, count, late=None, carry=()):
+    groups, n_y, _, head_dim = packed.shape
+    n_x = HEADS // KV_HEADS
     cap = first.shape[0]
+    early = near[3].shape[0]
     part = groups * n_y
     span = n_x * part
     vmem = pl.BlockSpec(memory_space=pltpu.VMEM)
     smem = pl.BlockSpec(memory_space=pltpu.SMEM)
+    anywhere = pl.BlockSpec(memory_space=pl.ANY)
     shape = jax.ShapeDtypeStruct
     dq = shape((n_y, count * groups, n_x * head_dim), bf16)
-    slots = MAXDOC if carry is not None else min(MAXDOC, count)
+    has_carry = late is not None
+    reach = begin + count
+    slots = min(MAXDOC, reach)
+    sums = (n_x, reach, part, head_dim)
+    more = (late, *carry) if has_carry else ()
     scratch = [
         pltpu.VMEM((2 * count, span, head_dim), bf16),
+        pltpu.VMEM((n_x, reach, part, head_dim), bf16),
+        pltpu.VMEM((n_x, reach, part, head_dim), bf16),
         pltpu.VMEM((slots, n_x, part, span), f32),
         pltpu.VMEM((slots, n_x, part, span), f32),
+        pltpu.VMEM((span, head_dim), f32),
+        pltpu.SemaphoreType.DMA((2 * n_x + (2 * n_x + 2 if has_carry else 0),)),
     ]
-    sums = (n_x, begin + count, part, head_dim)
-    total = [pltpu.VMEM((head_dim, span) if dqt else (span, head_dim), f32)]
-    if carry is None:
+    if has_carry:
+        out = (dq,) + (shape((n_y, cap * groups, head_dim), bf16),) * (2 * n_x)
+        scratch = scratch + [pltpu.VMEM(sums, f32)] * 2
+    else:
         out = (dq, shape(sums, f32), shape(sums, f32))
-        carry = ()
-        scratch = scratch + total
-    else:
-        out = (dq,) + (shape((n_y, cap * groups, head_dim), bf16),) * (2 * n_x)
-        scratch = scratch + [pltpu.VMEM(sums, f32)] * 2 + total
     pairs = count * 2
     return pl.pallas_call(
-        functools.partial(attention_kernel, begin, count, cap, n_x, bool(carry), dqt),
+        functools.partial(attention_kernel, begin, count, cap, early, n_x, has_carry),
         out_shape=out,
-        in_specs=[smem, smem] + [vmem] * (1 + 2 * n_x + len(carry)),
+        in_specs=[smem, smem, vmem] + [anywhere] * (len(near) + len(more)),
         out_specs=(vmem,) * len(out),
         scratch_shapes=scratch,
-        compiler_params=pltpu.CompilerParams(vmem_limit_bytes=48 * 2**20),
+        compiler_params=pltpu.CompilerParams(vmem_limit_bytes=60 * 2**20),
         cost_estimate=pl.CostEstimate(
             flops=pairs * 10 * span * span * head_dim, bytes_accessed=8 * 2**20, transcendentals=pairs * 2 * span * span),
         name="attention",
-    )(first, my_x, packed, *keys, *values, *carry)
-
-
-def pack_kernel(begin, count, cap, with_kv, *refs):
+    )(first, my_x, packed, *near, *more)
+
+
+def pack_kernel(begin, count, cap, early, *refs):
     lens_ref, groups_ref, offsets_ref, q_ref, g_ref = refs[:5]
-    if with_kv:
-        k_ref, v_ref, out_ref, pick, pick_kv = refs[5:]
+    if early:
+        k_ref, v_ref, out_ref, pick_quad, pick_one, pick_kv = refs[5:]
     else:
-        out_ref, pick = refs[5:]
-    n_grp = out_ref.shape[0]
+        out_ref, pick_quad, pick_one = refs[5:]
+    n_grp, _, _, head_dim = out_ref.shape
     units = q_ref.shape[0]
-    head_dim = out_ref.shape[3]
-    per = 2 * count
+    heads = q_ref.shape[1] // head_dim
+    per = 2 * QUAD
+    quads, ones = count // QUAD, count % QUAD
 
     @pl.when(pl.program_id(0) == 0)
     def _():
@@ -231,29 +264,43 @@
         start = dot(many, jnp.where(before, 1.0, 0.0).astype(bf16), NN)[:1].astype(jnp.int32)
         low = groups_ref[...] * cap + offsets_ref[...]
 
-        def choose(first, blocks, into):
-            rows = n_grp * 2 * blocks
-            row = lax.broadcasted_iota(jnp.int32, (rows, docs), 0)
-            place = row // (2 * blocks) * cap + first + row % blocks
+        def choose(rows, block, shift, width):
+            place = lax.broadcasted_iota(jnp.int32, (n_grp * rows, docs), 0)
+            place = place // rows * cap + block(place % rows)
             inside = (place >= low) & (place < low + lens)
             source = jnp.sum(jnp.where(inside, start - low + place + 1, 0), axis=1, keepdims=True) - 1
-            kind = lax.broadcasted_iota(jnp.int32, (rows, 1), 0) // blocks % 2
-            wanted = jnp.where(source >= 0, source + kind * units, -1)
-            column = lax.broadcasted_iota(jnp.int32, (rows, 2 * units), 1)
-            into[...] = jnp.where(column == wanted, 1.0, 0.0).astype(bf16)
-
-        choose(begin, count, pick)
-        if with_kv:
-            choose(0, cap, pick_kv)
-
-    moved = dot(pick[...], jnp.concatenate([q_ref[...], g_ref[...]], axis=0), NN)
-    heads = moved.shape[1] // head_dim
-    for h in range(heads):
-        slab = moved[:, h * head_dim:(h + 1) * head_dim].reshape(n_grp, per, head_dim)
-        out_ref[:, 0, h * per:(h + 1) * per, :] = slab.astype(bf16)
-    if with_kv:
+            row = lax.broadcasted_iota(jnp.int32, (n_grp * rows, 1), 0) % rows
+            wanted = jnp.where(source >= 0, source + shift(row) * units, -1)
+            column = lax.broadcasted_iota(jnp.int32, (n_grp * rows, width * units), 1)
+            return jnp.where(column == wanted, 1.0, 0.0).astype(bf16)
+
+        for j in range(quads):
+            pick_quad[j] = choose(per, lambda r: begin + j * QUAD + r % QUAD, lambda r: r // QUAD, 2)
+        for i in range(ones):
+            pick_one[i] = choose(per, lambda r: r * 0 + (begin + quads * QUAD + i), lambda r: r, 2 * heads)
+        if early:
+            rest = cap - early
+            pick_kv[...] = choose(
+                2 * cap,
+                lambda r: jnp.where(r < 2 * early, r % early, early + (r - 2 * early) % rest),
+                lambda r: jnp.where(r < 2 * early, r // early, (r - 2 * early) // rest),
+                2)
+
+    both = jnp.concatenate([q_ref[...], g_ref[...]], axis=0)
+    for j in range(quads):
+        moved = dot(pick_quad[j], both, NN)
+        for h in range(heads):
+            at = (j * heads + h) * per
+            slab = moved[:, h * head_dim:(h + 1) * head_dim].reshape(n_grp, per, head_dim)
+            out_ref[:, 0, at:at + per, :] = slab.astype(bf16)
+    if ones:
+        tall = jnp.concatenate([both[:, h * head_dim:(h + 1) * head_dim] for h in range(heads)], axis=0)
+    for i in range(ones):
+        at = (quads * heads + i) * per
+        out_ref[:, 0, at:at + per, :] = dot(pick_one[i], tall, NN).reshape(n_grp, per, head_dim).astype(bf16)
+    if early:
         both = dot(pick_kv[...], jnp.concatenate([k_ref[...], v_ref[...]], axis=0), NN)
-        out_ref[:, 0, heads * per:, :] = both.reshape(n_grp, 2 * cap, head_dim).astype(bf16)
+        out_ref[:, 0, 2 * heads * count:, :] = both.reshape(n_grp, 2 * cap, head_dim).astype(bf16)
 
 
 def pack(tables, q, g, kv, n_grp, n_y, begin, count, cap):
@@ -263,17 +310,21 @@
     table = pl.BlockSpec((1, tables[0].shape[1]), lambda y: (0, 0))
     wide = pl.BlockSpec((units, heads * HEAD_DIM), lambda y: (0, y))
     thin = pl.BlockSpec((units, HEAD_DIM), lambda y: (0, y))
-    scratch = [pltpu.VMEM((n_grp * 2 * count, 2 * units), bf16)]
+    tall = n_grp * 2 * QUAD
+    scratch = [
+        pltpu.VMEM((count // QUAD, tall, 2 * units), bf16),
+        pltpu.VMEM((max(1, count % QUAD), tall, 2 * heads * units), bf16),
+    ]
     if kv:
         scratch.append(pltpu.VMEM((n_grp * 2 * cap, 2 * units), bf16))
     return pl.pallas_call(
-        functools.partial(pack_kernel, begin, count, cap, bool(kv)),
+        functools.partial(pack_kernel, begin, count, cap, count if kv else 0),
         out_shape=jax.ShapeDtypeStruct((n_grp, n_y, rows, HEAD_DIM), bf16),
         grid=(n_y,),
         in_specs=[table] * 3 + [wide] * 2 + [thin] * len(kv),
         out_specs=pl.BlockSpec((n_grp, 1, rows, HEAD_DIM), lambda y: (0, y, 0, 0)),
         scratch_shapes=scratch,
-        compiler_params=pltpu.CompilerParams(vmem_limit_bytes=24 * 2**20),
+        compiler_params=pltpu.CompilerParams(vmem_limit_bytes=60 * 2**20),
         cost_estimate=pl.CostEstimate(flops=2 * 10**9, bytes_accessed=6 * 2**20, transcendentals=0),
         name="pack",
     )(*tables, q, g, *kv)
@@ -351,20 +402,21 @@
     early = exchange(pack(tables, q, g, (k, v), n_grp, n_y, 0, split, cap))
     late = exchange(pack(tables, q, g, (), n_grp, n_y, split, cap - split, cap))
 
-    at = n_x * 2 * split
-    k0, v0 = (
-        early[:, :, at + i * cap:at + (i + 1) * cap].transpose(2, 1, 0, 3).reshape(cap, n_y * n_grp, HEAD_DIM)
-        for i in range(2)
-    )
-    k3, v1 = step(k0, 1), step(v0, -1)
-    v3, k1 = step(v0, 1), step(k0, -1)
-    k2, v2 = step(k3, 1), step(v1, -1)
-    keys, values = (k0, k1, k2, k3), (v0, v1, v2, v3)
+    at = 2 * n_x * split
+
+    def keys_of(first_row, rows):
+        taken = early[:, :, at + first_row:at + first_row + rows]
+        return taken.transpose(2, 1, 0, 3).reshape(rows, n_y * n_grp, HEAD_DIM)
+
+    own = keys_of(0, 2 * split)
+    left, right = step(own, 1), step(own, -1)
+    near = (own, right, left, step(left[:split], 1), step(right[split:], -1))
+    far = lax.all_gather(keys_of(2 * split, 2 * (cap - split)), "x", axis=0)
 
     first = first_blocks(doc_lengths, doc_groups, doc_offsets, cap)
     my_x = lax.axis_index("x").astype(jnp.int32).reshape(1)
-    dq_early, k_sums, v_sums = attention(first, my_x, early, keys, values, 0, split)
-    dq_late, *grads = attention(first, my_x, late, keys, values, split, cap - split, (k_sums, v_sums))
+    dq_early, k_sums, v_sums = attention(first, my_x, early, near, 0, split)
+    dq_late, *grads = attention(first, my_x, late, near, split, cap - split, far, (k_sums, v_sums))
     dk, dv = grads[:n_x], grads[n_x:]
 
     dq_early = lax.all_to_all(dq_early, "y", 0, 0, tiled=True)

time: 238 us -> 241 us (1.013)
  the two profiles are of different devices: /device:TPU:193 before, /device:TPU:6 now
where the time goes in v4:
time: 241 us; the launch traced here: 237 us
  waiting for transfers between devices  111 us (46%)
  starting transfers between devices  73.3 us (30%)
  Pallas kernels  34.3 us (14%)
  between operations  14.4 us (6%)
    all_to_all x2, waiting for transfers between devices, exchange(): lax.all_to_all(message.reshape(n_grp * n_y, rows, HEAD_DIM), ('grp', 'y')...  50.3 us
    ppermute x10, starting transfers between devices, step(): return lax.ppermute(array, 'x', [(i, (i + by) % n_x) for i in range(n_x)])  31.9 us
    ppermute x10, waiting for transfers between devices, step(): return lax.ppermute(array, 'x', [(i, (i + by) % n_x) for i in range(n_x)])  29.2 us
    all_to_all x2, starting transfers between devices, exchange(): lax.all_to_all(message.reshape(n_grp * n_y, rows, HEAD_DIM), ('grp', 'y')...  26 us
    all_to_all x1, waiting for transfers between devices, on_device(): sums = lax.all_to_all(sums, 'y', 0, 0, tiled=True)  19.5 us
    pallas_call x2, Pallas kernels, pack(): pl.pallas_call(functools.partial(pack_kernel, begin, count, cap, count if...  15.8 us
    pallas_call x2, Pallas kernels, attention(): pl.pallas_call(functools.partial(attention_kernel, begin, count, cap, ear...  15 us
    all_to_all x1, waiting for transfers between devices, on_device(): dq_early = lax.all_to_all(dq_early, 'y', 0, 0, tiled=True)  12.3 us
  transfers between devices with their start and end apart: 16, of which 12 were waited for; matrix products, arithmetic and copies ran while one was open for 1% of the time, Pallas kernels for 11%

profile of v4, /device:TPU:6, one launch (start us, length us, event | category | flops | bytes accessed | tf_op | source)
XLA Modules:
  0.0 236.6 jit_solution(12281434595403279284)
XLA Ops:
  7.2 8.0 %pack.2 = bf16[16,8,64,128]{3,2,1,0:T(8,128)(2,1)} custom-call(s32[1,192]{1,0:T(1,128)} %bitcast.36, s32[1,192]{1,0:T(1,128)} %bitcast.34, s32[1,192]{1,0:T(1,128)} %bitcast.32, bf16[128,4096]{1,0:T(8,128)(2,1)} %bitcast.38, bf16[128,4096]{1,0:T(8,128)(2,1)} %bitcast.40, bf16[128,1024]{1,0:T(8,128)(2,1)} %bitcast.44, bf16[128,1024]{1,0:T(8,128)(2,1)} %bitcast.45), custom_call_target="tpu_custom_call" | custom-call | flops 2000000000 | bytes 6291456 | tf_op jit(solution)/shard_map/pack/pallas_call | solution.py:320
  15.1 17.8 %all-to-all-start = ((bf16[128,64,128]{2,1,0:T(8,128)(2,1)}), bf16[128,64,128]{2,1,0:T(8,128)(2,1)S(1)}, u32[]{:S(2)}, u32[]{:S(2)}) async-start(bf16[128,64,128]{2,1,0:T(8,128)(2,1)} %bitcast.24), calls=%async_computation | async-start | bytes 4194304 | tf_op jit(solution)/shard_map/all_to_all | solution.py:399
  32.9 7.8 %pack.3 = bf16[16,8,56,128]{3,2,1,0:T(8,128)(2,1)} custom-call(s32[1,192]{1,0:T(1,128)} %bitcast.37, s32[1,192]{1,0:T(1,128)} %bitcast.35, s32[1,192]{1,0:T(1,128)} %bitcast.33, bf16[128,4096]{1,0:T(8,128)(2,1)} %bitcast.39, bf16[128,4096]{1,0:T(8,128)(2,1)} %bitcast.41), custom_call_target="tpu_custom_call" | custom-call | flops 2000000000 | bytes 6291456 | tf_op jit(solution)/shard_map/pack/pallas_call | solution.py:320
  40.8 44.3 %all-to-all-done = bf16[128,64,128]{2,1,0:T(8,128)(2,1)S(1)} async-done(((bf16[128,64,128]{2,1,0:T(8,128)(2,1)}), bf16[128,64,128]{2,1,0:T(8,128)(2,1)S(1)}, u32[]{:S(2)}, u32[]{:S(2)}) %all-to-all-start) | async-done | bytes 2097184 | tf_op jit(solution)/shard_map/all_to_all | solution.py:399
  85.1 8.2 %all-to-all-start.2 = ((bf16[128,56,128]{2,1,0:T(8,128)(2,1)}), bf16[128,56,128]{2,1,0:T(8,128)(2,1)}, u32[]{:S(2)}, u32[]{:S(2)}) async-start(bf16[128,56,128]{2,1,0:T(8,128)(2,1)} %bitcast.25), calls=%async_computation.2 | async-start | bytes 3670016 | tf_op jit(solution)/shard_map/all_to_all | solution.py:399
  93.3 0.0 copy-start.8
  93.3 0.0 copy-start.10
  93.3 0.0 all-gather.2.cloned.1.call-start
  93.3 0.2 slice_bitcast_fusion
  93.5 0.0 copy-start.9
  93.6 1.1 copy.16
  94.6 0.0 all-gather.2.cloned.1.call-update
  94.7 0.0 copy-done.8
  94.7 0.0 copy-done.10
  94.7 0.0 copy-done.2
  94.7 0.1 slice_bitcast_fusion.1
  94.8 0.2 copy.15
  95.0 0.0 copy-start.5
  95.0 2.7 %collective-permute-start = (bf16[10,128,128]{2,1,0:T(8,128)(2,1)S(1)}, bf16[10,128,128]{2,1,0:T(8,128)(2,1)S(1)}, u32[]{:S(2)}, u32[]{:S(2)}) collective-permute-start(bf16[10,128,128]{2,1,0:T(8,128)(2,1)S(1)} %bitcast.28), channel_id=1, source_target_pairs={{0,24},{8,0},{16,8},{24,16},{1,25},{9,1},{17,9},{25,17},{2,26},{10... | collective-permute-start | bytes 983048 | tf_op jit(solution)/shard_map/ppermute | solution.py:385
  97.8 4.3 %collective-permute-start.1 = (bf16[10,128,128]{2,1,0:T(8,128)(2,1)S(1)}, bf16[10,128,128]{2,1,0:T(8,128)(2,1)S(1)}, u32[]{:S(2)}, u32[]{:S(2)}) collective-permute-start(bf16[10,128,128]{2,1,0:T(8,128)(2,1)S(1)} %bitcast.29), channel_id=1, source_target_pairs={{0,8},{8,16},{16,24},{24,0},{1,9},{9,17},{17,25},{25,1},{2,10},{10... | collective-permute-start | bytes 983048 | tf_op jit(solution)/shard_map/ppermute | solution.py:385
  102.1 0.0 copy-done.9
  102.1 0.1 select_reduce_fusion
  102.2 6.3 %collective-permute-done.1.refs_5_ = bf16[10,128,128]{2,1,0:T(8,128)(2,1)S(1)} collective-permute-done((bf16[10,128,128]{2,1,0:T(8,128)(2,1)S(1)}, bf16[10,128,128]{2,1,0:T(8,128)(2,1)S(1)}, u32[]{:S(2)}, u32[]{:S(2)}) %collective-permute-start.1) | collective-permute-done | bytes 327712 | tf_op jit(solution)/shard_map/ppermute | solution.py:385
  108.6 5.5 %collective-permute-start.2 = (bf16[5,128,128]{2,1,0:T(8,128)(2,1)S(1)}, bf16[5,128,128]{2,1,0:T(8,128)(2,1)S(1)}, u32[]{:S(2)}, u32[]{:S(2)}) collective-permute-start(bf16[5,128,128]{2,1,0:T(8,128)(2,1)S(1)} %slice.17), channel_id=1, source_target_pairs={{0,8},{8,16},{16,24},{24,0},{1,9},{9,17},{17,25},{25,1},{2,10},{10... | collective-permute-start | bytes 491528 | tf_op jit(solution)/shard_map/ppermute | solution.py:385
  114.1 0.0 collective-permute-done.refs_4_
  114.1 0.0 copy-start.6
  114.1 1.9 collective-permute-start.3
  116.1 0.6 broadcast_add_fusion.1.refs_0_
  116.7 4.6 %collective-permute-done.2.refs_6_ = bf16[5,128,128]{2,1,0:T(8,128)(2,1)S(1)} collective-permute-done((bf16[5,128,128]{2,1,0:T(8,128)(2,1)S(1)}, bf16[5,128,128]{2,1,0:T(8,128)(2,1)S(1)}, u32[]{:S(2)}, u32[]{:S(2)}) %collective-permute-start.2) | collective-permute-done | bytes 163872 | tf_op jit(solution)/shard_map/ppermute | solution.py:385
  121.3 3.9 %collective-permute-done.3.refs_7_ = bf16[5,128,128]{2,1,0:T(8,128)(2,1)S(1)} collective-permute-done((bf16[5,128,128]{2,1,0:T(8,128)(2,1)S(1)}, bf16[5,128,128]{2,1,0:T(8,128)(2,1)S(1)}, u32[]{:S(2)}, u32[]{:S(2)}) %collective-permute-start.3) | collective-permute-done | bytes 163872 | tf_op jit(solution)/shard_map/ppermute | solution.py:385
  125.2 0.0 copy-done.5
  125.2 0.0 copy-done.7
  125.2 0.0 copy-done.6
  125.2 0.0 copy-done.12
  125.2 0.6 copy-done.13
  125.8 7.6 %attention.2 = (bf16[8,80,512]{2,1,0:T(8,128)(2,1)}, f32[4,5,128,128]{3,2,1,0:T(8,128)}, f32[4,5,128,128]{3,2,1,0:T(8,128)}) custom-call(s32[12]{0:T(128)} %broadcast_add_fusion.1.refs_0_, s32[1]{0:T(128)} %bitcast.refs_1_, bf16[16,8,64,128]{3,2,1,0:T(8,128)(2,1)} %bitcast.23, bf16[10,128,128]{2,1,0:T(8,128)(2,1)} %bitcast.30, ...), custom_call_target="tpu_custom_call" | custom-call | flops 3355443200 | bytes 8388608 | tf_op jit(solution)/shard_map/attention/pallas_call | solution.py:233
  133.5 6.0 %all-to-all-done.2 = bf16[128,56,128]{2,1,0:T(8,128)(2,1)} async-done(((bf16[128,56,128]{2,1,0:T(8,128)(2,1)}), bf16[128,56,128]{2,1,0:T(8,128)(2,1)}, u32[]{:S(2)}, u32[]{:S(2)}) %all-to-all-start.2) | async-done | bytes 1835040 | tf_op jit(solution)/shard_map/all_to_all | solution.py:399
  139.5 4.9 %all-to-all-start.1 = ((bf16[8,80,512]{2,1,0:T(8,128)(2,1)}), bf16[8,80,512]{2,1,0:T(8,128)(2,1)S(1)}, u32[]{:S(2)}, u32[]{:S(2)}) async-start(bf16[8,80,512]{2,1,0:T(8,128)(2,1)} %get-tuple-element.17), calls=%async_computation.1 | async-start | bytes 1310720 | tf_op jit(solution)/shard_map/all_to_all | solution.py:422
  144.4 0.0 all-gather.2.cloned.1.call-done.refs_8_
  144.4 7.4 %attention.3 = (bf16[8,112,512]{2,1,0:T(8,128)(2,1)}, bf16[8,192,128]{2,1,0:T(8,128)(2,1)}, bf16[8,192,128]{2,1,0:T(8,128)(2,1)}, bf16[8,192,128]{2,1,0:T(8,128)...) custom-call(s32[12]{0:T(128)} %broadcast_add_fusion.1.refs_0_, ...), custom_call_target="tpu_custom_call" | custom-call | flops 4697620480 | bytes 8388608 | tf_op jit(solution)/shard_map/attention/pallas_call | solution.py:233
  151.8 0.0 copy-start.4
  151.8 12.3 %all-to-all-done.1.refs_0_ = bf16[8,80,512]{2,1,0:T(8,128)(2,1)S(1)} async-done(((bf16[8,80,512]{2,1,0:T(8,128)(2,1)}), bf16[8,80,512]{2,1,0:T(8,128)(2,1)S(1)}, u32[]{:S(2)}, u32[]{:S(2)}) %all-to-all-start.1) | async-done | bytes 655392 | tf_op jit(solution)/shard_map/all_to_all | solution.py:422
  164.1 3.7 %all-to-all-start.3 = ((bf16[8,112,512]{2,1,0:T(8,128)(2,1)}), bf16[8,112,512]{2,1,0:T(8,128)(2,1)S(1)}, u32[]{:S(2)}, u32[]{:S(2)}) async-start(bf16[8,112,512]{2,1,0:T(8,128)(2,1)} %get-tuple-element.20), calls=%async_computation.3 | async-start | bytes 1835008 | tf_op jit(solution)/shard_map/all_to_all | solution.py:423
  167.8 2.2 collective-permute-start.4
  170.1 3.6 %collective-permute-start.8 = (bf16[8,192,128]{2,1,0:T(8,128)(2,1)}, bf16[8,192,128]{2,1,0:T(8,128)(2,1)S(1)}, u32[]{:S(2)}, u32[]{:S(2)}) collective-permute-start(bf16[8,192,128]{2,1,0:T(8,128)(2,1)} %get-tuple-element.28), channel_id=1, source_target_pairs={{0,24},{8,0},{16,8},{24,16},{1,25},{9,1},{17,9},{25,17},{2,26},{10... | collective-permute-start | bytes 1179656 | tf_op jit(solution)/shard_map/ppermute | solution.py:385
  173.7 2.3 collective-permute-start.6
  176.0 0.0 copy-done.11
  176.0 4.8 %collective-permute-start.7 = (bf16[8,192,128]{2,1,0:T(8,128)(2,1)S(1)}, bf16[8,192,128]{2,1,0:T(8,128)(2,1)S(1)}, u32[]{:S(2)}, u32[]{:S(2)}) collective-permute-start(bf16[8,192,128]{2,1,0:T(8,128)(2,1)S(1)} %copy-done.11), channel_id=1, source_target_pairs={{0,8},{8,16},{16,24},{24,0},{1,9},{9,17},{17,25},{25,1},{2,10},{10... | collective-permute-start | bytes 1179656 | tf_op jit(solution)/shard_map/ppermute | solution.py:385
  180.8 0.5 collective-permute-done.4
  181.2 0.1 add_convert_fusion.1
  181.3 2.1 collective-permute-start.5
  183.4 2.0 collective-permute-done.8
  185.4 0.1 add_convert_fusion
  185.6 2.4 %collective-permute-start.9 = (bf16[8,192,128]{2,1,0:T(8,128)(2,1)S(1)}, bf16[8,192,128]{2,1,0:T(8,128)(2,1)S(1)}, u32[]{:S(2)}, u32[]{:S(2)}) collective-permute-start(bf16[8,192,128]{2,1,0:T(8,128)(2,1)S(1)} %add_convert_fusion), channel_id=1, source_target_pairs={{0,24},{8,0},{16,8},{24,16},{1,25},{9,1},{17,9},{25,17},{2,26},{10... | collective-permute-start | bytes 1179656 | tf_op jit(solution)/shard_map/ppermute | solution.py:385
  188.0 5.9 %collective-permute-done.6.refs_2_ = bf16[8,192,128]{2,1,0:T(8,128)(2,1)S(1)} collective-permute-done((bf16[8,192,128]{2,1,0:T(8,128)(2,1)}, bf16[8,192,128]{2,1,0:T(8,128)(2,1)S(1)}, u32[]{:S(2)}, u32[]{:S(2)}) %collective-permute-start.6) | collective-permute-done | bytes 393248 | tf_op jit(solution)/shard_map/ppermute | solution.py:385
  193.9 0.0 collective-permute-done.7.refs_4_
  193.9 2.9 %collective-permute-done.5.refs_1_ = bf16[8,192,128]{2,1,0:T(8,128)(2,1)S(1)} collective-permute-done((bf16[8,192,128]{2,1,0:T(8,128)(2,1)S(1)}, bf16[8,192,128]{2,1,0:T(8,128)(2,1)S(1)}, u32[]{:S(2)}, u32[]{:S(2)}) %collective-permute-start.5) | collective-permute-done | bytes 393248 | tf_op jit(solution)/shard_map/ppermute | solution.py:385
  196.8 3.1 %collective-permute-done.9.refs_5_ = bf16[8,192,128]{2,1,0:T(8,128)(2,1)S(1)} collective-permute-done((bf16[8,192,128]{2,1,0:T(8,128)(2,1)S(1)}, bf16[8,192,128]{2,1,0:T(8,128)(2,1)S(1)}, u32[]{:S(2)}, u32[]{:S(2)}) %collective-permute-start.9) | collective-permute-done | bytes 393248 | tf_op jit(solution)/shard_map/ppermute | solution.py:385
  199.9 1.2 add_up.1
  201.1 0.0 all-to-all-done.3.refs_1_
  201.1 6.8 %all-to-all-start.4 = ((bf16[8,384,128]{2,1,0:T(8,128)(2,1)}), bf16[8,384,128]{2,1,0:T(8,128)(2,1)S(1)}, u32[]{:S(2)}, u32[]{:S(2)}) async-start(bf16[8,384,128]{2,1,0:T(8,128)(2,1)} %add_up.1), calls=%async_computation.4 | async-start | bytes 1572864 | tf_op jit(solution)/shard_map/all_to_all | solution.py:432
  207.9 1.2 lay_out.2
  209.1 19.5 %all-to-all-done.4.refs_0_ = bf16[8,384,128]{2,1,0:T(8,128)(2,1)S(1)} async-done(((bf16[8,384,128]{2,1,0:T(8,128)(2,1)}), bf16[8,384,128]{2,1,0:T(8,128)(2,1)S(1)}, u32[]{:S(2)}, u32[]{:S(2)}) %all-to-all-start.4) | async-done | bytes 786464 | tf_op jit(solution)/shard_map/all_to_all | solution.py:432
  228.7 1.1 lay_out.3
  (16 shorter events, 0.1 us)
Async XLA Ops:
  15.1 69.9 %all-to-all-start = ((bf16[128,64,128]{2,1,0:T(8,128)(2,1)}), bf16[128,64,128]{2,1,0:T(8,128)(2,1)S(1)}, u32[]{:S(2)}, u32[]{:S(2)}) async-start(bf16[128,64,128]{2,1,0:T(8,128)(2,1)} %bitcast.24), calls=%async_computation | async-start | bytes 4194304 | tf_op jit(solution)/shard_map/all_to_all | solution.py:399
  85.1 9.6 %copy-start.2 = (bf16[128,64,128]{2,1,0:T(8,128)(2,1)}, bf16[128,64,128]{2,1,0:T(8,128)(2,1)S(1)}, u32[]{:S(2)}) copy-start(bf16[128,64,128]{2,1,0:T(8,128)(2,1)S(1)} %all-to-all-done) | copy-start | bytes 6291460
  85.1 54.4 %all-to-all-start.2 = ((bf16[128,56,128]{2,1,0:T(8,128)(2,1)}), bf16[128,56,128]{2,1,0:T(8,128)(2,1)}, u32[]{:S(2)}, u32[]{:S(2)}) async-start(bf16[128,56,128]{2,1,0:T(8,128)(2,1)} %bitcast.25), calls=%async_computation.2 | async-start | bytes 3670016 | tf_op jit(solution)/shard_map/all_to_all | solution.py:399
  93.3 1.4 copy-start.8
  93.3 1.4 copy-start.10
  93.3 51.1 %all-gather.2.cloned.1.call-start = ((), (), s32[]{:S(2)}) async-start(), calls=%async_computation.5 | async-start | bytes 2293760 | tf_op jit(solution)/shard_map/all_gather | solution.py:414
  93.5 8.5 %copy-start.9 = (s32[192]{0:T(256)S(1)}, s32[192]{0:T(256)}, u32[]{:S(2)}) copy-start(s32[192]{0:T(256)} %param.12) | copy-start | bytes 2308
  95.0 30.1 %copy-start.5 = (bf16[10,8,16,128]{3,2,1,0:T(8,128)(2,1)}, bf16[10,8,16,128]{3,2,1,0:T(8,128)(2,1)S(1)}, u32[]{:S(2)}) copy-start(bf16[10,8,16,128]{3,2,1,0:T(8,128)(2,1)S(1)} %copy.15) | copy-start | bytes 983044
  95.0 19.1 %collective-permute-start = (bf16[10,128,128]{2,1,0:T(8,128)(2,1)S(1)}, bf16[10,128,128]{2,1,0:T(8,128)(2,1)S(1)}, u32[]{:S(2)}, u32[]{:S(2)}) collective-permute-start(bf16[10,128,128]{2,1,0:T(8,128)(2,1)S(1)} %bitcast.28), channel_id=1, source_target_pairs={{0,24},{8,0},{16,8},{24,16},{1,25},{9,1},{17,9},{25,17},{2,26},{10... | collective-permute-start | bytes 983048 | tf_op jit(solution)/shard_map/ppermute | solution.py:385
  97.8 10.8 %collective-permute-start.1 = (bf16[10,128,128]{2,1,0:T(8,128)(2,1)S(1)}, bf16[10,128,128]{2,1,0:T(8,128)(2,1)S(1)}, u32[]{:S(2)}, u32[]{:S(2)}) collective-permute-start(bf16[10,128,128]{2,1,0:T(8,128)(2,1)S(1)} %bitcast.29), channel_id=1, source_target_pairs={{0,8},{8,16},{16,24},{24,0},{1,9},{9,17},{17,25},{25,1},{2,10},{10... | collective-permute-start | bytes 983048 | tf_op jit(solution)/shard_map/ppermute | solution.py:385
  108.6 16.6 %copy-start.7 = (bf16[10,128,128]{2,1,0:T(8,128)(2,1)}, bf16[10,128,128]{2,1,0:T(8,128)(2,1)S(1)}, u32[]{:S(2)}) copy-start(bf16[10,128,128]{2,1,0:T(8,128)(2,1)S(1)} %collective-permute-done.1.refs_5_) | copy-start | bytes 983044
  108.6 12.7 %collective-permute-start.2 = (bf16[5,128,128]{2,1,0:T(8,128)(2,1)S(1)}, bf16[5,128,128]{2,1,0:T(8,128)(2,1)S(1)}, u32[]{:S(2)}, u32[]{:S(2)}) collective-permute-start(bf16[5,128,128]{2,1,0:T(8,128)(2,1)S(1)} %slice.17), channel_id=1, source_target_pairs={{0,8},{8,16},{16,24},{24,0},{1,9},{9,17},{17,25},{25,1},{2,10},{10... | collective-permute-start | bytes 491528 | tf_op jit(solution)/shard_map/ppermute | solution.py:385
  114.1 11.1 %copy-start.6 = (bf16[10,128,128]{2,1,0:T(8,128)(2,1)}, bf16[10,128,128]{2,1,0:T(8,128)(2,1)S(1)}, u32[]{:S(2)}) copy-start(bf16[10,128,128]{2,1,0:T(8,128)(2,1)S(1)} %collective-permute-done.refs_4_) | copy-start | bytes 983044
  114.1 11.0 %collective-permute-start.3 = (bf16[5,128,128]{2,1,0:T(8,128)(2,1)S(1)}, bf16[5,128,128]{2,1,0:T(8,128)(2,1)S(1)}, u32[]{:S(2)}, u32[]{:S(2)}) collective-permute-start(bf16[5,128,128]{2,1,0:T(8,128)(2,1)S(1)} %slice.18), channel_id=1, source_target_pairs={{0,24},{8,0},{16,8},{24,16},{1,25},{9,1},{17,9},{25,17},{2,26},{10... | collective-permute-start | bytes 491528 | tf_op jit(solution)/shard_map/ppermute | solution.py:385
  121.2 3.9 %copy-start.12 = (bf16[5,128,128]{2,1,0:T(8,128)(2,1)}, bf16[5,128,128]{2,1,0:T(8,128)(2,1)S(1)}, u32[]{:S(2)}) copy-start(bf16[5,128,128]{2,1,0:T(8,128)(2,1)S(1)} %collective-permute-done.2.refs_6_) | copy-start | bytes 491524
  125.2 0.7 copy-start.13
  139.5 24.6 %all-to-all-start.1 = ((bf16[8,80,512]{2,1,0:T(8,128)(2,1)}), bf16[8,80,512]{2,1,0:T(8,128)(2,1)S(1)}, u32[]{:S(2)}, u32[]{:S(2)}) async-start(bf16[8,80,512]{2,1,0:T(8,128)(2,1)} %get-tuple-element.17), calls=%async_computation.1 | async-start | bytes 1310720 | tf_op jit(solution)/shard_map/all_to_all | solution.py:422
  151.8 24.2 %copy-start.11 = (bf16[8,192,128]{2,1,0:T(8,128)(2,1)S(1)}, bf16[8,192,128]{2,1,0:T(8,128)(2,1)}, u32[]{:S(2)}) copy-start(bf16[8,192,128]{2,1,0:T(8,128)(2,1)} %get-tuple-element.26) | copy-start | bytes 1179652
  151.8 29.4 %copy-start.4 = (bf16[8,192,128]{2,1,0:T(8,128)(2,1)S(1)}, bf16[8,192,128]{2,1,0:T(8,128)(2,1)}, u32[]{:S(2)}) copy-start(bf16[8,192,128]{2,1,0:T(8,128)(2,1)} %get-tuple-element.22) | copy-start | bytes 1179652
  151.8 33.6 %copy-start.3 = (bf16[8,192,128]{2,1,0:T(8,128)(2,1)S(1)}, bf16[8,192,128]{2,1,0:T(8,128)(2,1)}, u32[]{:S(2)}) copy-start(bf16[8,192,128]{2,1,0:T(8,128)(2,1)} %get-tuple-element.27) | copy-start | bytes 1179652
  164.1 35.8 %copy-start = (bf16[8,192,128]{2,1,0:T(8,128)(2,1)S(1)}, bf16[8,192,128]{2,1,0:T(8,128)(2,1)}, u32[]{:S(2)}) copy-start(bf16[8,192,128]{2,1,0:T(8,128)(2,1)} %get-tuple-element.21.refs_0_) | copy-start | bytes 1179652
  164.1 35.8 %copy-start.1 = (bf16[8,192,128]{2,1,0:T(8,128)(2,1)S(1)}, bf16[8,192,128]{2,1,0:T(8,128)(2,1)}, u32[]{:S(2)}) copy-start(bf16[8,192,128]{2,1,0:T(8,128)(2,1)} %get-tuple-element.25.refs_3_) | copy-start | bytes 1179652
  164.1 36.9 %all-to-all-start.3 = ((bf16[8,112,512]{2,1,0:T(8,128)(2,1)}), bf16[8,112,512]{2,1,0:T(8,128)(2,1)S(1)}, u32[]{:S(2)}, u32[]{:S(2)}) async-start(bf16[8,112,512]{2,1,0:T(8,128)(2,1)} %get-tuple-element.20), calls=%async_computation.3 | async-start | bytes 1835008 | tf_op jit(solution)/shard_map/all_to_all | solution.py:423
  167.8 13.4 %collective-permute-start.4 = (bf16[8,192,128]{2,1,0:T(8,128)(2,1)}, bf16[8,192,128]{2,1,0:T(8,128)(2,1)S(1)}, u32[]{:S(2)}, u32[]{:S(2)}) collective-permute-start(bf16[8,192,128]{2,1,0:T(8,128)(2,1)} %get-tuple-element.23), channel_id=1, source_target_pairs={{0,8},{8,16},{16,24},{24,0},{1,9},{9,17},{17,25},{25,1},{2,10},{10... | collective-permute-start | bytes 1179656 | tf_op jit(solution)/shard_map/ppermute | solution.py:385
  170.1 15.4 %collective-permute-start.8 = (bf16[8,192,128]{2,1,0:T(8,128)(2,1)}, bf16[8,192,128]{2,1,0:T(8,128)(2,1)S(1)}, u32[]{:S(2)}, u32[]{:S(2)}) collective-permute-start(bf16[8,192,128]{2,1,0:T(8,128)(2,1)} %get-tuple-element.28), channel_id=1, source_target_pairs={{0,24},{8,0},{16,8},{24,16},{1,25},{9,1},{17,9},{25,17},{2,26},{10... | collective-permute-start | bytes 1179656 | tf_op jit(solution)/shard_map/ppermute | solution.py:385
  173.7 20.2 %collective-permute-start.6 = (bf16[8,192,128]{2,1,0:T(8,128)(2,1)}, bf16[8,192,128]{2,1,0:T(8,128)(2,1)S(1)}, u32[]{:S(2)}, u32[]{:S(2)}) collective-permute-start(bf16[8,192,128]{2,1,0:T(8,128)(2,1)} %get-tuple-element.24), channel_id=1, source_target_pairs={{0,24},{8,0},{16,8},{24,16},{1,25},{9,1},{17,9},{25,17},{2,26},{10... | collective-permute-start | bytes 1179656 | tf_op jit(solution)/shard_map/ppermute | solution.py:385
  176.0 17.9 %collective-permute-start.7 = (bf16[8,192,128]{2,1,0:T(8,128)(2,1)S(1)}, bf16[8,192,128]{2,1,0:T(8,128)(2,1)S(1)}, u32[]{:S(2)}, u32[]{:S(2)}) collective-permute-start(bf16[8,192,128]{2,1,0:T(8,128)(2,1)S(1)} %copy-done.11), channel_id=1, source_target_pairs={{0,8},{8,16},{16,24},{24,0},{1,9},{9,17},{17,25},{25,1},{2,10},{10... | collective-permute-start | bytes 1179656 | tf_op jit(solution)/shard_map/ppermute | solution.py:385
  181.3 15.4 %collective-permute-start.5 = (bf16[8,192,128]{2,1,0:T(8,128)(2,1)S(1)}, bf16[8,192,128]{2,1,0:T(8,128)(2,1)S(1)}, u32[]{:S(2)}, u32[]{:S(2)}) collective-permute-start(bf16[8,192,128]{2,1,0:T(8,128)(2,1)S(1)} %add_convert_fusion.1), channel_id=1, source_target_pairs={{0,8},{8,16},{16,24},{24,0},{1,9},{9,17},{17,25},{25,1},{2,10},{10... | collective-permute-start | bytes 1179656 | tf_op jit(solution)/shard_map/ppermute | solution.py:385
  185.6 14.3 %collective-permute-start.9 = (bf16[8,192,128]{2,1,0:T(8,128)(2,1)S(1)}, bf16[8,192,128]{2,1,0:T(8,128)(2,1)S(1)}, u32[]{:S(2)}, u32[]{:S(2)}) collective-permute-start(bf16[8,192,128]{2,1,0:T(8,128)(2,1)S(1)} %add_convert_fusion), channel_id=1, source_target_pairs={{0,24},{8,0},{16,8},{24,16},{1,25},{9,1},{17,9},{25,17},{2,26},{10... | collective-permute-start | bytes 1179656 | tf_op jit(solution)/shard_map/ppermute | solution.py:385
  201.1 27.6 %all-to-all-start.4 = ((bf16[8,384,128]{2,1,0:T(8,128)(2,1)}), bf16[8,384,128]{2,1,0:T(8,128)(2,1)S(1)}, u32[]{:S(2)}, u32[]{:S(2)}) async-start(bf16[8,384,128]{2,1,0:T(8,128)(2,1)} %add_up.1), calls=%async_computation.4 | async-start | bytes 1572864 | tf_op jit(solution)/shard_map/all_to_all | solution.py:432
Sparse Core Ops, SparseCore 0:
  96.2 36.1 all-gather.1

commit v5 on v4

--- a/solution.py
+++ b/solution.py
@@ -14,6 +14,7 @@
 MAXDOC = 5
 EARLY = 5
 QUAD = 4
+AT_ONCE = 4
 NN = (((1,), (0,)), ((), ()))
 NT = (((1,), (1,)), ((), ()))
 TN = (((0,), (0,)), ((), ()))
@@ -28,14 +29,16 @@
 
 def attention_kernel(begin, count, cap, early, n_x, has_carry, *refs):
     first_ref, where_ref, in_ref = refs[:3]
-    near = refs[3:8]
+    near = refs[3:3 + n_x]
     if has_carry:
-        late_ref, k_carry, v_carry, dq_ref = refs[8:12]
-        dk_refs, dv_refs = refs[12:12 + n_x], refs[12 + n_x:12 + 2 * n_x]
-        refs = refs[12 + 2 * n_x:]
+        far = refs[3 + n_x:3 + 2 * n_x]
+        k_carry, v_carry, dq_ref = refs[3 + 2 * n_x:6 + 2 * n_x]
+        refs = refs[6 + 2 * n_x:]
+        dk_refs, dv_refs = refs[:n_x], refs[n_x:2 * n_x]
+        refs = refs[2 * n_x:]
         queries, keys, values, s_keep, p_keep, q_acc, sem, k_acc, v_acc = refs
     else:
-        dq_ref, k_acc, v_acc, queries, keys, values, s_keep, p_keep, q_acc, sem = refs[8:]
+        dq_ref, k_acc, v_acc, queries, keys, values, s_keep, p_keep, q_acc, sem = refs[3 + n_x:]
     groups, n_y, _, head_dim = in_ref.shape
     heads = n_x
     part = groups * n_y
@@ -46,16 +49,13 @@
     my_x = where_ref[0]
 
     moves = []
-    own, right, left, far_k, far_v = near
-    for slot, k_from, k_row, v_from, v_row in (
-        (0, own, 0, own, early), (1, right, 0, right, early), (2, far_k, 0, far_v, 0), (3, left, 0, left, early)):
-        moves.append((k_from.at[pl.ds(k_row, early)], keys.at[slot, pl.ds(0, early)]))
-        moves.append((v_from.at[pl.ds(v_row, early)], values.at[slot, pl.ds(0, early)]))
+    for slot in range(n_x):
+        moves.append((near[slot].at[pl.ds(0, early)], keys.at[slot, pl.ds(0, early)]))
+        moves.append((near[slot].at[pl.ds(early, early)], values.at[slot, pl.ds(0, early)]))
     if has_carry:
         for slot in range(n_x):
-            x = lax.rem(my_x + slot, n_x)
-            moves.append((late_ref.at[x, pl.ds(0, rest)], keys.at[slot, pl.ds(early, rest)]))
-            moves.append((late_ref.at[x, pl.ds(rest, rest)], values.at[slot, pl.ds(early, rest)]))
+            moves.append((far[slot].at[pl.ds(0, rest)], keys.at[slot, pl.ds(early, rest)]))
+            moves.append((far[slot].at[pl.ds(rest, rest)], values.at[slot, pl.ds(early, rest)]))
         moves.append((k_carry, k_acc.at[:, pl.ds(0, early)]))
         moves.append((v_carry, v_acc.at[:, pl.ds(0, early)]))
     copies = [pltpu.make_async_copy(source, target, sem.at[i]) for i, (source, target) in enumerate(moves)]
@@ -202,7 +202,7 @@
     groups, n_y, _, head_dim = packed.shape
     n_x = HEADS // KV_HEADS
     cap = first.shape[0]
-    early = near[3].shape[0]
+    early = near[0].shape[0] // 2
     part = groups * n_y
     span = n_x * part
     vmem = pl.BlockSpec(memory_space=pltpu.VMEM)
@@ -214,7 +214,7 @@
     reach = begin + count
     slots = min(MAXDOC, reach)
     sums = (n_x, reach, part, head_dim)
-    more = (late, *carry) if has_carry else ()
+    more = (*late, *carry) if has_carry else ()
     scratch = [
         pltpu.VMEM((2 * count, span, head_dim), bf16),
         pltpu.VMEM((n_x, reach, part, head_dim), bf16),
@@ -243,7 +243,7 @@
     )(first, my_x, packed, *near, *more)
 
 
-def pack_kernel(begin, count, cap, early, *refs):
+def pack_kernel(begin, count, cap, early, heads, *refs):
     lens_ref, groups_ref, offsets_ref, q_ref, g_ref = refs[:5]
     if early:
         k_ref, v_ref, out_ref, pick_quad, pick_one, pick_kv = refs[5:]
@@ -251,7 +251,6 @@
         out_ref, pick_quad, pick_one = refs[5:]
     n_grp, _, _, head_dim = out_ref.shape
     units = q_ref.shape[0]
-    heads = q_ref.shape[1] // head_dim
     per = 2 * QUAD
     quads, ones = count // QUAD, count % QUAD
 
@@ -286,30 +285,34 @@
                 lambda r: jnp.where(r < 2 * early, r // early, (r - 2 * early) // rest),
                 2)
 
-    both = jnp.concatenate([q_ref[...], g_ref[...]], axis=0)
-    for j in range(quads):
-        moved = dot(pick_quad[j], both, NN)
-        for h in range(heads):
-            at = (j * heads + h) * per
-            slab = moved[:, h * head_dim:(h + 1) * head_dim].reshape(n_grp, per, head_dim)
-            out_ref[:, 0, at:at + per, :] = slab.astype(bf16)
-    if ones:
-        tall = jnp.concatenate([both[:, h * head_dim:(h + 1) * head_dim] for h in range(heads)], axis=0)
-    for i in range(ones):
-        at = (quads * heads + i) * per
-        out_ref[:, 0, at:at + per, :] = dot(pick_one[i], tall, NN).reshape(n_grp, per, head_dim).astype(bf16)
-    if early:
-        both = dot(pick_kv[...], jnp.concatenate([k_ref[...], v_ref[...]], axis=0), NN)
-        out_ref[:, 0, 2 * heads * count:, :] = both.reshape(n_grp, 2 * cap, head_dim).astype(bf16)
-
-
-def pack(tables, q, g, kv, n_grp, n_y, begin, count, cap):
+    width = heads * head_dim
+    for y in range(q_ref.shape[1] // width):
+        mine = slice(y * width, (y + 1) * width)
+        both = jnp.concatenate([q_ref[:, mine], g_ref[:, mine]], axis=0)
+        for j in range(quads):
+            moved = dot(pick_quad[j], both, NN)
+            for h in range(heads):
+                at = (j * heads + h) * per
+                slab = moved[:, h * head_dim:(h + 1) * head_dim].reshape(n_grp, per, head_dim)
+                out_ref[:, y, at:at + per, :] = slab.astype(bf16)
+        if ones:
+            tall = jnp.concatenate([both[:, h * head_dim:(h + 1) * head_dim] for h in range(heads)], axis=0)
+        for i in range(ones):
+            at = (quads * heads + i) * per
+            out_ref[:, y, at:at + per, :] = dot(pick_one[i], tall, NN).reshape(n_grp, per, head_dim).astype(bf16)
+        if early:
+            mine = slice(y * head_dim, (y + 1) * head_dim)
+            both = dot(pick_kv[...], jnp.concatenate([k_ref[:, mine], v_ref[:, mine]], axis=0), NN)
+            out_ref[:, y, 2 * heads * count:, :] = both.reshape(n_grp, 2 * cap, head_dim).astype(bf16)
+
+
+def pack(tables, q, g, kv, n_grp, n_y, begin, count, cap, each=AT_ONCE):
     units = q.shape[0]
     heads = q.shape[1] // (n_y * HEAD_DIM)
     rows = heads * 2 * count + (2 * cap if kv else 0)
     table = pl.BlockSpec((1, tables[0].shape[1]), lambda y: (0, 0))
-    wide = pl.BlockSpec((units, heads * HEAD_DIM), lambda y: (0, y))
-    thin = pl.BlockSpec((units, HEAD_DIM), lambda y: (0, y))
+    wide = pl.BlockSpec((units, each * heads * HEAD_DIM), lambda y: (0, y))
+    thin = pl.BlockSpec((units, each * HEAD_DIM), lambda y: (0, y))
     tall = n_grp * 2 * QUAD
     scratch = [
         pltpu.VMEM((count // QUAD, tall, 2 * units), bf16),
@@ -318,11 +321,11 @@
     if kv:
         scratch.append(pltpu.VMEM((n_grp * 2 * cap, 2 * units), bf16))
     return pl.pallas_call(
-        functools.partial(pack_kernel, begin, count, cap, count if kv else 0),
+        functools.partial(pack_kernel, begin, count, cap, count if kv else 0, heads),
         out_shape=jax.ShapeDtypeStruct((n_grp, n_y, rows, HEAD_DIM), bf16),
-        grid=(n_y,),
+        grid=(n_y // each,),
         in_specs=[table] * 3 + [wide] * 2 + [thin] * len(kv),
-        out_specs=pl.BlockSpec((n_grp, 1, rows, HEAD_DIM), lambda y: (0, y, 0, 0)),
+        out_specs=pl.BlockSpec((n_grp, each, rows, HEAD_DIM), lambda y: (0, y, 0, 0)),
         scratch_shapes=scratch,
         compiler_params=pltpu.CompilerParams(vmem_limit_bytes=60 * 2**20),
         cost_estimate=pl.CostEstimate(flops=2 * 10**9, bytes_accessed=6 * 2**20, transcendentals=0),
@@ -408,14 +411,17 @@
         taken = early[:, :, at + first_row:at + first_row + rows]
         return taken.transpose(2, 1, 0, 3).reshape(rows, n_y * n_grp, HEAD_DIM)
 
-    own = keys_of(0, 2 * split)
-    left, right = step(own, 1), step(own, -1)
-    near = (own, right, left, step(left[:split], 1), step(right[split:], -1))
-    far = lax.all_gather(keys_of(2 * split, 2 * (cap - split)), "x", axis=0)
+    def gather(own):
+        return (own, step(own, -1), step(own, 2), step(own, 1))
+
+    near = gather(keys_of(0, 2 * split))
+    other, _, _ = lax.optimization_barrier((keys_of(2 * split, 2 * (cap - split)), near[1], near[3]))
+    far = gather(other)
 
     first = first_blocks(doc_lengths, doc_groups, doc_offsets, cap)
     my_x = lax.axis_index("x").astype(jnp.int32).reshape(1)
     dq_early, k_sums, v_sums = attention(first, my_x, early, near, 0, split)
+    dq_early, *far = lax.optimization_barrier((dq_early, *far))
     dq_late, *grads = attention(first, my_x, late, near, split, cap - split, far, (k_sums, v_sums))
     dk, dv = grads[:n_x], grads[n_x:]
 

time: 241 us -> 225 us (0.934); the launches traced: 237 us -> 225 us
  waiting for transfers between devices: 111 us -> 97.2 us
  between operations: 14.4 us -> 1.03 us
  Pallas kernels: 34.3 us -> 43.2 us
  starting transfers between devices: 73.3 us -> 81.1 us
    pallas_call x2, Pallas kernels: 15 us -> 29.6 us  [attention(): pl.pallas_call(functools.partial(attention_kernel, begin, count, cap, ear...]
    pallas_call x2, Pallas kernels: 15.8 us -> 10.1 us  [pack(): pl.pallas_call(functools.partial(pack_kernel, begin, count, cap, count if...]
    ppermute x10 -> x12, starting transfers between devices: 31.9 us -> 37.5 us  [step(): return lax.ppermute(array, 'x', [(i, (i + by) % n_x) for i in range(n_x)])]
    all_to_all x1, waiting for transfers between devices: 12.3 us -> 7.21 us  [on_device(): dq_early = lax.all_to_all(dq_early, 'y', 0, 0, tiled=True)]
    ppermute x10 -> x12, waiting for transfers between devices: 29.2 us -> 24.2 us  [step(): return lax.ppermute(array, 'x', [(i, (i + by) % n_x) for i in range(n_x)])]
    all_to_all x2, waiting for transfers between devices: 50.3 us -> 47 us  [exchange(): lax.all_to_all(message.reshape(n_grp * n_y, rows, HEAD_DIM), ('grp', 'y')...]
  transfers between devices with their start and end apart: 16 -> 17, of which waited for: 12 -> 9; matrix products, arithmetic and copies ran while one was open for 1% -> 1% of each run, Pallas kernels for 11% -> 16%
where the time goes in v5:
time: 225 us
  waiting for transfers between devices  97.2 us (43%)
  starting transfers between devices  81.1 us (36%)
  Pallas kernels  43.2 us (19%)
    all_to_all x2, waiting for transfers between devices, exchange(): lax.all_to_all(message.reshape(n_grp * n_y, rows, HEAD_DIM), ('grp', 'y')...  47 us
    ppermute x12, starting transfers between devices, step(): return lax.ppermute(array, 'x', [(i, (i + by) % n_x) for i in range(n_x)])  37.5 us
    pallas_call x2, Pallas kernels, attention(): pl.pallas_call(functools.partial(attention_kernel, begin, count, cap, ear...  29.6 us
    all_to_all x2, starting transfers between devices, exchange(): lax.all_to_all(message.reshape(n_grp * n_y, rows, HEAD_DIM), ('grp', 'y')...  26.1 us
    ppermute x12, waiting for transfers between devices, step(): return lax.ppermute(array, 'x', [(i, (i + by) % n_x) for i in range(n_x)])  24.2 us
    all_to_all x1, waiting for transfers between devices, on_device(): sums = lax.all_to_all(sums, 'y', 0, 0, tiled=True)  18.7 us
    pallas_call x2, Pallas kernels, pack(): pl.pallas_call(functools.partial(pack_kernel, begin, count, cap, count if...  10.1 us
    all_to_all x1, waiting for transfers between devices, on_device(): dq_early = lax.all_to_all(dq_early, 'y', 0, 0, tiled=True)  7.21 us
  transfers between devices with their start and end apart: 17, of which 9 were waited for; matrix products, arithmetic and copies ran while one was open for 1% of the time, Pallas kernels for 16%

profile of v5, /device:TPU:6, one launch (start us, length us, event | category | flops | bytes accessed | tf_op | source)
XLA Modules:
  0.0 225.1 jit_solution(4224858203368600254)
XLA Ops:
  0.6 5.1 %pack.2 = bf16[16,8,64,128]{3,2,1,0:T(8,128)(2,1)} custom-call(s32[1,192]{1,0:T(1,128)} %bitcast.40, s32[1,192]{1,0:T(1,128)} %bitcast.38, s32[1,192]{1,0:T(1,128)} %bitcast.36, bf16[128,4096]{1,0:T(8,128)(2,1)} %bitcast.42, bf16[128,4096]{1,0:T(8,128)(2,1)} %bitcast.44, bf16[128,1024]{1,0:T(8,128)(2,1)} %bitcast.48, bf16[128,1024]{1,0:T(8,128)(2,1)} %bitcast.49), custom_call_target="tpu_custom_call" | custom-call | flops 2000000000 | bytes 6291456 | tf_op jit(solution)/shard_map/pack/pallas_call | solution.py:323
  5.7 17.8 %all-to-all-start = ((bf16[128,64,128]{2,1,0:T(8,128)(2,1)}), bf16[128,64,128]{2,1,0:T(8,128)(2,1)S(1)}, u32[]{:S(2)}, u32[]{:S(2)}) async-start(bf16[128,64,128]{2,1,0:T(8,128)(2,1)} %bitcast.24), calls=%async_computation | async-start | bytes 4194304 | tf_op jit(solution)/shard_map/all_to_all | solution.py:402
  23.5 5.1 %pack.3 = bf16[16,8,56,128]{3,2,1,0:T(8,128)(2,1)} custom-call(s32[1,192]{1,0:T(1,128)} %bitcast.41, s32[1,192]{1,0:T(1,128)} %bitcast.39, s32[1,192]{1,0:T(1,128)} %bitcast.37, bf16[128,4096]{1,0:T(8,128)(2,1)} %bitcast.43, bf16[128,4096]{1,0:T(8,128)(2,1)} %bitcast.45), custom_call_target="tpu_custom_call" | custom-call | flops 2000000000 | bytes 6291456 | tf_op jit(solution)/shard_map/pack/pallas_call | solution.py:323
  28.6 47.0 %all-to-all-done = bf16[128,64,128]{2,1,0:T(8,128)(2,1)S(1)} async-done(((bf16[128,64,128]{2,1,0:T(8,128)(2,1)}), bf16[128,64,128]{2,1,0:T(8,128)(2,1)S(1)}, u32[]{:S(2)}, u32[]{:S(2)}) %all-to-all-start) | async-done | bytes 2097184 | tf_op jit(solution)/shard_map/all_to_all | solution.py:402
  75.6 8.3 %all-to-all-start.2 = ((bf16[128,56,128]{2,1,0:T(8,128)(2,1)}), bf16[128,56,128]{2,1,0:T(8,128)(2,1)}, u32[]{:S(2)}, u32[]{:S(2)}) async-start(bf16[128,56,128]{2,1,0:T(8,128)(2,1)} %bitcast.25), calls=%async_computation.2 | async-start | bytes 3670016 | tf_op jit(solution)/shard_map/all_to_all | solution.py:402
  84.0 0.0 copy-done.8
  84.0 0.0 copy-done.7
  84.0 0.0 copy-done.9
  84.0 0.1 slice_bitcast_fusion.1
  84.1 0.2 copy.12
  84.3 0.0 copy-start.6
  84.3 2.7 %collective-permute-start = (bf16[10,128,128]{2,1,0:T(8,128)(2,1)S(1)}, bf16[10,128,128]{2,1,0:T(8,128)(2,1)S(1)}, u32[]{:S(2)}, u32[]{:S(2)}) collective-permute-start(bf16[10,128,128]{2,1,0:T(8,128)(2,1)S(1)} %bitcast.31), channel_id=1, source_target_pairs={{0,24},{8,0},{16,8},{24,16},{1,25},{9,1},{17,9},{25,17},{2,26},{10... | collective-permute-start | bytes 983048 | tf_op jit(solution)/shard_map/ppermute | solution.py:388
  87.1 4.3 %collective-permute-start.2 = (bf16[10,128,128]{2,1,0:T(8,128)(2,1)S(1)}, bf16[10,128,128]{2,1,0:T(8,128)(2,1)S(1)}, u32[]{:S(2)}, u32[]{:S(2)}) collective-permute-start(bf16[10,128,128]{2,1,0:T(8,128)(2,1)S(1)} %bitcast.32), channel_id=1, source_target_pairs={{0,8},{8,16},{16,24},{24,0},{1,9},{9,17},{17,25},{25,1},{2,10},{10... | collective-permute-start | bytes 983048 | tf_op jit(solution)/shard_map/ppermute | solution.py:388
  91.4 0.1 select_reduce_fusion
  91.5 2.1 collective-permute-start.1
  93.6 0.0 copy-done.2
  93.6 0.2 slice_bitcast_fusion
  93.9 0.3 copy.13
  94.2 0.0 copy-start.3
  94.2 9.5 %collective-permute-done.refs_4_ = bf16[10,128,128]{2,1,0:T(8,128)(2,1)S(1)} collective-permute-done((bf16[10,128,128]{2,1,0:T(8,128)(2,1)S(1)}, bf16[10,128,128]{2,1,0:T(8,128)(2,1)S(1)}, u32[]{:S(2)}, u32[]{:S(2)}) %collective-permute-start) | collective-permute-done | bytes 327712 | tf_op jit(solution)/shard_map/ppermute | solution.py:388
  103.6 1.2 collective-permute-done.2.refs_6_
  104.9 1.9 collective-permute-start.3
  106.8 7.0 %collective-permute-start.4 = (bf16[14,128,128]{2,1,0:T(8,128)(2,1)S(1)}, bf16[14,128,128]{2,1,0:T(8,128)(2,1)S(1)}, u32[]{:S(2)}, u32[]{:S(2)}) collective-permute-start(bf16[14,128,128]{2,1,0:T(8,128)(2,1)S(1)} %bitcast.28), channel_id=1, source_target_pairs={{0,16},{8,24},{16,0},{24,8},{1,17},{9,25},{17,1},{25,9},{2,18},{10... | collective-permute-start | bytes 1376264 | tf_op jit(solution)/shard_map/ppermute | solution.py:388
  113.8 1.9 collective-permute-start.5
  115.7 0.6 broadcast_add_fusion.1.refs_0_
  116.3 0.0 collective-permute-done.1.refs_5_
  116.3 0.0 copy-done.6
  116.3 0.0 copy-done.14
  116.3 0.0 copy-done.15
  116.3 0.7 copy-done.16
  117.0 22.2 %attention.2 = (bf16[8,80,512]{2,1,0:T(8,128)(2,1)}, f32[4,5,128,128]{3,2,1,0:T(8,128)}, f32[4,5,128,128]{3,2,1,0:T(8,128)}) custom-call(s32[12]{0:T(128)} %broadcast_add_fusion.1.refs_0_, s32[1]{0:T(128)} %bitcast.refs_1_, bf16[16,8,64,128]{3,2,1,0:T(8,128)(2,1)} %bitcast.23, bf16[10,128,128]{2,1,0:T(8,128)(2,1)} %bitcast.34, ...), custom_call_target="tpu_custom_call" | custom-call | flops 3355443200 | bytes 8388608 | tf_op jit(solution)/shard_map/attention/pallas_call | solution.py:233
  139.2 0.0 collective-permute-done.3.refs_8_
  139.2 0.0 copy-start.10
  139.3 0.0 collective-permute-done.4.refs_9_
  139.3 0.0 collective-permute-done.5.refs_10_
  139.3 0.0 all-to-all-done.2
  139.3 6.9 %all-to-all-start.1 = ((bf16[8,80,512]{2,1,0:T(8,128)(2,1)}), bf16[8,80,512]{2,1,0:T(8,128)(2,1)S(1)}, u32[]{:S(2)}, u32[]{:S(2)}) async-start(bf16[8,80,512]{2,1,0:T(8,128)(2,1)} %get-tuple-element.25), calls=%async_computation.1 | async-start | bytes 1310720 | tf_op jit(solution)/shard_map/all_to_all | solution.py:428
  146.2 0.0 copy-done.11
  146.2 0.0 copy-done.12
  146.2 7.4 %attention.3 = (bf16[8,112,512]{2,1,0:T(8,128)(2,1)}, bf16[8,192,128]{2,1,0:T(8,128)(2,1)}, bf16[8,192,128]{2,1,0:T(8,128)(2,1)}, bf16[8,192,128]{2,1,0:T(8,128)...) custom-call(s32[12]{0:T(128)} %broadcast_add_fusion.1.refs_0_, ...), custom_call_target="tpu_custom_call" | custom-call | flops 4697620480 | bytes 8388608 | tf_op jit(solution)/shard_map/attention/pallas_call | solution.py:233
  153.6 0.0 copy-start.5
  153.7 7.2 %all-to-all-done.1.refs_0_ = bf16[8,80,512]{2,1,0:T(8,128)(2,1)S(1)} async-done(((bf16[8,80,512]{2,1,0:T(8,128)(2,1)}), bf16[8,80,512]{2,1,0:T(8,128)(2,1)S(1)}, u32[]{:S(2)}, u32[]{:S(2)}) %all-to-all-start.1) | async-done | bytes 655392 | tf_op jit(solution)/shard_map/all_to_all | solution.py:428
  160.9 3.7 %all-to-all-start.3 = ((bf16[8,112,512]{2,1,0:T(8,128)(2,1)}), bf16[8,112,512]{2,1,0:T(8,128)(2,1)S(1)}, u32[]{:S(2)}, u32[]{:S(2)}) async-start(bf16[8,112,512]{2,1,0:T(8,128)(2,1)} %get-tuple-element.32), calls=%async_computation.3 | async-start | bytes 1835008 | tf_op jit(solution)/shard_map/all_to_all | solution.py:429
  164.6 2.5 %collective-permute-start.6 = (bf16[8,192,128]{2,1,0:T(8,128)(2,1)}, bf16[8,192,128]{2,1,0:T(8,128)(2,1)S(1)}, u32[]{:S(2)}, u32[]{:S(2)}) collective-permute-start(bf16[8,192,128]{2,1,0:T(8,128)(2,1)} %get-tuple-element.35), channel_id=1, source_target_pairs={{0,8},{8,16},{16,24},{24,0},{1,9},{9,17},{17,25},{25,1},{2,10},{10... | collective-permute-start | bytes 1179656 | tf_op jit(solution)/shard_map/ppermute | solution.py:388
  167.0 3.4 %collective-permute-start.10 = (bf16[8,192,128]{2,1,0:T(8,128)(2,1)}, bf16[8,192,128]{2,1,0:T(8,128)(2,1)S(1)}, u32[]{:S(2)}, u32[]{:S(2)}) collective-permute-start(bf16[8,192,128]{2,1,0:T(8,128)(2,1)} %get-tuple-element.40), channel_id=1, source_target_pairs={{0,24},{8,0},{16,8},{24,16},{1,25},{9,1},{17,9},{25,17},{2,26},{10... | collective-permute-start | bytes 1179656 | tf_op jit(solution)/shard_map/ppermute | solution.py:388
  170.4 3.9 %collective-permute-start.8 = (bf16[8,192,128]{2,1,0:T(8,128)(2,1)}, bf16[8,192,128]{2,1,0:T(8,128)(2,1)S(1)}, u32[]{:S(2)}, u32[]{:S(2)}) collective-permute-start(bf16[8,192,128]{2,1,0:T(8,128)(2,1)} %get-tuple-element.36), channel_id=1, source_target_pairs={{0,24},{8,0},{16,8},{24,16},{1,25},{9,1},{17,9},{25,17},{2,26},{10... | collective-permute-start | bytes 1179656 | tf_op jit(solution)/shard_map/ppermute | solution.py:388
  174.3 0.0 copy-done.13
  174.4 3.1 %collective-permute-start.9 = (bf16[8,192,128]{2,1,0:T(8,128)(2,1)S(1)}, bf16[8,192,128]{2,1,0:T(8,128)(2,1)S(1)}, u32[]{:S(2)}, u32[]{:S(2)}) collective-permute-start(bf16[8,192,128]{2,1,0:T(8,128)(2,1)S(1)} %copy-done.13), channel_id=1, source_target_pairs={{0,8},{8,16},{16,24},{24,0},{1,9},{9,17},{17,25},{25,1},{2,10},{10... | collective-permute-start | bytes 1179656 | tf_op jit(solution)/shard_map/ppermute | solution.py:388
  177.5 0.0 collective-permute-done.6
  177.5 0.1 add_convert_fusion.1
  177.6 2.5 %collective-permute-start.7 = (bf16[8,192,128]{2,1,0:T(8,128)(2,1)S(1)}, bf16[8,192,128]{2,1,0:T(8,128)(2,1)S(1)}, u32[]{:S(2)}, u32[]{:S(2)}) collective-permute-start(bf16[8,192,128]{2,1,0:T(8,128)(2,1)S(1)} %add_convert_fusion.1), channel_id=1, source_target_pairs={{0,8},{8,16},{16,24},{24,0},{1,9},{9,17},{17,25},{25,1},{2,10},{10... | collective-permute-start | bytes 1179656 | tf_op jit(solution)/shard_map/ppermute | solution.py:388
  180.1 2.3 %collective-permute-done.10 = bf16[8,192,128]{2,1,0:T(8,128)(2,1)S(1)} collective-permute-done((bf16[8,192,128]{2,1,0:T(8,128)(2,1)}, bf16[8,192,128]{2,1,0:T(8,128)(2,1)S(1)}, u32[]{:S(2)}, u32[]{:S(2)}) %collective-permute-start.10) | collective-permute-done | bytes 393248 | tf_op jit(solution)/shard_map/ppermute | solution.py:388
  182.4 0.1 add_convert_fusion
  182.5 2.2 collective-permute-start.11
  184.7 6.1 %collective-permute-done.8.refs_2_ = bf16[8,192,128]{2,1,0:T(8,128)(2,1)S(1)} collective-permute-done((bf16[8,192,128]{2,1,0:T(8,128)(2,1)}, bf16[8,192,128]{2,1,0:T(8,128)(2,1)S(1)}, u32[]{:S(2)}, u32[]{:S(2)}) %collective-permute-start.8) | collective-permute-done | bytes 393248 | tf_op jit(solution)/shard_map/ppermute | solution.py:388
  190.8 0.0 collective-permute-done.9.refs_4_
  190.8 1.8 collective-permute-done.7.refs_1_
  192.6 3.3 %collective-permute-done.11.refs_5_ = bf16[8,192,128]{2,1,0:T(8,128)(2,1)S(1)} collective-permute-done((bf16[8,192,128]{2,1,0:T(8,128)(2,1)S(1)}, bf16[8,192,128]{2,1,0:T(8,128)(2,1)S(1)}, u32[]{:S(2)}, u32[]{:S(2)}) %collective-permute-start.11) | collective-permute-done | bytes 393248 | tf_op jit(solution)/shard_map/ppermute | solution.py:388
  196.0 1.2 add_up.1
  197.1 0.0 all-to-all-done.3.refs_1_
  197.1 6.9 %all-to-all-start.4 = ((bf16[8,384,128]{2,1,0:T(8,128)(2,1)}), bf16[8,384,128]{2,1,0:T(8,128)(2,1)S(1)}, u32[]{:S(2)}, u32[]{:S(2)}) async-start(bf16[8,384,128]{2,1,0:T(8,128)(2,1)} %add_up.1), calls=%async_computation.4 | async-start | bytes 1572864 | tf_op jit(solution)/shard_map/all_to_all | solution.py:438
  204.1 1.2 lay_out.2
  205.3 18.7 %all-to-all-done.4.refs_0_ = bf16[8,384,128]{2,1,0:T(8,128)(2,1)S(1)} async-done(((bf16[8,384,128]{2,1,0:T(8,128)(2,1)}), bf16[8,384,128]{2,1,0:T(8,128)(2,1)S(1)}, u32[]{:S(2)}, u32[]{:S(2)}) %all-to-all-start.4) | async-done | bytes 786464 | tf_op jit(solution)/shard_map/all_to_all | solution.py:438
  224.0 1.1 lay_out.3
  (21 shorter events, 0.0 us)
Async XLA Ops:
  5.7 69.9 %all-to-all-start = ((bf16[128,64,128]{2,1,0:T(8,128)(2,1)}), bf16[128,64,128]{2,1,0:T(8,128)(2,1)S(1)}, u32[]{:S(2)}, u32[]{:S(2)}) async-start(bf16[128,64,128]{2,1,0:T(8,128)(2,1)} %bitcast.24), calls=%async_computation | async-start | bytes 4194304 | tf_op jit(solution)/shard_map/all_to_all | solution.py:402
  75.6 18.0 %copy-start.2 = (bf16[128,64,128]{2,1,0:T(8,128)(2,1)}, bf16[128,64,128]{2,1,0:T(8,128)(2,1)S(1)}, u32[]{:S(2)}) copy-start(bf16[128,64,128]{2,1,0:T(8,128)(2,1)S(1)} %all-to-all-done) | copy-start | bytes 6291460
  75.6 8.4 %copy-start.8 = (s32[192]{0:T(256)S(1)}, s32[192]{0:T(256)}, u32[]{:S(2)}) copy-start(s32[192]{0:T(256)} %param.12) | copy-start | bytes 2308
  75.6 8.4 %copy-start.7 = (s32[192]{0:T(256)S(1)}, s32[192]{0:T(256)}, u32[]{:S(2)}) copy-start(s32[192]{0:T(256)} %param.13) | copy-start | bytes 2308
  75.6 8.4 %copy-start.9 = (s32[192]{0:T(256)S(1)}, s32[192]{0:T(256)}, u32[]{:S(2)}) copy-start(s32[192]{0:T(256)} %param.11) | copy-start | bytes 2308
  75.6 63.7 %all-to-all-start.2 = ((bf16[128,56,128]{2,1,0:T(8,128)(2,1)}), bf16[128,56,128]{2,1,0:T(8,128)(2,1)}, u32[]{:S(2)}, u32[]{:S(2)}) async-start(bf16[128,56,128]{2,1,0:T(8,128)(2,1)} %bitcast.25), calls=%async_computation.2 | async-start | bytes 3670016 | tf_op jit(solution)/shard_map/all_to_all | solution.py:402
  84.3 32.0 %copy-start.6 = (bf16[10,8,16,128]{3,2,1,0:T(8,128)(2,1)}, bf16[10,8,16,128]{3,2,1,0:T(8,128)(2,1)S(1)}, u32[]{:S(2)}) copy-start(bf16[10,8,16,128]{3,2,1,0:T(8,128)(2,1)S(1)} %copy.12) | copy-start | bytes 983044
  84.3 19.3 %collective-permute-start = (bf16[10,128,128]{2,1,0:T(8,128)(2,1)S(1)}, bf16[10,128,128]{2,1,0:T(8,128)(2,1)S(1)}, u32[]{:S(2)}, u32[]{:S(2)}) collective-permute-start(bf16[10,128,128]{2,1,0:T(8,128)(2,1)S(1)} %bitcast.31), channel_id=1, source_target_pairs={{0,24},{8,0},{16,8},{24,16},{1,25},{9,1},{17,9},{25,17},{2,26},{10... | collective-permute-start | bytes 983048 | tf_op jit(solution)/shard_map/ppermute | solution.py:388
  87.1 17.8 %collective-permute-start.2 = (bf16[10,128,128]{2,1,0:T(8,128)(2,1)S(1)}, bf16[10,128,128]{2,1,0:T(8,128)(2,1)S(1)}, u32[]{:S(2)}, u32[]{:S(2)}) collective-permute-start(bf16[10,128,128]{2,1,0:T(8,128)(2,1)S(1)} %bitcast.32), channel_id=1, source_target_pairs={{0,8},{8,16},{16,24},{24,0},{1,9},{9,17},{17,25},{25,1},{2,10},{10... | collective-permute-start | bytes 983048 | tf_op jit(solution)/shard_map/ppermute | solution.py:388
  91.5 24.8 %collective-permute-start.1 = (bf16[10,128,128]{2,1,0:T(8,128)(2,1)S(1)}, bf16[10,128,128]{2,1,0:T(8,128)(2,1)S(1)}, u32[]{:S(2)}, u32[]{:S(2)}) collective-permute-start(bf16[10,128,128]{2,1,0:T(8,128)(2,1)S(1)} %bitcast.33), channel_id=1, source_target_pairs={{0,16},{8,24},{16,0},{24,8},{1,17},{9,25},{17,1},{25,9},{2,18},{10... | collective-permute-start | bytes 983048 | tf_op jit(solution)/shard_map/ppermute | solution.py:388
  94.2 45.1 %copy-start.3 = (bf16[14,8,16,128]{3,2,1,0:T(8,128)(2,1)}, bf16[14,8,16,128]{3,2,1,0:T(8,128)(2,1)S(1)}, u32[]{:S(2)}) copy-start(bf16[14,8,16,128]{3,2,1,0:T(8,128)(2,1)S(1)} %copy.13) | copy-start | bytes 1376260
  103.6 12.7 %copy-start.14 = (bf16[10,128,128]{2,1,0:T(8,128)(2,1)}, bf16[10,128,128]{2,1,0:T(8,128)(2,1)S(1)}, u32[]{:S(2)}) copy-start(bf16[10,128,128]{2,1,0:T(8,128)(2,1)S(1)} %collective-permute-done.refs_4_) | copy-start | bytes 983044
  104.9 11.5 %copy-start.15 = (bf16[10,128,128]{2,1,0:T(8,128)(2,1)}, bf16[10,128,128]{2,1,0:T(8,128)(2,1)S(1)}, u32[]{:S(2)}) copy-start(bf16[10,128,128]{2,1,0:T(8,128)(2,1)S(1)} %collective-permute-done.2.refs_6_) | copy-start | bytes 983044
  104.9 34.4 %collective-permute-start.3 = (bf16[14,128,128]{2,1,0:T(8,128)(2,1)S(1)}, bf16[14,128,128]{2,1,0:T(8,128)(2,1)S(1)}, u32[]{:S(2)}, u32[]{:S(2)}) collective-permute-start(bf16[14,128,128]{2,1,0:T(8,128)(2,1)S(1)} %bitcast.27), channel_id=1, source_target_pairs={{0,24},{8,0},{16,8},{24,16},{1,25},{9,1},{17,9},{25,17},{2,26},{10... | collective-permute-start | bytes 1376264 | tf_op jit(solution)/shard_map/ppermute | solution.py:388
  106.8 32.5 %collective-permute-start.4 = (bf16[14,128,128]{2,1,0:T(8,128)(2,1)S(1)}, bf16[14,128,128]{2,1,0:T(8,128)(2,1)S(1)}, u32[]{:S(2)}, u32[]{:S(2)}) collective-permute-start(bf16[14,128,128]{2,1,0:T(8,128)(2,1)S(1)} %bitcast.28), channel_id=1, source_target_pairs={{0,16},{8,24},{16,0},{24,8},{1,17},{9,25},{17,1},{25,9},{2,18},{10... | collective-permute-start | bytes 1376264 | tf_op jit(solution)/shard_map/ppermute | solution.py:388
  113.8 25.5 %collective-permute-start.5 = (bf16[14,128,128]{2,1,0:T(8,128)(2,1)S(1)}, bf16[14,128,128]{2,1,0:T(8,128)(2,1)S(1)}, u32[]{:S(2)}, u32[]{:S(2)}) collective-permute-start(bf16[14,128,128]{2,1,0:T(8,128)(2,1)S(1)} %bitcast.29), channel_id=1, source_target_pairs={{0,8},{8,16},{16,24},{24,0},{1,9},{9,17},{17,25},{25,1},{2,10},{10... | collective-permute-start | bytes 1376264 | tf_op jit(solution)/shard_map/ppermute | solution.py:388
  116.3 0.7 copy-start.16
  139.2 6.9 %copy-start.10 = (bf16[14,128,128]{2,1,0:T(8,128)(2,1)}, bf16[14,128,128]{2,1,0:T(8,128)(2,1)S(1)}, u32[]{:S(2)}) copy-start(bf16[14,128,128]{2,1,0:T(8,128)(2,1)S(1)} %collective-permute-done.3.refs_8_) | copy-start | bytes 1376260
  139.3 6.9 %copy-start.11 = (bf16[14,128,128]{2,1,0:T(8,128)(2,1)}, bf16[14,128,128]{2,1,0:T(8,128)(2,1)S(1)}, u32[]{:S(2)}) copy-start(bf16[14,128,128]{2,1,0:T(8,128)(2,1)S(1)} %collective-permute-done.4.refs_9_) | copy-start | bytes 1376260
  139.3 6.9 %copy-start.12 = (bf16[14,128,128]{2,1,0:T(8,128)(2,1)}, bf16[14,128,128]{2,1,0:T(8,128)(2,1)S(1)}, u32[]{:S(2)}) copy-start(bf16[14,128,128]{2,1,0:T(8,128)(2,1)S(1)} %collective-permute-done.5.refs_10_) | copy-start | bytes 1376260
  139.3 21.6 %all-to-all-start.1 = ((bf16[8,80,512]{2,1,0:T(8,128)(2,1)}), bf16[8,80,512]{2,1,0:T(8,128)(2,1)S(1)}, u32[]{:S(2)}, u32[]{:S(2)}) async-start(bf16[8,80,512]{2,1,0:T(8,128)(2,1)} %get-tuple-element.25), calls=%async_computation.1 | async-start | bytes 1310720 | tf_op jit(solution)/shard_map/all_to_all | solution.py:428
  153.6 20.7 %copy-start.13 = (bf16[8,192,128]{2,1,0:T(8,128)(2,1)S(1)}, bf16[8,192,128]{2,1,0:T(8,128)(2,1)}, u32[]{:S(2)}) copy-start(bf16[8,192,128]{2,1,0:T(8,128)(2,1)} %get-tuple-element.38) | copy-start | bytes 1179652
  153.6 23.9 %copy-start.5 = (bf16[8,192,128]{2,1,0:T(8,128)(2,1)S(1)}, bf16[8,192,128]{2,1,0:T(8,128)(2,1)}, u32[]{:S(2)}) copy-start(bf16[8,192,128]{2,1,0:T(8,128)(2,1)} %get-tuple-element.34) | copy-start | bytes 1179652
  153.6 28.8 %copy-start.4 = (bf16[8,192,128]{2,1,0:T(8,128)(2,1)S(1)}, bf16[8,192,128]{2,1,0:T(8,128)(2,1)}, u32[]{:S(2)}) copy-start(bf16[8,192,128]{2,1,0:T(8,128)(2,1)} %get-tuple-element.39) | copy-start | bytes 1179652
  160.9 35.1 %copy-start = (bf16[8,192,128]{2,1,0:T(8,128)(2,1)S(1)}, bf16[8,192,128]{2,1,0:T(8,128)(2,1)}, u32[]{:S(2)}) copy-start(bf16[8,192,128]{2,1,0:T(8,128)(2,1)} %get-tuple-element.33.refs_0_) | copy-start | bytes 1179652
  160.9 35.1 %copy-start.1 = (bf16[8,192,128]{2,1,0:T(8,128)(2,1)S(1)}, bf16[8,192,128]{2,1,0:T(8,128)(2,1)}, u32[]{:S(2)}) copy-start(bf16[8,192,128]{2,1,0:T(8,128)(2,1)} %get-tuple-element.37.refs_3_) | copy-start | bytes 1179652
  160.9 36.3 %all-to-all-start.3 = ((bf16[8,112,512]{2,1,0:T(8,128)(2,1)}), bf16[8,112,512]{2,1,0:T(8,128)(2,1)S(1)}, u32[]{:S(2)}, u32[]{:S(2)}) async-start(bf16[8,112,512]{2,1,0:T(8,128)(2,1)} %get-tuple-element.32), calls=%async_computation.3 | async-start | bytes 1835008 | tf_op jit(solution)/shard_map/all_to_all | solution.py:429
  164.6 12.9 %collective-permute-start.6 = (bf16[8,192,128]{2,1,0:T(8,128)(2,1)}, bf16[8,192,128]{2,1,0:T(8,128)(2,1)S(1)}, u32[]{:S(2)}, u32[]{:S(2)}) collective-permute-start(bf16[8,192,128]{2,1,0:T(8,128)(2,1)} %get-tuple-element.35), channel_id=1, source_target_pairs={{0,8},{8,16},{16,24},{24,0},{1,9},{9,17},{17,25},{25,1},{2,10},{10... | collective-permute-start | bytes 1179656 | tf_op jit(solution)/shard_map/ppermute | solution.py:388
  167.0 15.4 %collective-permute-start.10 = (bf16[8,192,128]{2,1,0:T(8,128)(2,1)}, bf16[8,192,128]{2,1,0:T(8,128)(2,1)S(1)}, u32[]{:S(2)}, u32[]{:S(2)}) collective-permute-start(bf16[8,192,128]{2,1,0:T(8,128)(2,1)} %get-tuple-element.40), channel_id=1, source_target_pairs={{0,24},{8,0},{16,8},{24,16},{1,25},{9,1},{17,9},{25,17},{2,26},{10... | collective-permute-start | bytes 1179656 | tf_op jit(solution)/shard_map/ppermute | solution.py:388
  170.4 20.4 %collective-permute-start.8 = (bf16[8,192,128]{2,1,0:T(8,128)(2,1)}, bf16[8,192,128]{2,1,0:T(8,128)(2,1)S(1)}, u32[]{:S(2)}, u32[]{:S(2)}) collective-permute-start(bf16[8,192,128]{2,1,0:T(8,128)(2,1)} %get-tuple-element.36), channel_id=1, source_target_pairs={{0,24},{8,0},{16,8},{24,16},{1,25},{9,1},{17,9},{25,17},{2,26},{10... | collective-permute-start | bytes 1179656 | tf_op jit(solution)/shard_map/ppermute | solution.py:388
  174.4 16.5 %collective-permute-start.9 = (bf16[8,192,128]{2,1,0:T(8,128)(2,1)S(1)}, bf16[8,192,128]{2,1,0:T(8,128)(2,1)S(1)}, u32[]{:S(2)}, u32[]{:S(2)}) collective-permute-start(bf16[8,192,128]{2,1,0:T(8,128)(2,1)S(1)} %copy-done.13), channel_id=1, source_target_pairs={{0,8},{8,16},{16,24},{24,0},{1,9},{9,17},{17,25},{25,1},{2,10},{10... | collective-permute-start | bytes 1179656 | tf_op jit(solution)/shard_map/ppermute | solution.py:388
  177.6 15.0 %collective-permute-start.7 = (bf16[8,192,128]{2,1,0:T(8,128)(2,1)S(1)}, bf16[8,192,128]{2,1,0:T(8,128)(2,1)S(1)}, u32[]{:S(2)}, u32[]{:S(2)}) collective-permute-start(bf16[8,192,128]{2,1,0:T(8,128)(2,1)S(1)} %add_convert_fusion.1), channel_id=1, source_target_pairs={{0,8},{8,16},{16,24},{24,0},{1,9},{9,17},{17,25},{25,1},{2,10},{10... | collective-permute-start | bytes 1179656 | tf_op jit(solution)/shard_map/ppermute | solution.py:388
  182.5 13.4 %collective-permute-start.11 = (bf16[8,192,128]{2,1,0:T(8,128)(2,1)S(1)}, bf16[8,192,128]{2,1,0:T(8,128)(2,1)S(1)}, u32[]{:S(2)}, u32[]{:S(2)}) collective-permute-start(bf16[8,192,128]{2,1,0:T(8,128)(2,1)S(1)} %add_convert_fusion), channel_id=1, source_target_pairs={{0,24},{8,0},{16,8},{24,16},{1,25},{9,1},{17,9},{25,17},{2,26},{10... | collective-permute-start | bytes 1179656 | tf_op jit(solution)/shard_map/ppermute | solution.py:388
  197.1 26.9 %all-to-all-start.4 = ((bf16[8,384,128]{2,1,0:T(8,128)(2,1)}), bf16[8,384,128]{2,1,0:T(8,128)(2,1)S(1)}, u32[]{:S(2)}, u32[]{:S(2)}) async-start(bf16[8,384,128]{2,1,0:T(8,128)(2,1)} %add_up.1), calls=%async_computation.4 | async-start | bytes 1572864 | tf_op jit(solution)/shard_map/all_to_all | solution.py:438

commit v6 on v5

--- a/solution.py
+++ b/solution.py
@@ -39,7 +39,7 @@
         queries, keys, values, s_keep, p_keep, q_acc, sem, k_acc, v_acc = refs
     else:
         dq_ref, k_acc, v_acc, queries, keys, values, s_keep, p_keep, q_acc, sem = refs[3 + n_x:]
-    groups, n_y, _, head_dim = in_ref.shape
+    n_y, groups, _, head_dim = in_ref.shape
     heads = n_x
     part = groups * n_y
     span = heads * part
@@ -72,7 +72,7 @@
     def sort_y(y, _):
         def turned(starts):
             taken = jnp.concatenate(
-                [in_ref[:, y, start:start + per, :].reshape(mixed, head_dim) for start in starts], axis=1)
+                [in_ref[y, :, start:start + per, :].reshape(mixed, head_dim) for start in starts], axis=1)
             out = dot(turn, taken, NN).astype(bf16)
             return [out[:, i * head_dim:(i + 1) * head_dim].reshape(per, groups, head_dim) for i in range(len(starts))]
 
@@ -199,7 +199,7 @@
 
 
 def attention(first, my_x, packed, near, begin, count, late=None, carry=()):
-    groups, n_y, _, head_dim = packed.shape
+    n_y, groups, _, head_dim = packed.shape
     n_x = HEADS // KV_HEADS
     cap = first.shape[0]
     early = near[0].shape[0] // 2
@@ -249,7 +249,7 @@
         k_ref, v_ref, out_ref, pick_quad, pick_one, pick_kv = refs[5:]
     else:
         out_ref, pick_quad, pick_one = refs[5:]
-    n_grp, _, _, head_dim = out_ref.shape
+    _, n_grp, _, head_dim = out_ref.shape
     units = q_ref.shape[0]
     per = 2 * QUAD
     quads, ones = count // QUAD, count % QUAD
@@ -294,16 +294,16 @@
             for h in range(heads):
                 at = (j * heads + h) * per
                 slab = moved[:, h * head_dim:(h + 1) * head_dim].reshape(n_grp, per, head_dim)
-                out_ref[:, y, at:at + per, :] = slab.astype(bf16)
+                out_ref[y, :, at:at + per, :] = slab.astype(bf16)
         if ones:
             tall = jnp.concatenate([both[:, h * head_dim:(h + 1) * head_dim] for h in range(heads)], axis=0)
         for i in range(ones):
             at = (quads * heads + i) * per
-            out_ref[:, y, at:at + per, :] = dot(pick_one[i], tall, NN).reshape(n_grp, per, head_dim).astype(bf16)
+            out_ref[y, :, at:at + per, :] = dot(pick_one[i], tall, NN).reshape(n_grp, per, head_dim).astype(bf16)
         if early:
             mine = slice(y * head_dim, (y + 1) * head_dim)
             both = dot(pick_kv[...], jnp.concatenate([k_ref[:, mine], v_ref[:, mine]], axis=0), NN)
-            out_ref[:, y, 2 * heads * count:, :] = both.reshape(n_grp, 2 * cap, head_dim).astype(bf16)
+            out_ref[y, :, 2 * heads * count:, :] = both.reshape(n_grp, 2 * cap, head_dim).astype(bf16)
 
 
 def pack(tables, q, g, kv, n_grp, n_y, begin, count, cap, each=AT_ONCE):
@@ -322,10 +322,10 @@
         scratch.append(pltpu.VMEM((n_grp * 2 * cap, 2 * units), bf16))
     return pl.pallas_call(
         functools.partial(pack_kernel, begin, count, cap, count if kv else 0, heads),
-        out_shape=jax.ShapeDtypeStruct((n_grp, n_y, rows, HEAD_DIM), bf16),
+        out_shape=jax.ShapeDtypeStruct((n_y, n_grp, rows, HEAD_DIM), bf16),
         grid=(n_y // each,),
         in_specs=[table] * 3 + [wide] * 2 + [thin] * len(kv),
-        out_specs=pl.BlockSpec((n_grp, each, rows, HEAD_DIM), lambda y: (0, y, 0, 0)),
+        out_specs=pl.BlockSpec((each, n_grp, rows, HEAD_DIM), lambda y: (y, 0, 0, 0)),
         scratch_shapes=scratch,
         compiler_params=pltpu.CompilerParams(vmem_limit_bytes=60 * 2**20),
         cost_estimate=pl.CostEstimate(flops=2 * 10**9, bytes_accessed=6 * 2**20, transcendentals=0),
@@ -399,8 +399,8 @@
 
     def exchange(message):
         rows = message.shape[2]
-        home = lax.all_to_all(message.reshape(n_grp * n_y, rows, HEAD_DIM), ("grp", "y"), 0, 0, tiled=True)
-        return home.reshape(n_grp, n_y, rows, HEAD_DIM)
+        home = lax.all_to_all(message.reshape(n_y * n_grp, rows, HEAD_DIM), ("y", "grp"), 0, 0, tiled=True)
+        return home.reshape(n_y, n_grp, rows, HEAD_DIM)
 
     early = exchange(pack(tables, q, g, (k, v), n_grp, n_y, 0, split, cap))
     late = exchange(pack(tables, q, g, (), n_grp, n_y, split, cap - split, cap))
@@ -409,14 +409,13 @@
 
     def keys_of(first_row, rows):
         taken = early[:, :, at + first_row:at + first_row + rows]
-        return taken.transpose(2, 1, 0, 3).reshape(rows, n_y * n_grp, HEAD_DIM)
+        return taken.transpose(2, 0, 1, 3).reshape(rows, n_y * n_grp, HEAD_DIM)
 
     def gather(own):
         return (own, step(own, -1), step(own, 2), step(own, 1))
 
     near = gather(keys_of(0, 2 * split))
-    other, _, _ = lax.optimization_barrier((keys_of(2 * split, 2 * (cap - split)), near[1], near[3]))
-    far = gather(other)
+    far = gather(keys_of(2 * split, 2 * (cap - split)))
 
     first = first_blocks(doc_lengths, doc_groups, doc_offsets, cap)
     my_x = lax.axis_index("x").astype(jnp.int32).reshape(1)

time: 225 us -> 227 us (level)
  the two profiles are of different devices: /device:TPU:6 before, /device:TPU:65 now
where the time goes in v6:
time: 227 us; the launch traced here: 224 us
  waiting for transfers between devices  83.4 us (37%)
  starting transfers between devices  82.5 us (36%)
  Pallas kernels  54.4 us (24%)
    all_to_all x2, waiting for transfers between devices, exchange(): lax.all_to_all(message.reshape(n_y * n_grp, rows, HEAD_DIM), ('y', 'grp')...  46.4 us
    pallas_call x2, Pallas kernels, attention(): pl.pallas_call(functools.partial(attention_kernel, begin, count, cap, ear...  40.9 us
    ppermute x12, starting transfers between devices, step(): return lax.ppermute(array, 'x', [(i, (i + by) % n_x) for i in range(n_x)])  36.6 us
    all_to_all x2, starting transfers between devices, exchange(): lax.all_to_all(message.reshape(n_y * n_grp, rows, HEAD_DIM), ('y', 'grp')...  26 us
    all_to_all x1, waiting for transfers between devices, on_device(): sums = lax.all_to_all(sums, 'y', 0, 0, tiled=True)  19.2 us
    ppermute x12, waiting for transfers between devices, step(): return lax.ppermute(array, 'x', [(i, (i + by) % n_x) for i in range(n_x)])  17.8 us
    pallas_call x2, Pallas kernels, pack(): pl.pallas_call(functools.partial(pack_kernel, begin, count, cap, count if...  10 us
    all_to_all x1, starting transfers between devices, on_device(): dq_late = lax.all_to_all(dq_late, 'y', 0, 0, tiled=True)  6.78 us
  transfers between devices with their start and end apart: 17, of which 8 were waited for; matrix products, arithmetic and copies ran while one was open for 1% of the time, Pallas kernels for 22%

profile of v6, /device:TPU:65, one launch (start us, length us, event | category | flops | bytes accessed | tf_op | source)
XLA Modules:
  0.0 223.5 jit_solution(4372360913077220317)
XLA Ops:
  0.6 5.0 %pack.2 = bf16[8,16,64,128]{3,2,1,0:T(8,128)(2,1)} custom-call(s32[1,192]{1,0:T(1,128)} %bitcast.40, s32[1,192]{1,0:T(1,128)} %bitcast.38, s32[1,192]{1,0:T(1,128)} %bitcast.36, bf16[128,4096]{1,0:T(8,128)(2,1)} %bitcast.42, bf16[128,4096]{1,0:T(8,128)(2,1)} %bitcast.44, bf16[128,1024]{1,0:T(8,128)(2,1)} %bitcast.48, bf16[128,1024]{1,0:T(8,128)(2,1)} %bitcast.49), custom_call_target="tpu_custom_call" | custom-call | flops 2000000000 | bytes 6291456 | tf_op jit(solution)/shard_map/pack/pallas_call | solution.py:323
  5.7 16.9 %all-to-all-start = ((bf16[128,64,128]{2,1,0:T(8,128)(2,1)}), bf16[128,64,128]{2,1,0:T(8,128)(2,1)S(1)}, u32[]{:S(2)}, u32[]{:S(2)}) async-start(bf16[128,64,128]{2,1,0:T(8,128)(2,1)} %bitcast.24), calls=%async_computation | async-start | bytes 4194304 | tf_op jit(solution)/shard_map/all_to_all | solution.py:402
  22.5 5.0 %pack.3 = bf16[8,16,56,128]{3,2,1,0:T(8,128)(2,1)} custom-call(s32[1,192]{1,0:T(1,128)} %bitcast.41, s32[1,192]{1,0:T(1,128)} %bitcast.39, s32[1,192]{1,0:T(1,128)} %bitcast.37, bf16[128,4096]{1,0:T(8,128)(2,1)} %bitcast.43, bf16[128,4096]{1,0:T(8,128)(2,1)} %bitcast.45), custom_call_target="tpu_custom_call" | custom-call | flops 2000000000 | bytes 6291456 | tf_op jit(solution)/shard_map/pack/pallas_call | solution.py:323
  27.5 46.4 %all-to-all-done = bf16[128,64,128]{2,1,0:T(8,128)(2,1)S(1)} async-done(((bf16[128,64,128]{2,1,0:T(8,128)(2,1)}), bf16[128,64,128]{2,1,0:T(8,128)(2,1)S(1)}, u32[]{:S(2)}, u32[]{:S(2)}) %all-to-all-start) | async-done | bytes 2097184 | tf_op jit(solution)/shard_map/all_to_all | solution.py:402
  73.9 9.1 %all-to-all-start.2 = ((bf16[128,56,128]{2,1,0:T(8,128)(2,1)}), bf16[128,56,128]{2,1,0:T(8,128)(2,1)}, u32[]{:S(2)}, u32[]{:S(2)}) async-start(bf16[128,56,128]{2,1,0:T(8,128)(2,1)} %bitcast.25), calls=%async_computation.2 | async-start | bytes 3670016 | tf_op jit(solution)/shard_map/all_to_all | solution.py:402
  83.0 0.0 copy-done.8
  83.1 0.0 copy-done.7
  83.1 0.0 copy-done.9
  83.1 0.1 slice_bitcast_fusion.1
  83.2 0.1 copy.12
  83.3 0.0 copy-start.6
  83.3 4.4 %collective-permute-start = (bf16[10,128,128]{2,1,0:T(8,128)(2,1)S(1)}, bf16[10,128,128]{2,1,0:T(8,128)(2,1)S(1)}, u32[]{:S(2)}, u32[]{:S(2)}) collective-permute-start(bf16[10,128,128]{2,1,0:T(8,128)(2,1)S(1)} %bitcast.31), channel_id=1, source_target_pairs={{0,24},{8,0},{16,8},{24,16},{1,25},{9,1},{17,9},{25,17},{2,26},{10... | collective-permute-start | bytes 983048 | tf_op jit(solution)/shard_map/ppermute | solution.py:388
  87.7 0.1 select_reduce_fusion
  87.8 2.4 %collective-permute-start.1 = (bf16[10,128,128]{2,1,0:T(8,128)(2,1)S(1)}, bf16[10,128,128]{2,1,0:T(8,128)(2,1)S(1)}, u32[]{:S(2)}, u32[]{:S(2)}) collective-permute-start(bf16[10,128,128]{2,1,0:T(8,128)(2,1)S(1)} %bitcast.32), channel_id=1, source_target_pairs={{0,16},{8,24},{16,0},{24,8},{1,17},{9,25},{17,1},{25,9},{2,18},{10... | collective-permute-start | bytes 983048 | tf_op jit(solution)/shard_map/ppermute | solution.py:388
  90.2 2.5 %collective-permute-start.2 = (bf16[10,128,128]{2,1,0:T(8,128)(2,1)S(1)}, bf16[10,128,128]{2,1,0:T(8,128)(2,1)S(1)}, u32[]{:S(2)}, u32[]{:S(2)}) collective-permute-start(bf16[10,128,128]{2,1,0:T(8,128)(2,1)S(1)} %bitcast.33), channel_id=1, source_target_pairs={{0,8},{8,16},{16,24},{24,0},{1,9},{9,17},{17,25},{25,1},{2,10},{10... | collective-permute-start | bytes 983048 | tf_op jit(solution)/shard_map/ppermute | solution.py:388
  92.8 0.0 copy-done.2
  92.8 0.2 slice_bitcast_fusion
  93.0 0.1 copy.13
  93.1 0.0 copy-start.3
  93.1 4.0 %collective-permute-start.3 = (bf16[14,128,128]{2,1,0:T(8,128)(2,1)S(1)}, bf16[14,128,128]{2,1,0:T(8,128)(2,1)S(1)}, u32[]{:S(2)}, u32[]{:S(2)}) collective-permute-start(bf16[14,128,128]{2,1,0:T(8,128)(2,1)S(1)} %bitcast.27), channel_id=1, source_target_pairs={{0,24},{8,0},{16,8},{24,16},{1,25},{9,1},{17,9},{25,17},{2,26},{10... | collective-permute-start | bytes 1376264 | tf_op jit(solution)/shard_map/ppermute | solution.py:388
  97.1 3.1 %collective-permute-start.4 = (bf16[14,128,128]{2,1,0:T(8,128)(2,1)S(1)}, bf16[14,128,128]{2,1,0:T(8,128)(2,1)S(1)}, u32[]{:S(2)}, u32[]{:S(2)}) collective-permute-start(bf16[14,128,128]{2,1,0:T(8,128)(2,1)S(1)} %bitcast.28), channel_id=1, source_target_pairs={{0,16},{8,24},{16,0},{24,8},{1,17},{9,25},{17,1},{25,9},{2,18},{10... | collective-permute-start | bytes 1376264 | tf_op jit(solution)/shard_map/ppermute | solution.py:388
  100.3 0.3 collective-permute-done.refs_4_
  100.6 1.9 collective-permute-start.5
  102.5 0.6 broadcast_add_fusion.1.refs_0_
  103.1 0.0 collective-permute-done.1.refs_5_
  103.1 5.8 %collective-permute-done.2.refs_6_ = bf16[10,128,128]{2,1,0:T(8,128)(2,1)S(1)} collective-permute-done((bf16[10,128,128]{2,1,0:T(8,128)(2,1)S(1)}, bf16[10,128,128]{2,1,0:T(8,128)(2,1)S(1)}, u32[]{:S(2)}, u32[]{:S(2)}) %collective-permute-start.2) | collective-permute-done | bytes 327712 | tf_op jit(solution)/shard_map/ppermute | solution.py:388
  108.9 0.0 copy-done.6
  108.9 0.0 copy-done.14
  108.9 0.0 copy-done.15
  108.9 0.7 copy-done.16
  109.6 22.2 %attention.2 = (bf16[8,80,512]{2,1,0:T(8,128)(2,1)}, f32[4,5,128,128]{3,2,1,0:T(8,128)}, f32[4,5,128,128]{3,2,1,0:T(8,128)}) custom-call(s32[12]{0:T(128)} %broadcast_add_fusion.1.refs_0_, s32[1]{0:T(128)} %bitcast.refs_1_, bf16[8,16,64,128]{3,2,1,0:T(8,128)(2,1)} %bitcast.23, bf16[10,128,128]{2,1,0:T(8,128)(2,1)} %bitcast.34, ...), custom_call_target="tpu_custom_call" | custom-call | flops 3355443200 | bytes 8388608 | tf_op jit(solution)/shard_map/attention/pallas_call | solution.py:233
  131.8 0.0 copy-done.3
  131.8 0.0 collective-permute-done.3.refs_8_
  131.8 0.0 collective-permute-done.4.refs_9_
  131.9 0.0 collective-permute-done.5.refs_10_
  131.9 0.0 all-to-all-done.2
  131.9 6.7 %all-to-all-start.1 = ((bf16[8,80,512]{2,1,0:T(8,128)(2,1)}), bf16[8,80,512]{2,1,0:T(8,128)(2,1)S(1)}, u32[]{:S(2)}, u32[]{:S(2)}) async-start(bf16[8,80,512]{2,1,0:T(8,128)(2,1)} %get-tuple-element.23), calls=%async_computation.1 | async-start | bytes 1310720 | tf_op jit(solution)/shard_map/all_to_all | solution.py:427
  138.6 18.7 %attention.3 = (bf16[8,112,512]{2,1,0:T(8,128)(2,1)}, bf16[8,192,128]{2,1,0:T(8,128)(2,1)}, bf16[8,192,128]{2,1,0:T(8,128)(2,1)}, bf16[8,192,128]{2,1,0:T(8,128)...) custom-call(s32[12]{0:T(128)} %broadcast_add_fusion.1.refs_0_, ...), custom_call_target="tpu_custom_call" | custom-call | flops 4697620480 | bytes 8388608 | tf_op jit(solution)/shard_map/attention/pallas_call | solution.py:233
  157.4 0.0 copy-start.5
  157.4 0.0 copy-start.4
  157.4 0.0 all-to-all-done.1.refs_0_
  157.4 0.0 copy-start
  157.4 6.8 %all-to-all-start.3 = ((bf16[8,112,512]{2,1,0:T(8,128)(2,1)}), bf16[8,112,512]{2,1,0:T(8,128)(2,1)S(1)}, u32[]{:S(2)}, u32[]{:S(2)}) async-start(bf16[8,112,512]{2,1,0:T(8,128)(2,1)} %get-tuple-element.30), calls=%async_computation.3 | async-start | bytes 1835008 | tf_op jit(solution)/shard_map/all_to_all | solution.py:428
  164.2 1.9 collective-permute-start.6
  166.1 4.6 %collective-permute-start.10 = (bf16[8,192,128]{2,1,0:T(8,128)(2,1)}, bf16[8,192,128]{2,1,0:T(8,128)(2,1)S(1)}, u32[]{:S(2)}, u32[]{:S(2)}) collective-permute-start(bf16[8,192,128]{2,1,0:T(8,128)(2,1)} %get-tuple-element.38), channel_id=1, source_target_pairs={{0,24},{8,0},{16,8},{24,16},{1,25},{9,1},{17,9},{25,17},{2,26},{10... | collective-permute-start | bytes 1179656 | tf_op jit(solution)/shard_map/ppermute | solution.py:388
  170.7 1.9 collective-permute-start.8
  172.6 3.4 %collective-permute-start.9 = (bf16[8,192,128]{2,1,0:T(8,128)(2,1)S(1)}, bf16[8,192,128]{2,1,0:T(8,128)(2,1)S(1)}, u32[]{:S(2)}, u32[]{:S(2)}) collective-permute-start(bf16[8,192,128]{2,1,0:T(8,128)(2,1)S(1)} %copy-done.13), channel_id=1, source_target_pairs={{0,8},{8,16},{16,24},{24,0},{1,9},{9,17},{17,25},{25,1},{2,10},{10... | collective-permute-start | bytes 1179656 | tf_op jit(solution)/shard_map/ppermute | solution.py:388
  176.0 0.6 collective-permute-done.6
  176.6 0.1 add_convert_fusion.1
  176.8 1.9 collective-permute-start.7
  178.7 0.0 collective-permute-done.10
  178.7 0.1 add_convert_fusion
  178.8 4.6 %collective-permute-start.11 = (bf16[8,192,128]{2,1,0:T(8,128)(2,1)S(1)}, bf16[8,192,128]{2,1,0:T(8,128)(2,1)S(1)}, u32[]{:S(2)}, u32[]{:S(2)}) collective-permute-start(bf16[8,192,128]{2,1,0:T(8,128)(2,1)S(1)} %add_convert_fusion), channel_id=1, source_target_pairs={{0,24},{8,0},{16,8},{24,16},{1,25},{9,1},{17,9},{25,17},{2,26},{10... | collective-permute-start | bytes 1179656 | tf_op jit(solution)/shard_map/ppermute | solution.py:388
  183.4 2.7 %collective-permute-done.8.refs_2_ = bf16[8,192,128]{2,1,0:T(8,128)(2,1)S(1)} collective-permute-done((bf16[8,192,128]{2,1,0:T(8,128)(2,1)}, bf16[8,192,128]{2,1,0:T(8,128)(2,1)S(1)}, u32[]{:S(2)}, u32[]{:S(2)}) %collective-permute-start.8) | collective-permute-done | bytes 393248 | tf_op jit(solution)/shard_map/ppermute | solution.py:388
  186.1 0.0 collective-permute-done.9.refs_4_
  186.1 6.2 %collective-permute-done.7.refs_1_ = bf16[8,192,128]{2,1,0:T(8,128)(2,1)S(1)} collective-permute-done((bf16[8,192,128]{2,1,0:T(8,128)(2,1)S(1)}, bf16[8,192,128]{2,1,0:T(8,128)(2,1)S(1)}, u32[]{:S(2)}, u32[]{:S(2)}) %collective-permute-start.7) | collective-permute-done | bytes 393248 | tf_op jit(solution)/shard_map/ppermute | solution.py:388
  192.3 2.1 collective-permute-done.11.refs_5_
  194.4 0.0 copy-done.1
  194.4 1.2 add_up.1
  195.6 0.0 all-to-all-done.3.refs_1_
  195.6 6.4 %all-to-all-start.4 = ((bf16[8,384,128]{2,1,0:T(8,128)(2,1)}), bf16[8,384,128]{2,1,0:T(8,128)(2,1)S(1)}, u32[]{:S(2)}, u32[]{:S(2)}) async-start(bf16[8,384,128]{2,1,0:T(8,128)(2,1)} %add_up.1), calls=%async_computation.4 | async-start | bytes 1572864 | tf_op jit(solution)/shard_map/all_to_all | solution.py:437
  201.9 1.2 lay_out.2
  203.2 19.2 %all-to-all-done.4.refs_0_ = bf16[8,384,128]{2,1,0:T(8,128)(2,1)S(1)} async-done(((bf16[8,384,128]{2,1,0:T(8,128)(2,1)}), bf16[8,384,128]{2,1,0:T(8,128)(2,1)S(1)}, u32[]{:S(2)}, u32[]{:S(2)}) %all-to-all-start.4) | async-done | bytes 786464 | tf_op jit(solution)/shard_map/all_to_all | solution.py:437
  222.4 1.1 lay_out.3
  (21 shorter events, 0.0 us)
Async XLA Ops:
  5.7 68.3 %all-to-all-start = ((bf16[128,64,128]{2,1,0:T(8,128)(2,1)}), bf16[128,64,128]{2,1,0:T(8,128)(2,1)S(1)}, u32[]{:S(2)}, u32[]{:S(2)}) async-start(bf16[128,64,128]{2,1,0:T(8,128)(2,1)} %bitcast.24), calls=%async_computation | async-start | bytes 4194304 | tf_op jit(solution)/shard_map/all_to_all | solution.py:402
  73.9 18.8 %copy-start.2 = (bf16[128,64,128]{2,1,0:T(8,128)(2,1)}, bf16[128,64,128]{2,1,0:T(8,128)(2,1)S(1)}, u32[]{:S(2)}) copy-start(bf16[128,64,128]{2,1,0:T(8,128)(2,1)S(1)} %all-to-all-done) | copy-start | bytes 6291460
  73.9 9.1 %copy-start.8 = (s32[192]{0:T(256)S(1)}, s32[192]{0:T(256)}, u32[]{:S(2)}) copy-start(s32[192]{0:T(256)} %param.12) | copy-start | bytes 2308
  73.9 9.2 %copy-start.7 = (s32[192]{0:T(256)S(1)}, s32[192]{0:T(256)}, u32[]{:S(2)}) copy-start(s32[192]{0:T(256)} %param.13) | copy-start | bytes 2308
  73.9 9.2 %copy-start.9 = (s32[192]{0:T(256)S(1)}, s32[192]{0:T(256)}, u32[]{:S(2)}) copy-start(s32[192]{0:T(256)} %param.11) | copy-start | bytes 2308
  73.9 58.0 %all-to-all-start.2 = ((bf16[128,56,128]{2,1,0:T(8,128)(2,1)}), bf16[128,56,128]{2,1,0:T(8,128)(2,1)}, u32[]{:S(2)}, u32[]{:S(2)}) async-start(bf16[128,56,128]{2,1,0:T(8,128)(2,1)} %bitcast.25), calls=%async_computation.2 | async-start | bytes 3670016 | tf_op jit(solution)/shard_map/all_to_all | solution.py:402
  83.3 25.6 %copy-start.6 = (bf16[10,8,16,128]{3,2,1,0:T(8,128)(2,1)}, bf16[10,8,16,128]{3,2,1,0:T(8,128)(2,1)S(1)}, u32[]{:S(2)}) copy-start(bf16[10,8,16,128]{3,2,1,0:T(8,128)(2,1)S(1)} %copy.12) | copy-start | bytes 983044
  83.3 17.3 %collective-permute-start = (bf16[10,128,128]{2,1,0:T(8,128)(2,1)S(1)}, bf16[10,128,128]{2,1,0:T(8,128)(2,1)S(1)}, u32[]{:S(2)}, u32[]{:S(2)}) collective-permute-start(bf16[10,128,128]{2,1,0:T(8,128)(2,1)S(1)} %bitcast.31), channel_id=1, source_target_pairs={{0,24},{8,0},{16,8},{24,16},{1,25},{9,1},{17,9},{25,17},{2,26},{10... | collective-permute-start | bytes 983048 | tf_op jit(solution)/shard_map/ppermute | solution.py:388
  87.8 15.3 %collective-permute-start.1 = (bf16[10,128,128]{2,1,0:T(8,128)(2,1)S(1)}, bf16[10,128,128]{2,1,0:T(8,128)(2,1)S(1)}, u32[]{:S(2)}, u32[]{:S(2)}) collective-permute-start(bf16[10,128,128]{2,1,0:T(8,128)(2,1)S(1)} %bitcast.32), channel_id=1, source_target_pairs={{0,16},{8,24},{16,0},{24,8},{1,17},{9,25},{17,1},{25,9},{2,18},{10... | collective-permute-start | bytes 983048 | tf_op jit(solution)/shard_map/ppermute | solution.py:388
  90.2 18.7 %collective-permute-start.2 = (bf16[10,128,128]{2,1,0:T(8,128)(2,1)S(1)}, bf16[10,128,128]{2,1,0:T(8,128)(2,1)S(1)}, u32[]{:S(2)}, u32[]{:S(2)}) collective-permute-start(bf16[10,128,128]{2,1,0:T(8,128)(2,1)S(1)} %bitcast.33), channel_id=1, source_target_pairs={{0,8},{8,16},{16,24},{24,0},{1,9},{9,17},{17,25},{25,1},{2,10},{10... | collective-permute-start | bytes 983048 | tf_op jit(solution)/shard_map/ppermute | solution.py:388
  93.1 38.7 %copy-start.3 = (bf16[14,8,16,128]{3,2,1,0:T(8,128)(2,1)}, bf16[14,8,16,128]{3,2,1,0:T(8,128)(2,1)S(1)}, u32[]{:S(2)}) copy-start(bf16[14,8,16,128]{3,2,1,0:T(8,128)(2,1)S(1)} %copy.13) | copy-start | bytes 1376260
  93.1 38.7 %collective-permute-start.3 = (bf16[14,128,128]{2,1,0:T(8,128)(2,1)S(1)}, bf16[14,128,128]{2,1,0:T(8,128)(2,1)S(1)}, u32[]{:S(2)}, u32[]{:S(2)}) collective-permute-start(bf16[14,128,128]{2,1,0:T(8,128)(2,1)S(1)} %bitcast.27), channel_id=1, source_target_pairs={{0,24},{8,0},{16,8},{24,16},{1,25},{9,1},{17,9},{25,17},{2,26},{10... | collective-permute-start | bytes 1376264 | tf_op jit(solution)/shard_map/ppermute | solution.py:388
  97.1 34.8 %collective-permute-start.4 = (bf16[14,128,128]{2,1,0:T(8,128)(2,1)S(1)}, bf16[14,128,128]{2,1,0:T(8,128)(2,1)S(1)}, u32[]{:S(2)}, u32[]{:S(2)}) collective-permute-start(bf16[14,128,128]{2,1,0:T(8,128)(2,1)S(1)} %bitcast.28), channel_id=1, source_target_pairs={{0,16},{8,24},{16,0},{24,8},{1,17},{9,25},{17,1},{25,9},{2,18},{10... | collective-permute-start | bytes 1376264 | tf_op jit(solution)/shard_map/ppermute | solution.py:388
  100.6 8.3 %copy-start.14 = (bf16[10,128,128]{2,1,0:T(8,128)(2,1)}, bf16[10,128,128]{2,1,0:T(8,128)(2,1)S(1)}, u32[]{:S(2)}) copy-start(bf16[10,128,128]{2,1,0:T(8,128)(2,1)S(1)} %collective-permute-done.refs_4_) | copy-start | bytes 983044
  100.6 31.3 %collective-permute-start.5 = (bf16[14,128,128]{2,1,0:T(8,128)(2,1)S(1)}, bf16[14,128,128]{2,1,0:T(8,128)(2,1)S(1)}, u32[]{:S(2)}, u32[]{:S(2)}) collective-permute-start(bf16[14,128,128]{2,1,0:T(8,128)(2,1)S(1)} %bitcast.29), channel_id=1, source_target_pairs={{0,8},{8,16},{16,24},{24,0},{1,9},{9,17},{17,25},{25,1},{2,10},{10... | collective-permute-start | bytes 1376264 | tf_op jit(solution)/shard_map/ppermute | solution.py:388
  103.1 5.8 %copy-start.15 = (bf16[10,128,128]{2,1,0:T(8,128)(2,1)}, bf16[10,128,128]{2,1,0:T(8,128)(2,1)S(1)}, u32[]{:S(2)}) copy-start(bf16[10,128,128]{2,1,0:T(8,128)(2,1)S(1)} %collective-permute-done.1.refs_5_) | copy-start | bytes 983044
  108.9 0.7 copy-start.16
  131.8 6.8 %copy-start.10 = (bf16[14,128,128]{2,1,0:T(8,128)(2,1)}, bf16[14,128,128]{2,1,0:T(8,128)(2,1)S(1)}, u32[]{:S(2)}) copy-start(bf16[14,128,128]{2,1,0:T(8,128)(2,1)S(1)} %collective-permute-done.3.refs_8_) | copy-start | bytes 1376260
  131.9 6.8 %copy-start.11 = (bf16[14,128,128]{2,1,0:T(8,128)(2,1)}, bf16[14,128,128]{2,1,0:T(8,128)(2,1)S(1)}, u32[]{:S(2)}) copy-start(bf16[14,128,128]{2,1,0:T(8,128)(2,1)S(1)} %collective-permute-done.4.refs_9_) | copy-start | bytes 1376260
  131.9 6.8 %copy-start.12 = (bf16[14,128,128]{2,1,0:T(8,128)(2,1)}, bf16[14,128,128]{2,1,0:T(8,128)(2,1)S(1)}, u32[]{:S(2)}) copy-start(bf16[14,128,128]{2,1,0:T(8,128)(2,1)S(1)} %collective-permute-done.5.refs_10_) | copy-start | bytes 1376260
  131.9 25.5 %all-to-all-start.1 = ((bf16[8,80,512]{2,1,0:T(8,128)(2,1)}), bf16[8,80,512]{2,1,0:T(8,128)(2,1)S(1)}, u32[]{:S(2)}, u32[]{:S(2)}) async-start(bf16[8,80,512]{2,1,0:T(8,128)(2,1)} %get-tuple-element.23), calls=%async_computation.1 | async-start | bytes 1310720 | tf_op jit(solution)/shard_map/all_to_all | solution.py:427
  157.4 15.3 %copy-start.13 = (bf16[8,192,128]{2,1,0:T(8,128)(2,1)S(1)}, bf16[8,192,128]{2,1,0:T(8,128)(2,1)}, u32[]{:S(2)}) copy-start(bf16[8,192,128]{2,1,0:T(8,128)(2,1)} %get-tuple-element.36) | copy-start | bytes 1179652
  157.4 19.3 %copy-start.5 = (bf16[8,192,128]{2,1,0:T(8,128)(2,1)S(1)}, bf16[8,192,128]{2,1,0:T(8,128)(2,1)}, u32[]{:S(2)}) copy-start(bf16[8,192,128]{2,1,0:T(8,128)(2,1)} %get-tuple-element.32) | copy-start | bytes 1179652
  157.4 21.3 %copy-start.4 = (bf16[8,192,128]{2,1,0:T(8,128)(2,1)S(1)}, bf16[8,192,128]{2,1,0:T(8,128)(2,1)}, u32[]{:S(2)}) copy-start(bf16[8,192,128]{2,1,0:T(8,128)(2,1)} %get-tuple-element.37) | copy-start | bytes 1179652
  157.4 37.0 %copy-start = (bf16[8,192,128]{2,1,0:T(8,128)(2,1)S(1)}, bf16[8,192,128]{2,1,0:T(8,128)(2,1)}, u32[]{:S(2)}) copy-start(bf16[8,192,128]{2,1,0:T(8,128)(2,1)} %get-tuple-element.31.refs_0_) | copy-start | bytes 1179652
  157.4 37.0 %copy-start.1 = (bf16[8,192,128]{2,1,0:T(8,128)(2,1)S(1)}, bf16[8,192,128]{2,1,0:T(8,128)(2,1)}, u32[]{:S(2)}) copy-start(bf16[8,192,128]{2,1,0:T(8,128)(2,1)} %get-tuple-element.35.refs_3_) | copy-start | bytes 1179652
  157.4 38.1 %all-to-all-start.3 = ((bf16[8,112,512]{2,1,0:T(8,128)(2,1)}), bf16[8,112,512]{2,1,0:T(8,128)(2,1)S(1)}, u32[]{:S(2)}, u32[]{:S(2)}) async-start(bf16[8,112,512]{2,1,0:T(8,128)(2,1)} %get-tuple-element.30), calls=%async_computation.3 | async-start | bytes 1835008 | tf_op jit(solution)/shard_map/all_to_all | solution.py:428
  164.2 12.4 %collective-permute-start.6 = (bf16[8,192,128]{2,1,0:T(8,128)(2,1)}, bf16[8,192,128]{2,1,0:T(8,128)(2,1)S(1)}, u32[]{:S(2)}, u32[]{:S(2)}) collective-permute-start(bf16[8,192,128]{2,1,0:T(8,128)(2,1)} %get-tuple-element.33), channel_id=1, source_target_pairs={{0,8},{8,16},{16,24},{24,0},{1,9},{9,17},{17,25},{25,1},{2,10},{10... | collective-permute-start | bytes 1179656 | tf_op jit(solution)/shard_map/ppermute | solution.py:388
  166.1 12.6 %collective-permute-start.10 = (bf16[8,192,128]{2,1,0:T(8,128)(2,1)}, bf16[8,192,128]{2,1,0:T(8,128)(2,1)S(1)}, u32[]{:S(2)}, u32[]{:S(2)}) collective-permute-start(bf16[8,192,128]{2,1,0:T(8,128)(2,1)} %get-tuple-element.38), channel_id=1, source_target_pairs={{0,24},{8,0},{16,8},{24,16},{1,25},{9,1},{17,9},{25,17},{2,26},{10... | collective-permute-start | bytes 1179656 | tf_op jit(solution)/shard_map/ppermute | solution.py:388
  170.7 15.4 %collective-permute-start.8 = (bf16[8,192,128]{2,1,0:T(8,128)(2,1)}, bf16[8,192,128]{2,1,0:T(8,128)(2,1)S(1)}, u32[]{:S(2)}, u32[]{:S(2)}) collective-permute-start(bf16[8,192,128]{2,1,0:T(8,128)(2,1)} %get-tuple-element.34), channel_id=1, source_target_pairs={{0,24},{8,0},{16,8},{24,16},{1,25},{9,1},{17,9},{25,17},{2,26},{10... | collective-permute-start | bytes 1179656 | tf_op jit(solution)/shard_map/ppermute | solution.py:388
  172.6 13.4 %collective-permute-start.9 = (bf16[8,192,128]{2,1,0:T(8,128)(2,1)S(1)}, bf16[8,192,128]{2,1,0:T(8,128)(2,1)S(1)}, u32[]{:S(2)}, u32[]{:S(2)}) collective-permute-start(bf16[8,192,128]{2,1,0:T(8,128)(2,1)S(1)} %copy-done.13), channel_id=1, source_target_pairs={{0,8},{8,16},{16,24},{24,0},{1,9},{9,17},{17,25},{25,1},{2,10},{10... | collective-permute-start | bytes 1179656 | tf_op jit(solution)/shard_map/ppermute | solution.py:388
  176.8 15.6 %collective-permute-start.7 = (bf16[8,192,128]{2,1,0:T(8,128)(2,1)S(1)}, bf16[8,192,128]{2,1,0:T(8,128)(2,1)S(1)}, u32[]{:S(2)}, u32[]{:S(2)}) collective-permute-start(bf16[8,192,128]{2,1,0:T(8,128)(2,1)S(1)} %add_convert_fusion.1), channel_id=1, source_target_pairs={{0,8},{8,16},{16,24},{24,0},{1,9},{9,17},{17,25},{25,1},{2,10},{10... | collective-permute-start | bytes 1179656 | tf_op jit(solution)/shard_map/ppermute | solution.py:388
  178.8 15.6 %collective-permute-start.11 = (bf16[8,192,128]{2,1,0:T(8,128)(2,1)S(1)}, bf16[8,192,128]{2,1,0:T(8,128)(2,1)S(1)}, u32[]{:S(2)}, u32[]{:S(2)}) collective-permute-start(bf16[8,192,128]{2,1,0:T(8,128)(2,1)S(1)} %add_convert_fusion), channel_id=1, source_target_pairs={{0,24},{8,0},{16,8},{24,16},{1,25},{9,1},{17,9},{25,17},{2,26},{10... | collective-permute-start | bytes 1179656 | tf_op jit(solution)/shard_map/ppermute | solution.py:388
  195.6 26.8 %all-to-all-start.4 = ((bf16[8,384,128]{2,1,0:T(8,128)(2,1)}), bf16[8,384,128]{2,1,0:T(8,128)(2,1)S(1)}, u32[]{:S(2)}, u32[]{:S(2)}) async-start(bf16[8,384,128]{2,1,0:T(8,128)(2,1)} %add_up.1), calls=%async_computation.4 | async-start | bytes 1572864 | tf_op jit(solution)/shard_map/all_to_all | solution.py:437
